TPU v7x, 32 devices: a whole 2x2x4 slice. The times are simulated.
32 devices in a mesh: cuts: 2 (over x), outer: 16 (over z, y, core).
Axes of the slice: x: 2, y: 2, z: 4, core: 2. Of those that a mesh axis runs over, the one named last changes fastest.
Arguments:
- stem_tensor: bfloat16 [32, 512, 2, 512], P(('cuts', 'outer')), parts along dimension 0, may hold values from -6 to 6
- leaf_left: bfloat16 [4, 2, 8192, 2, 512], P(None, None, 'outer'), may hold values from -0.09375 to 0.09375
- leaf_right: bfloat16 [4, 2, 8192, 2, 512], P(None, None, 'outer'), may hold values from -0.125 to 0.125
- slice_bits: int32 [8], P('cuts'), parts along dimension 0, may hold values from 0 to 1, as said below
Outputs:
- stem_out: bfloat16 [32, 512, 2, 512], P(('cuts', 'outer')), parts along dimension 0
There are 2 independent parts, one for each index of `cuts`. A program takes and returns all parts, laid end to end along the dimension named above; an argument that names none is the same for every part. Nothing has to cross between parts.
Inputs may be any that keep to these rules, and one draw needn't show every extreme that they name: `slice_bits`: the first entry is the index of the part modulo 2, so neighbouring parts contract different slices; the other entries are drawn independently.
All inputs are finite; a program needn't handle non-finite values.
Results may differ from a plain program's by a relative error of at most 0.01.
Values may be sent and summed in bfloat16 or wider, within the bound.
No kernel may reach another device: no remote copies, remote signals or barrier semaphores. Data moves between devices by JAX's collectives and lax.ppermute only.
A program may use at most 64 MiB of HBM per device.

v0:
```python
import jax
import jax.numpy as jnp
from jax import lax
from jax.sharding import PartitionSpec as P

ROUNDS = 2


def leaf_term(left_leaf, right_leaf, row_count):
    depth = left_leaf.shape[0]
    width = right_leaf.shape[2]
    product = lax.dot_general(
        left_leaf.reshape(depth, 2 * row_count),
        right_leaf.reshape(depth, 2 * width),
        (((0,), (0,)), ((), ())),
        preferred_element_type=jnp.float32,
    )
    product = product.reshape(2, row_count, 2, width)
    real_part = product[0, :, 0] - product[1, :, 1]
    imag_part = product[0, :, 1] + product[1, :, 0]
    return jnp.stack([real_part, imag_part], axis=1)


def absorb_columns(stem_tile, q_branch):
    width = q_branch.shape[0]
    q_flat = q_branch.reshape(width, 2 * width)
    from_real = jnp.dot(stem_tile[:, 0, :], q_flat, preferred_element_type=jnp.float32)
    from_imag = jnp.dot(stem_tile[:, 1, :], q_flat, preferred_element_type=jnp.float32)
    real_part = from_real[:, :width] - from_imag[:, width:]
    imag_part = from_real[:, width:] + from_imag[:, :width]
    return jnp.stack([real_part, imag_part], axis=1).astype(jnp.bfloat16)


def on_device(stem_tensor, leaf_left, leaf_right, slice_bits):
    width = stem_tensor.shape[1]
    state = stem_tensor
    for round_index in range(ROUNDS):
        leaves = []
        for branch_index in (2 * round_index, 2 * round_index + 1):
            chosen = slice_bits[branch_index]
            leaves.append(
                (
                    lax.dynamic_index_in_dim(leaf_left[branch_index], chosen, 0, keepdims=False),
                    lax.dynamic_index_in_dim(leaf_right[branch_index], chosen, 0, keepdims=False),
                )
            )
        totals = lax.psum(
            (
                leaf_term(leaves[0][0], leaves[0][1], width),
                leaf_term(leaves[1][0], leaves[1][1], width),
            ),
            "outer",
        )
        p_branch = totals[0].astype(jnp.bfloat16)
        q_branch = totals[1].astype(jnp.bfloat16)
        absorbed = absorb_columns(state[0], q_branch)[None]
        p_flat = p_branch.reshape(width, 2 * width)
        received = lax.all_to_all(absorbed, "outer", split_axis=1, concat_axis=0, tiled=True)
        items = received.shape[3]
        regrouped = received.reshape(width, 2, items)
        from_real = lax.dot_general(
            p_flat, regrouped[:, 0, :], (((0,), (0,)), ((), ())), preferred_element_type=jnp.float32
        )
        from_imag = lax.dot_general(
            p_flat, regrouped[:, 1, :], (((0,), (0,)), ((), ())), preferred_element_type=jnp.float32
        )
        real_part = from_real[:width] - from_imag[width:]
        imag_part = from_real[width:] + from_imag[:width]
        renewed = jnp.stack([real_part, imag_part], axis=1).astype(jnp.bfloat16)
        state = renewed[None]
    return state


def solution(mesh):
    return jax.shard_map(
        on_device,
        mesh=mesh,
        in_specs=(
            P(("cuts", "outer"), None, None, None),
            P(None, None, "outer", None, None),
            P(None, None, "outer", None, None),
            P("cuts"),
        ),
        out_specs=P(("cuts", "outer"), None, None, None),
        check_vma=False,
    )
```

profile of v0, /device:TPU:11, one launch (start us, length us, event | category | flops | bytes accessed | tf_op | source)
XLA Modules:
  0.0 341.8 jit_solution(12925352407086176754)
XLA Ops:
  6.3 8.9 %fusion.42 = (bf16[1,2,512,2,512]{4,3,2,1,0:T(2,128)(2,1)S(1)}, bf16[1,2,512,2,512]{4,3,2,1,0:T(2,128)(2,1)}, bf16[1,2,512,2,512]{4,3,2,1,0:T(2,128)(2,1)}, bf16[1,2,512,2,512]{4,3,2,1,0:T(2,128)(2,1)}) fusion(bf16[4,2,512,2,512]{4,3,2,1,0:T(2,128)(2,1)} %param.5), kind=kLoop, calls=%fused_computation.82 | loop fusion | bytes 16777216 | tf_op jit(solution)/shard_map/slice | solution.py:43
  16.6 3.6 %constant_dynamic-slice_fusion.1 = (bf16[1,1,512,2,512]{4,3,2,1,0:T(2,128)(2,1)S(1)}, bf16[1,1,512,2,512]{4,3,2,1,0:T(2,128)(2,1)}) fusion(bf16[1,2,512,2,512]{4,3,2,1,0:T(2,128)(2,1)} %get-tuple-element.12, s32[]{:T(128)S(6)} %select_n.20, bf16[1,2,512,2,512]{4,3,2,1,0:T(2,128)(2,1)S(1)} %get-tuple-element.9, s32[]{:T(128)S(6)} %select_n.19), kind=kLoop, calls=%fused_computation.75 | loop fusion | bytes 4194312 | tf_op jit(solution)/shard_map/jit(dynamic_index_in_dim)/dynamic_slice | solution.py:43
  20.2 2.4 copy.67
  22.6 8.8 %fusion.43 = (bf16[1,2,512,2,512]{4,3,2,1,0:T(2,128)(2,1)S(1)}, bf16[1,2,512,2,512]{4,3,2,1,0:T(2,128)(2,1)}, bf16[1,2,512,2,512]{4,3,2,1,0:T(2,128)(2,1)}, bf16[1,2,512,2,512]{4,3,2,1,0:T(2,128)(2,1)S(1)}) fusion(bf16[4,2,512,2,512]{4,3,2,1,0:T(2,128)(2,1)} %param.6), kind=kLoop, calls=%fused_computation.83 | loop fusion | bytes 16777216 | tf_op jit(solution)/shard_map/slice | solution.py:44
  31.5 2.4 constant_dynamic-slice_fusion
  33.9 2.5 copy.69
  36.4 2.5 fusion.19
  40.7 4.4 %constant_dynamic-slice_fusion.5 = (bf16[1,1,512,2,512]{4,3,2,1,0:T(2,128)(2,1)}, bf16[1,1,512,2,512]{4,3,2,1,0:T(2,128)(2,1)}) fusion(bf16[1,2,512,2,512]{4,3,2,1,0:T(2,128)(2,1)} %get-tuple-element.10, s32[]{:T(128)S(6)} %select_n.18, bf16[1,2,512,2,512]{4,3,2,1,0:T(2,128)(2,1)} %get-tuple-element.11, s32[]{:T(128)S(6)} %select_n.17), kind=kLoop, calls=%fused_computation.79 | loop fusion | bytes 4194312 | tf_op jit(solution)/shard_map/jit(dynamic_index_in_dim)/dynamic_slice | solution.py:43
  45.1 3.7 %copy.63 = bf16[1,1,512,2,512]{2,4,3,1,0:T(8,128)(2,1)} copy(bf16[1,1,512,2,512]{4,3,2,1,0:T(2,128)(2,1)} %get-tuple-element.41) | data formatting | bytes 2097152
  48.8 4.3 %constant_dynamic-slice_fusion.4 = (bf16[1,1,512,2,512]{4,3,2,1,0:T(2,128)(2,1)}, bf16[1,1,512,2,512]{4,3,2,1,0:T(2,128)(2,1)}) fusion(bf16[1,2,512,2,512]{4,3,2,1,0:T(2,128)(2,1)} %get-tuple-element.14, s32[]{:T(128)S(6)} %select_n.18, bf16[1,2,512,2,512]{4,3,2,1,0:T(2,128)(2,1)} %get-tuple-element.15, s32[]{:T(128)S(6)} %select_n.17), kind=kLoop, calls=%fused_computation.78 | loop fusion | bytes 4194312 | tf_op jit(solution)/shard_map/jit(dynamic_index_in_dim)/dynamic_slice | solution.py:44
  53.1 3.7 %copy.65 = bf16[1,1,512,2,512]{2,4,3,1,0:T(8,128)(2,1)} copy(bf16[1,1,512,2,512]{4,3,2,1,0:T(2,128)(2,1)} %get-tuple-element.37) | data formatting | bytes 2097152
  56.8 2.8 fusion.22
  61.6 2.5 copy.71
  64.1 3.7 %copy.73 = bf16[1,1,512,2,512]{2,4,3,1,0:T(8,128)(2,1)} copy(bf16[1,1,512,2,512]{4,3,2,1,0:T(2,128)(2,1)} %get-tuple-element.35) | data formatting | bytes 2097152
  67.8 2.5 fusion.16
  72.3 2.5 copy.59
  74.8 3.7 %copy.61 = bf16[1,1,512,2,512]{2,4,3,1,0:T(8,128)(2,1)} copy(bf16[1,1,512,2,512]{4,3,2,1,0:T(2,128)(2,1)} %get-tuple-element.38) | data formatting | bytes 2097152
  78.6 2.5 fusion.25
  83.1 182.2 %all-reduce.2 = (bf16[512,2,512]{2,0,1:T(8,128)(2,1)}, bf16[512,2,512]{2,0,1:T(8,128)(2,1)}, bf16[512,2,512]{2,0,1:T(8,128)(2,1)}, bf16[512,2,512]{2,0,1:T(8,128)(2,1)S(1)}) all-reduce(f32[512,2,512]{2,0,1:T(8,128)} %pad_maximum_fusion, f32[512,2,512]{2,0,1:T(8,128)} %pad_maximum_fusion.3, ...), channel_id=1, replica_groups=mesh['cuts'=2,'outer'=16] {'outer'}, use_global_device_ids=true, to_apply=%region_0.1 | all-reduce | flops 2097152 | bytes 12582912 | tf_op jit(solution)/shard_map/psum | solution.py:47
  268.9 2.1 copy.46
  271.0 6.0 %all-to-all-start = ((bf16[1,512,2,512]{3,2,0,1:T(2,128)(2,1)}), bf16[1,512,2,512]{3,2,0,1:T(2,128)(2,1)S(1)}, u32[]{:S(2)}, u32[]{:S(2)}) async-start(bf16[1,512,2,512]{3,2,0,1:T(2,128)(2,1)} %copy.46), calls=%async_computation | async-start | bytes 2097152 | tf_op jit(solution)/shard_map/all_to_all | solution.py:58
  279.0 22.8 %all-to-all-done = bf16[1,512,2,512]{3,2,0,1:T(2,128)(2,1)S(1)} async-done(((bf16[1,512,2,512]{3,2,0,1:T(2,128)(2,1)}), bf16[1,512,2,512]{3,2,0,1:T(2,128)(2,1)S(1)}, u32[]{:S(2)}, u32[]{:S(2)}) %all-to-all-start) | async-done | bytes 1048608 | tf_op jit(solution)/shard_map/all_to_all | solution.py:58
  307.7 5.0 %all-to-all-start.1 = ((bf16[1,512,2,512]{3,2,0,1:T(2,128)(2,1)}), bf16[1,512,2,512]{3,2,0,1:T(2,128)(2,1)S(1)}, u32[]{:S(2)}, u32[]{:S(2)}) async-start(bf16[1,512,2,512]{3,2,0,1:T(2,128)(2,1)} %copy.51), calls=%async_computation.1 | async-start | bytes 2097152 | tf_op jit(solution)/shard_map/all_to_all | solution.py:58
  313.2 24.3 %all-to-all-done.1 = bf16[1,512,2,512]{3,2,0,1:T(2,128)(2,1)S(1)} async-done(((bf16[1,512,2,512]{3,2,0,1:T(2,128)(2,1)}), bf16[1,512,2,512]{3,2,0,1:T(2,128)(2,1)S(1)}, u32[]{:S(2)}, u32[]{:S(2)}) %all-to-all-start.1) | async-done | bytes 1048608 | tf_op jit(solution)/shard_map/all_to_all | solution.py:58
  (44 shorter events, 24.3 us)
Async XLA Ops:
  64.1 3.7 %copy-start.1 = (bf16[1,1,512,2,512]{2,4,3,1,0:T(8,128)(2,1)S(1)}, bf16[1,1,512,2,512]{2,4,3,1,0:T(8,128)(2,1)}, u32[]{:S(2)}) copy-start(bf16[1,1,512,2,512]{2,4,3,1,0:T(8,128)(2,1)} %copy.71) | copy-start | bytes 3145732
  70.8 1.5 copy-start
  74.8 3.7 %copy-start.2 = (bf16[1,1,512,2,512]{2,4,3,1,0:T(8,128)(2,1)S(1)}, bf16[1,1,512,2,512]{2,4,3,1,0:T(8,128)(2,1)}, u32[]{:S(2)}) copy-start(bf16[1,1,512,2,512]{2,4,3,1,0:T(8,128)(2,1)} %copy.59) | copy-start | bytes 3145732
  265.3 1.2 copy-start.3
  271.0 6.0 %copy-start.5 = (bf16[512,2,512]{2,0,1:T(8,128)(2,1)S(1)}, bf16[512,2,512]{2,0,1:T(8,128)(2,1)}, u32[]{:S(2)}) copy-start(bf16[512,2,512]{2,0,1:T(8,128)(2,1)} %get-tuple-element.7) | copy-start | bytes 3145732
  271.0 30.8 %all-to-all-start = ((bf16[1,512,2,512]{3,2,0,1:T(2,128)(2,1)}), bf16[1,512,2,512]{3,2,0,1:T(2,128)(2,1)S(1)}, u32[]{:S(2)}, u32[]{:S(2)}) async-start(bf16[1,512,2,512]{3,2,0,1:T(2,128)(2,1)} %copy.46), calls=%async_computation | async-start | bytes 2097152 | tf_op jit(solution)/shard_map/all_to_all | solution.py:58
  305.6 7.1 %copy-start.4 = (bf16[512,2,512]{2,0,1:T(8,128)(2,1)S(1)}, bf16[512,2,512]{2,0,1:T(8,128)(2,1)}, u32[]{:S(2)}) copy-start(bf16[512,2,512]{2,0,1:T(8,128)(2,1)} %get-tuple-element.5) | copy-start | bytes 3145732
  307.7 29.8 %all-to-all-start.1 = ((bf16[1,512,2,512]{3,2,0,1:T(2,128)(2,1)}), bf16[1,512,2,512]{3,2,0,1:T(2,128)(2,1)S(1)}, u32[]{:S(2)}, u32[]{:S(2)}) async-start(bf16[1,512,2,512]{3,2,0,1:T(2,128)(2,1)} %copy.51), calls=%async_computation.1 | async-start | bytes 2097152 | tf_op jit(solution)/shard_map/all_to_all | solution.py:58
where the time goes:
time: 343 us; the launch traced here: 342 us
  blocking collectives  182 us (53%)
  local copies, waits for them, and re-layouts  69.2 us (20%)
  waiting for transfers between devices  47.1 us (14%)
  matrix products  16.1 us (5%)
  starting transfers between devices  10.9 us (3%)
  other arithmetic  8.63 us (3%)
  between operations  7.62 us (2%)
    psum x1, blocking collectives, on_device(): lax.psum((leaf_term(leaves[0][0], leaves[0][1], width), leaf_term(leaves[...  182 us
    all_to_all x2, waiting for transfers between devices, on_device(): lax.all_to_all(absorbed, 'outer', split_axis=1, concat_axis=0, tiled=True)  47.1 us
    unnamed x21, local copies, waits for them, and re-layouts  25.6 us
    all_to_all x2, starting transfers between devices, on_device(): lax.all_to_all(absorbed, 'outer', split_axis=1, concat_axis=0, tiled=True)  10.9 us
    dot_general x4, matrix products, leaf_term(): lax.dot_general(left_leaf.reshape(depth, 2 * row_count), right_leaf.resha...  10.3 us
    slice x1, local copies, waits for them, and re-layouts, on_device(): leaf_left[branch_index]  8.94 us
    slice x1, local copies, waits for them, and re-layouts, on_device(): leaf_right[branch_index]  8.84 us
    dynamic_slice x2, local copies, waits for them, and re-layouts, on_device(): lax.dynamic_index_in_dim(leaf_left[branch_index], chosen, 0, keepdims=False)  8.03 us
  transfers between devices with their start and end apart: 2, of which 2 were waited for; matrix products, arithmetic and copies ran while one was open for 1% of the time, Pallas kernels for 0%

commit v1 on v0

v1 whole, which is shorter than its diff:
```python
import functools

import jax
import jax.numpy as jnp
from jax import lax
from jax.experimental import pallas as pl
from jax.experimental.pallas import tpu as pltpu
from jax.sharding import PartitionSpec as P

ROUNDS = 2
GROUPS = ((0,), (2,), (1,), (3,))
VMEM_LIMIT = 48 << 20
bf16, f32 = jnp.bfloat16, jnp.float32

SMEM_SPEC = pl.BlockSpec(memory_space=pltpu.SMEM)
VMEM_SPEC = pl.BlockSpec(memory_space=pltpu.VMEM)
ANY_SPEC = pl.BlockSpec(memory_space=pl.ANY)


def call(body, out_shape, in_specs, scratch=(), flops=0, moved=0):
    return pl.pallas_call(
        body,
        out_shape=out_shape,
        in_specs=in_specs,
        out_specs=jax.tree.map(lambda _: VMEM_SPEC, out_shape),
        scratch_shapes=list(scratch),
        compiler_params=pltpu.CompilerParams(vmem_limit_bytes=VMEM_LIMIT),
        cost_estimate=pl.CostEstimate(flops=flops, bytes_accessed=moved, transcendentals=0),
    )


def tdot(a, b):
    return lax.dot_general(a, b, (((0,), (0,)), ((), ())), preferred_element_type=f32)


def dot(a, b):
    return jnp.dot(a, b, preferred_element_type=f32)


def leaf_body(branches, meta, left, right, keep, send, lhs, rhs, both, sems):
    depth, width = left.shape[2], left.shape[4]
    core = meta[0] & 1
    copies = []
    for at, j in enumerate(branches):
        first, second = (right, left) if j % 2 == 0 else (left, right)
        for which, (ref, buf) in enumerate(((first, lhs), (second, rhs))):
            flat = ref.reshape(ref.shape[0], ref.shape[1], 2 * depth, width)
            copy = pltpu.make_async_copy(flat.at[j, meta[1 + j]], buf.at[at], sems.at[at, which])
            copy.start()
            copies.append(copy)
    rows = lax.broadcasted_iota(jnp.int32, (2 * depth // 8, 8, width), 1)
    is_real = (rows & 1) == 0
    for at in range(len(branches)):
        copies[2 * at + 1].wait()
        wide = rhs[at].astype(f32).reshape(2 * depth // 8, 8, width)
        signed = jnp.where(is_real, wide, -wide)
        swapped = jnp.where(is_real, pltpu.roll(wide, 7, 1), pltpu.roll(wide, 1, 1))
        both[core] = signed.reshape(2 * depth, width).astype(bf16)
        both[1 - core] = swapped.reshape(2 * depth, width).astype(bf16)
        copies[2 * at].wait()
        send[at] = tdot(lhs[at], both[1]).astype(bf16)
        keep[at] = tdot(lhs[at], both[0])


def leaf_partials(meta, left, right, branches):
    count, depth, width = len(branches), left.shape[2], left.shape[4]
    shape = (count, width, width)
    return call(
        functools.partial(leaf_body, branches),
        (jax.ShapeDtypeStruct(shape, f32), jax.ShapeDtypeStruct(shape, bf16)),
        [SMEM_SPEC, ANY_SPEC, ANY_SPEC],
        [
            pltpu.VMEM((count, 2 * depth, width), bf16),
            pltpu.VMEM((count, 2 * depth, width), bf16),
            pltpu.VMEM((2, 2 * depth, width), bf16),
            pltpu.SemaphoreType.DMA((count, 2)),
        ],
        flops=count * 8 * depth * width * width,
        moved=count * 8 * depth * width,
    )(meta, left, right)


def add_body(shift, meta, keep, recv, keep_out, send_out):
    half = keep_out.shape[1]
    bit = (meta[0] >> shift) & 1
    mine = pl.multiple_of(bit * half, half)
    other = pl.multiple_of((1 - bit) * half, half)
    send_out[...] = (keep[:, pl.ds(other, half)] + recv[:, pl.ds(other, half)].astype(f32)).astype(bf16)
    keep_out[...] = keep[:, pl.ds(mine, half)] + recv[:, pl.ds(mine, half)].astype(f32)


def add_and_split(meta, keep, recv, shift):
    count, rows, width = keep.shape
    half = rows // 2
    if half % 16:
        total = (keep + recv.astype(f32)).reshape(count, 2, half, width)
        bit = (meta[0] >> shift) & 1
        return (
            lax.dynamic_index_in_dim(total, bit, 1, keepdims=False),
            lax.dynamic_index_in_dim(total, 1 - bit, 1, keepdims=False).astype(bf16),
        )
    shape = (count, half, width)
    return call(
        functools.partial(add_body, shift),
        (jax.ShapeDtypeStruct(shape, f32), jax.ShapeDtypeStruct(shape, bf16)),
        [SMEM_SPEC, VMEM_SPEC, VMEM_SPEC],
        moved=count * rows * width * 9,
    )(meta, keep, recv)


def swap_with(x, mask, size):
    return lax.ppermute(x, "outer", [(i, i ^ mask) for i in range(size)])


def full_sum(meta, left, right, branches, size):
    levels = size.bit_length() - 1
    keep, send = leaf_partials(meta, left, right, branches)
    recv = swap_with(send, 1, size)
    for shift in range(1, levels):
        keep, send = add_and_split(meta, keep, recv, shift)
        recv = swap_with(send, 1 << shift, size)
    total = (keep + recv.astype(f32)).astype(bf16)[None]
    for shift in reversed(range(1, levels)):
        total = jnp.concatenate([total, swap_with(total, 1 << shift, size)], axis=0)
    other = swap_with(total, 1, size)
    return total, other


def in_order(meta, planes, at):
    own, other = planes[0][:, at], planes[1][:, at]
    blocks, rows, width = own.shape
    if rows % 16:
        order = block_of(meta, blocks) ^ jnp.arange(blocks)
        own, other = (x[order].reshape(1, blocks * rows, width) for x in (own, other))
    return own, other


def block_of(meta, blocks):
    place, found, shift = meta[0] >> 1, 0, blocks >> 1
    while shift:
        found = found + (place & 1) * shift
        place, shift = place >> 1, shift >> 1
    return found


def prepare_body(meta, stem, out, wide):
    count, width = stem.shape[0], stem.shape[2]
    core = meta[0] & 1
    flat = stem[...].reshape(2 * count, width)
    for at in range(width // 128):
        wide[at] = flat[:, at * 128 : (at + 1) * 128].astype(f32)
    for at in range(width // 128):
        here = slice(at * 128, (at + 1) * 128)
        there = slice(width + at * 128, width + (at + 1) * 128)
        real = wide[at, pl.ds(0, count, stride=2), :]
        imag = wide[at, pl.ds(1, count, stride=2), :]
        out[core, :, here] = real.astype(bf16)
        out[core, :, there] = imag.astype(bf16)
        out[1 - core, :, here] = (-imag).astype(bf16)
        out[1 - core, :, there] = real.astype(bf16)


def prepare(meta, stem):
    count, _, width = stem.shape
    return call(
        prepare_body,
        jax.ShapeDtypeStruct((2, count, 2 * width), bf16),
        [SMEM_SPEC, VMEM_SPEC],
        [pltpu.VMEM((width // 128, 2 * count, 128), f32)],
        moved=6 * count * width * 2,
    )(meta, stem)


def first_body(meta, own, other, right, out):
    blocks, rows, width = own.shape
    me = block_of(meta, blocks)
    mine = own[...].reshape(blocks * rows, width)
    theirs = other[...].reshape(blocks * rows, width)
    tile = 256
    for at in range(right.shape[2] // tile):
        here = slice(at * tile, (at + 1) * tile)
        value = dot(mine, right[0, :, here]) + dot(theirs, right[1, :, here])
        value = value.astype(bf16).reshape(blocks, rows, tile)
        for t in range(blocks):
            out[me ^ t, :, here] = value[t]


def first_product(meta, own, other, right):
    blocks, rows, width = own.shape
    return call(
        first_body,
        jax.ShapeDtypeStruct((blocks, rows, right.shape[2]), bf16),
        [SMEM_SPEC] + [VMEM_SPEC] * 3,
        flops=8 * blocks * rows * width * width,
        moved=10 * width * width,
    )(meta, own, other, right)


def joined_body(meta, own0, other0, own1, other1, out, right):
    blocks, rows, width = own0.shape
    me = block_of(meta, blocks)
    core = meta[0] & 1
    for t in range(blocks):
        own, other = own1[t], other1[t]
        real = jnp.where(core == 0, own, other)
        imag = jnp.where(core == 0, other, own)
        right[core, me ^ t, :, :width] = real
        right[core, me ^ t, :, width:] = imag
        right[1 - core, me ^ t, :, :width] = -imag
        right[1 - core, me ^ t, :, width:] = real
    mine = own0[...].reshape(blocks * rows, width)
    theirs = other0[...].reshape(blocks * rows, width)
    tile = 256
    for at in range(2 * width // tile):
        here = slice(at * tile, (at + 1) * tile)
        there = slice((at * tile + width) % (2 * width), (at * tile + width) % (2 * width) + tile)
        first = right[0, :, :, here].reshape(blocks * rows, tile)
        second = right[1, :, :, here].reshape(blocks * rows, tile)
        value = dot(mine, first) + dot(theirs, second)
        turned = value if at * tile < width else -value
        value = value.astype(bf16).reshape(blocks, rows, tile)
        turned = turned.astype(bf16).reshape(blocks, rows, tile)
        for t in range(blocks):
            out[0, me ^ t, :, here] = value[t]
            out[1, me ^ t, :, there] = turned[t]


def joined_right(meta, own0, other0, own1, other1):
    blocks, rows, width = own0.shape
    return call(
        joined_body,
        jax.ShapeDtypeStruct((2, blocks, rows, 2 * width), bf16),
        [SMEM_SPEC] + [VMEM_SPEC] * 4,
        [pltpu.VMEM((2, blocks, rows, 2 * width), bf16)],
        flops=8 * blocks * rows * width * width,
        moved=16 * width * width,
    )(meta, own0, other0, own1, other1)


def last_body(meta, own, other, stem, factor, out, right, middle, wide, sem):
    blocks, rows, width = own.shape
    total = blocks * rows
    count = stem.shape[0]
    me = block_of(meta, blocks)
    core = meta[0] & 1
    right[core] = stem[...]
    right[1 - core, :, :width] = -stem[:, width:]
    right[1 - core, :, width:] = stem[:, :width]
    mine = own[...].reshape(total, width)
    theirs = other[...].reshape(total, width)
    tile = 256
    for at in range(2 * width // tile):
        here = slice(at * tile, (at + 1) * tile)
        middle[:, here] = (dot(mine, right[0, :, here]) + dot(theirs, right[1, :, here])).astype(bf16)
    for at in range(width // tile):
        for part in range(2):
            here = slice(part * width + at * tile, part * width + (at + 1) * tile)
            value = dot(middle[:, :width], factor[0, :, here]) + dot(middle[:, width:], factor[1, :, here])
            for sub in range(tile // 128):
                wide[at * (tile // 128) + sub, pl.ds(part, total, stride=2), :] = value[:, sub * 128 : (sub + 1) * 128]
    for at in range(width // 128):
        for t in range(blocks):
            piece = wide[at, 2 * rows * t : 2 * rows * (t + 1), :]
            out[me ^ t, :, at * 128 : (at + 1) * 128] = piece.astype(bf16)


def last_product(meta, own, other, stem, factor):
    blocks, rows, width = own.shape
    count = stem.shape[0]
    return call(
        last_body,
        jax.ShapeDtypeStruct((blocks, 2 * rows, width), bf16),
        [SMEM_SPEC] + [VMEM_SPEC] * 4,
        [
            pltpu.VMEM((2, count, 2 * width), bf16),
            pltpu.VMEM((blocks * rows, 2 * width), bf16),
            pltpu.VMEM((width // 128, 2 * blocks * rows, 128), f32),
            pltpu.SemaphoreType.DMA,
        ],
        flops=16 * blocks * rows * width * width,
        moved=20 * width * width,
    )(meta, own, other, stem, factor)


def on_device(size, stem_tensor, leaf_left, leaf_right, slice_bits):
    width = stem_tensor.shape[1]
    place = lax.axis_index("outer").astype(jnp.int32)
    meta = jnp.concatenate([place[None], slice_bits.astype(jnp.int32)])
    sums = {}
    for branches in GROUPS:
        planes = full_sum(meta, leaf_left, leaf_right, branches, size)
        for at, j in enumerate(branches):
            sums[j] = in_order(meta, planes, at)
    spread = lax.all_to_all(stem_tensor[0], "outer", split_axis=0, concat_axis=0, tiled=True)
    right = prepare(meta, spread)
    state = first_product(meta, *sums[0], right).reshape(width, 2 * width)
    state = lax.all_to_all(state, "outer", split_axis=0, concat_axis=0, tiled=True)
    factor = joined_right(meta, *sums[1], *sums[3]).reshape(2, width, 2 * width)
    result = last_product(meta, *sums[2], state, factor)
    return result.reshape(stem_tensor.shape)


def solution(mesh):
    return jax.shard_map(
        functools.partial(on_device, mesh.shape["outer"]),
        mesh=mesh,
        in_specs=(
            P(("cuts", "outer"), None, None, None),
            P(None, None, "outer", None, None),
            P(None, None, "outer", None, None),
            P("cuts"),
        ),
        out_specs=P(("cuts", "outer"), None, None, None),
        check_vma=False,
    )
```

time: 343 us -> 166 us (0.48)
  blocking collectives: 182 us -> 0 us
  local copies, waits for them, and re-layouts: 69.2 us -> 6.13 us
  starting transfers between devices: 10.9 us -> 62 us
  Pallas kernels: 0 us -> 33.6 us
  matrix products: 16.1 us -> 0 us
  waiting for transfers between devices: 47.1 us -> 60.4 us
  between operations: 7.62 us -> 0.24 us
  other arithmetic: 8.63 us -> 2.09 us
    psum x1 -> x0, blocking collectives: 182 us -> none  [on_device(): lax.psum((leaf_term(leaves[0][0], leaves[0][1], width), leaf_term(leaves[...]
    ppermute x0 -> x32, waiting for transfers between devices: none -> 60.4 us  [swap_with(): return lax.ppermute(x, 'outer', [(i, i ^ mask) for i in range(size)])]
    all_to_all x2, waiting for transfers between devices: 47.1 us -> 0.01 us  [the longest x1 0.01 us: on_device(): lax.all_to_all(stem_tensor[0], 'outer', split_axis=0, concat_axis=0, tile...]
    ppermute x0 -> x32, starting transfers between devices: none -> 45.8 us  [swap_with(): return lax.ppermute(x, 'outer', [(i, i ^ mask) for i in range(size)])]
    pallas_call x0 -> x20, Pallas kernels: none -> 33.6 us  [the longest x4 15.5 us: leaf_partials(): call(functools.partial(leaf_body, branches), (jax.ShapeDtypeStruct(shape,...]
    unnamed x21 -> x8, local copies, waits for them, and re-layouts: 25.6 us -> 3.89 us
    slice x3 -> x0, local copies, waits for them, and re-layouts: 19.2 us -> none  [the longest x1 8.94 us: on_device(): leaf_left[branch_index]]
    dot_general x12 -> x0, matrix products: 16.1 us -> none  [the longest x4 10.3 us: leaf_term(): lax.dot_general(left_leaf.reshape(depth, 2 * row_count), right_leaf.resha...]
  transfers between devices with their start and end apart: 2 -> 34, of which waited for: 2 -> 13; matrix products, arithmetic and copies ran while one was open for 1% -> 1% of each run, Pallas kernels for 0% -> 16%
where the time goes in v1:
time: 166 us; the launch traced here: 165 us
  starting transfers between devices  62 us (37%)
  waiting for transfers between devices  60.4 us (36%)
  Pallas kernels  33.6 us (20%)
  local copies, waits for them, and re-layouts  6.13 us (4%)
  other arithmetic  2.09 us (1%)
    ppermute x32, waiting for transfers between devices, swap_with(): return lax.ppermute(x, 'outer', [(i, i ^ mask) for i in range(size)])  60.4 us
    ppermute x32, starting transfers between devices, swap_with(): return lax.ppermute(x, 'outer', [(i, i ^ mask) for i in range(size)])  45.8 us
    pallas_call x4, Pallas kernels, leaf_partials(): call(functools.partial(leaf_body, branches), (jax.ShapeDtypeStruct(shape,...  15.5 us
    all_to_all x1, starting transfers between devices, on_device(): lax.all_to_all(state, 'outer', split_axis=0, concat_axis=0, tiled=True)  10.6 us
    pallas_call x12, Pallas kernels, add_and_split(): call(functools.partial(add_body, shift), (jax.ShapeDtypeStruct(shape, f32...  7.32 us
    all_to_all x1, starting transfers between devices, on_device(): lax.all_to_all(stem_tensor[0], 'outer', split_axis=0, concat_axis=0, tile...  5.63 us
    unnamed x8, local copies, waits for them, and re-layouts  3.89 us
  transfers between devices with their start and end apart: 34, of which 13 were waited for; matrix products, arithmetic and copies ran while one was open for 1% of the time, Pallas kernels for 16%

profile of v1, /device:TPU:11, one launch (start us, length us, event | category | flops | bytes accessed | tf_op | source)
XLA Modules:
  0.0 164.5 jit_solution(5486669021638583478)
XLA Ops:
  0.7 3.9 %shard_map.50 = (f32[1,512,512]{2,1,0:T(8,128)S(1)}, bf16[1,512,512]{2,1,0:T(8,128)(2,1)S(1)}) custom-call(s32[5]{0:T(128)S(1)} %pad_add_fusion.meta, bf16[4,2,512,2,512]{4,3,2,1,0:T(2,128)(2,1)} %left.7, bf16[4,2,512,2,512]{4,3,2,1,0:T(2,128)(2,1)} %right.7), custom_call_target="tpu_custom_call" | custom-call | flops 1073741824 | bytes 2097152 | tf_op jit(solution)/shard_map/pallas_call | solution.py:68
  8.8 5.6 %all-to-all-start = ((bf16[512,2,512]{2,1,0:T(2,128)(2,1)}), bf16[512,2,512]{2,1,0:T(2,128)(2,1)S(1)}, u32[]{:S(2)}, u32[]{:S(2)}) async-start(bf16[512,2,512]{2,1,0:T(2,128)(2,1)} %bitcast.7), calls=%async_computation | async-start | bytes 2097152 | tf_op jit(solution)/shard_map/all_to_all | solution.py:294
  15.9 3.9 %shard_map.60 = (f32[1,512,512]{2,1,0:T(8,128)S(1)}, bf16[1,512,512]{2,1,0:T(8,128)(2,1)S(1)}) custom-call(s32[5]{0:T(128)S(1)} %pad_add_fusion.meta, bf16[4,2,512,2,512]{4,3,2,1,0:T(2,128)(2,1)} %left.7, bf16[4,2,512,2,512]{4,3,2,1,0:T(2,128)(2,1)} %right.7), custom_call_target="tpu_custom_call" | custom-call | flops 1073741824 | bytes 2097152 | tf_op jit(solution)/shard_map/pallas_call | solution.py:68
  21.4 14.3 %collective-permute-done.10.recv = bf16[1,128,512]{2,1,0:T(8,128)(2,1)S(1)} collective-permute-done((bf16[1,128,512]{2,1,0:T(8,128)(2,1)S(1)}, bf16[1,128,512]{2,1,0:T(8,128)(2,1)S(1)}, u32[]{:S(2)}, u32[]{:S(2)}) %collective-permute-start.10) | collective-permute-done | bytes 131104 | tf_op jit(solution)/shard_map/ppermute | solution.py:112
  37.2 3.9 %shard_map.56 = (f32[1,512,512]{2,1,0:T(8,128)S(1)}, bf16[1,512,512]{2,1,0:T(8,128)(2,1)S(1)}) custom-call(s32[5]{0:T(128)S(1)} %pad_add_fusion.meta, bf16[4,2,512,2,512]{4,3,2,1,0:T(2,128)(2,1)} %left.7, bf16[4,2,512,2,512]{4,3,2,1,0:T(2,128)(2,1)} %right.7), custom_call_target="tpu_custom_call" | custom-call | flops 1073741824 | bytes 2097152 | tf_op jit(solution)/shard_map/pallas_call | solution.py:68
  43.5 3.9 %shard_map.46 = (f32[1,512,512]{2,1,0:T(8,128)S(1)}, bf16[1,512,512]{2,1,0:T(8,128)(2,1)S(1)}) custom-call(s32[5]{0:T(128)S(1)} %pad_add_fusion.meta, bf16[4,2,512,2,512]{4,3,2,1,0:T(2,128)(2,1)} %left.7, bf16[4,2,512,2,512]{4,3,2,1,0:T(2,128)(2,1)} %right.7), custom_call_target="tpu_custom_call" | custom-call | flops 1073741824 | bytes 2097152 | tf_op jit(solution)/shard_map/pallas_call | solution.py:68
  50.0 3.4 %collective-permute-done.13 = bf16[2,1,64,512]{3,2,0,1:T(8,128)(2,1)S(1)} collective-permute-done((bf16[2,1,64,512]{3,2,0,1:T(8,128)(2,1)S(1)}, bf16[2,1,64,512]{3,2,0,1:T(8,128)(2,1)S(1)}, u32[]{:S(2)}, u32[]{:S(2)}) %collective-permute-start.13) | collective-permute-done | bytes 131104 | tf_op jit(solution)/shard_map/ppermute | solution.py:112
  60.4 3.6 %collective-permute-start.15 = (bf16[8,1,64,512]{3,2,0,1:T(8,128)(2,1)S(1)}, bf16[8,1,64,512]{3,2,0,1:T(8,128)(2,1)S(1)}, u32[]{:S(2)}, u32[]{:S(2)}) collective-permute-start(bf16[8,1,64,512]{3,2,0,1:T(8,128)(2,1)S(1)} %get-tuple-element.73), channel_id=1, source_target_pairs={{0,1},{1,0},{2,3},{3,2},{4,5},{5,4},{6,7},{7,6},{8,9},{9,8},{10,11... | collective-permute-start | bytes 1572872 | tf_op jit(solution)/shard_map/ppermute | solution.py:112
  67.4 4.1 %collective-permute-done.17.recv = bf16[1,256,512]{2,1,0:T(8,128)(2,1)S(1)} collective-permute-done((bf16[1,256,512]{2,1,0:T(8,128)(2,1)S(1)}, bf16[1,256,512]{2,1,0:T(8,128)(2,1)S(1)}, u32[]{:S(2)}, u32[]{:S(2)}) %collective-permute-start.17) | collective-permute-done | bytes 262176 | tf_op jit(solution)/shard_map/ppermute | solution.py:112
  73.0 4.1 %collective-permute-done.1.recv = bf16[1,256,512]{2,1,0:T(8,128)(2,1)S(1)} collective-permute-done((bf16[1,256,512]{2,1,0:T(8,128)(2,1)S(1)}, bf16[1,256,512]{2,1,0:T(8,128)(2,1)S(1)}, u32[]{:S(2)}, u32[]{:S(2)}) %collective-permute-start.1) | collective-permute-done | bytes 262176 | tf_op jit(solution)/shard_map/ppermute | solution.py:112
  79.2 2.1 %collective-permute-start.27 = (bf16[1,64,512]{2,1,0:T(8,128)(2,1)S(1)}, bf16[1,64,512]{2,1,0:T(8,128)(2,1)S(1)}, u32[]{:S(2)}, u32[]{:S(2)}) collective-permute-start(bf16[1,64,512]{2,1,0:T(8,128)(2,1)S(1)} %get-tuple-element.68), channel_id=1, source_target_pairs={{0,8},{1,9},{2,10},{3,11},{4,12},{5,13},{6,14},{7,15},{8,0},{9,1},... | collective-permute-start | bytes 196616 | tf_op jit(solution)/shard_map/ppermute | solution.py:112
  82.9 2.1 %collective-permute-start.3 = (bf16[1,64,512]{2,1,0:T(8,128)(2,1)S(1)}, bf16[1,64,512]{2,1,0:T(8,128)(2,1)S(1)}, u32[]{:S(2)}, u32[]{:S(2)}) collective-permute-start(bf16[1,64,512]{2,1,0:T(8,128)(2,1)S(1)} %get-tuple-element.44), channel_id=1, source_target_pairs={{0,8},{1,9},{2,10},{3,11},{4,12},{5,13},{6,14},{7,15},{8,0},{9,1},... | collective-permute-start | bytes 196616 | tf_op jit(solution)/shard_map/ppermute | solution.py:112
  85.8 2.7 %shard_map.54.right = bf16[2,512,1024]{2,1,0:T(8,128)(2,1)S(1)} custom-call(s32[5]{0:T(128)S(1)} %pad_add_fusion.meta, bf16[512,2,512]{2,1,0:T(2,128)(2,1)S(1)} %all-to-all-done.stem), custom_call_target="tpu_custom_call" | custom-call | bytes 3145728 | tf_op jit(solution)/shard_map/pallas_call | solution.py:165
  88.5 2.8 %shard_map.55 = bf16[8,64,1024]{2,1,0:T(8,128)(2,1)} custom-call(s32[5]{0:T(128)S(1)} %pad_add_fusion.meta, bf16[8,64,512]{2,1,0:T(8,128)(2,1)S(1)} %get-tuple-element.74.own, bf16[8,64,512]{2,1,0:T(8,128)(2,1)S(1)} %bitcast.27, bf16[2,512,1024]{2,1,0:T(8,128)(2,1)S(1)} %shard_map.54.right), custom_call_target="tpu_custom_call" | custom-call | flops 1073741824 | bytes 2621440 | tf_op jit(solution)/shard_map/pallas_call | solution.py:190
  91.4 10.6 %all-to-all-start.1 = ((bf16[16,32,1024]{2,1,0:T(8,128)(2,1)}), bf16[16,32,1024]{2,1,0:T(8,128)(2,1)S(1)}, u32[]{:S(2)}, u32[]{:S(2)}) async-start(bf16[16,32,1024]{2,1,0:T(8,128)(2,1)} %bitcast.8), calls=%async_computation.1 | async-start | bytes 2097152 | tf_op jit(solution)/shard_map/all_to_all | solution.py:297
  102.0 2.2 %collective-permute-start.20 = (bf16[1,1,64,512]{3,2,0,1:T(8,128)(2,1)S(1)}, bf16[1,1,64,512]{3,2,0,1:T(8,128)(2,1)S(1)}, u32[]{:S(2)}, u32[]{:S(2)}) collective-permute-start(bf16[1,1,64,512]{3,2,0,1:T(8,128)(2,1)S(1)} %fusion.2), channel_id=1, source_target_pairs={{0,8},{1,9},{2,10},{3,11},{4,12},{5,13},{6,14},{7,15},{8,0},{9,1},... | collective-permute-start | bytes 196616 | tf_op jit(solution)/shard_map/ppermute | solution.py:112
  104.8 24.2 %collective-permute-done.20 = bf16[1,1,64,512]{3,2,0,1:T(8,128)(2,1)S(1)} collective-permute-done((bf16[1,1,64,512]{3,2,0,1:T(8,128)(2,1)S(1)}, bf16[1,1,64,512]{3,2,0,1:T(8,128)(2,1)S(1)}, u32[]{:S(2)}, u32[]{:S(2)}) %collective-permute-start.20) | collective-permute-done | bytes 65568 | tf_op jit(solution)/shard_map/ppermute | solution.py:112
  129.0 3.2 %collective-permute-start.21 = (bf16[2,1,64,512]{3,2,0,1:T(8,128)(2,1)S(1)}, bf16[2,1,64,512]{3,2,0,1:T(8,128)(2,1)S(1)}, u32[]{:S(2)}, u32[]{:S(2)}) collective-permute-start(bf16[2,1,64,512]{3,2,0,1:T(8,128)(2,1)S(1)} %pad_maximum_fusion.10), channel_id=1, source_target_pairs={{0,4},{1,5},{2,6},{3,7},{4,0},{5,1},{6,2},{7,3},{8,12},{9,13},{10,... | collective-permute-start | bytes 393224 | tf_op jit(solution)/shard_map/ppermute | solution.py:112
  139.1 4.1 %collective-permute-start.31 = (bf16[8,1,64,512]{3,2,0,1:T(8,128)(2,1)S(1)}, bf16[8,1,64,512]{3,2,0,1:T(8,128)(2,1)S(1)}, u32[]{:S(2)}, u32[]{:S(2)}) collective-permute-start(bf16[8,1,64,512]{3,2,0,1:T(8,128)(2,1)S(1)} %get-tuple-element.69), channel_id=1, source_target_pairs={{0,1},{1,0},{2,3},{3,2},{4,5},{5,4},{6,7},{7,6},{8,9},{9,8},{10,11... | collective-permute-start | bytes 1572872 | tf_op jit(solution)/shard_map/ppermute | solution.py:112
  144.1 4.8 %collective-permute-start.23 = (bf16[8,1,64,512]{3,2,0,1:T(8,128)(2,1)S(1)}, bf16[8,1,64,512]{3,2,0,1:T(8,128)(2,1)S(1)}, u32[]{:S(2)}, u32[]{:S(2)}) collective-permute-start(bf16[8,1,64,512]{3,2,0,1:T(8,128)(2,1)S(1)} %get-tuple-element.71), channel_id=1, source_target_pairs={{0,1},{1,0},{2,3},{3,2},{4,5},{5,4},{6,7},{7,6},{8,9},{9,8},{10,11... | collective-permute-start | bytes 1572872 | tf_op jit(solution)/shard_map/ppermute | solution.py:112
  150.6 2.5 %collective-permute-start.7 = (bf16[8,1,64,512]{3,2,0,1:T(8,128)(2,1)S(1)}, bf16[8,1,64,512]{3,2,0,1:T(8,128)(2,1)S(1)}, u32[]{:S(2)}, u32[]{:S(2)}) collective-permute-start(bf16[8,1,64,512]{3,2,0,1:T(8,128)(2,1)S(1)} %get-tuple-element.75), channel_id=1, source_target_pairs={{0,1},{1,0},{2,3},{3,2},{4,5},{5,4},{6,7},{7,6},{8,9},{9,8},{10,11... | collective-permute-start | bytes 1572872 | tf_op jit(solution)/shard_map/ppermute | solution.py:112
  153.1 2.0 %shard_map.64 = bf16[2,8,64,1024]{3,2,1,0:T(8,128)(2,1)S(1)} custom-call(s32[5]{0:T(128)S(1)} %pad_add_fusion.meta, bf16[8,64,512]{2,1,0:T(8,128)(2,1)S(1)} %get-tuple-element.72.own0, bf16[8,64,512]{2,1,0:T(8,128)(2,1)S(1)} %bitcast.29, bf16[8,64,512]{2,1,0:T(8,128)(2,1)S(1)} %get-tuple-element.70.own1, bf16[8,64,512]{2,1,0:T(8,128)(2,1)S(1)} %bitcast.28), custom_call_target="tpu_custom_call" | custom-call | flops 1073741824 | bytes 4194304 | tf_op jit(solution)/shard_map/pallas_call | solution.py:230
  158.0 3.2 %shard_map.65 = bf16[8,128,512]{2,1,0:T(8,128)(2,1)S(1)} custom-call(s32[5]{0:T(128)S(1)} %pad_add_fusion.meta, bf16[8,64,512]{2,1,0:T(8,128)(2,1)S(1)} %copy-done.1, bf16[8,64,512]{2,1,0:T(8,128)(2,1)S(1)} %bitcast.30, bf16[512,1024]{1,0:T(8,128)(2,1)S(1)} %bitcast.26, bf16[2,512,1024]{2,1,0:T(8,128)(2,1)S(1)} %bitcast.25), custom_call_target="tpu_custom_call" | custom-call | flops 2147483648 | bytes 5242880 | tf_op jit(solution)/shard_map/pallas_call | solution.py:270
  162.3 2.2 %reshape.11 = bf16[1,512,2,512]{3,2,1,0:T(2,128)(2,1)} reshape(bf16[8,128,512]{2,1,0:T(8,128)(2,1)} %copy-done) | data formatting | bytes 2097152 | tf_op jit(solution)/shard_map/reshape | solution.py:300
  (90 shorter events, 44.9 us)
Async XLA Ops:
  7.5 7.6 %collective-permute-start.9 = (bf16[1,256,512]{2,1,0:T(8,128)(2,1)S(1)}, bf16[1,256,512]{2,1,0:T(8,128)(2,1)S(1)}, u32[]{:S(2)}, u32[]{:S(2)}) collective-permute-start(bf16[1,256,512]{2,1,0:T(8,128)(2,1)S(1)} %get-tuple-element.48), channel_id=1, source_target_pairs={{0,2},{1,3},{2,0},{3,1},{4,6},{5,7},{6,4},{7,5},{8,10},{9,11},{10,... | collective-permute-start | bytes 786440 | tf_op jit(solution)/shard_map/ppermute | solution.py:112
  8.8 77.0 %all-to-all-start = ((bf16[512,2,512]{2,1,0:T(2,128)(2,1)}), bf16[512,2,512]{2,1,0:T(2,128)(2,1)S(1)}, u32[]{:S(2)}, u32[]{:S(2)}) async-start(bf16[512,2,512]{2,1,0:T(2,128)(2,1)} %bitcast.7), calls=%async_computation | async-start | bytes 2097152 | tf_op jit(solution)/shard_map/all_to_all | solution.py:294
  15.7 19.9 %collective-permute-start.10 = (bf16[1,128,512]{2,1,0:T(8,128)(2,1)S(1)}, bf16[1,128,512]{2,1,0:T(8,128)(2,1)S(1)}, u32[]{:S(2)}, u32[]{:S(2)}) collective-permute-start(bf16[1,128,512]{2,1,0:T(8,128)(2,1)S(1)} %get-tuple-element.50), channel_id=1, source_target_pairs={{0,4},{1,5},{2,6},{3,7},{4,0},{5,1},{6,2},{7,3},{8,12},{9,13},{10,... | collective-permute-start | bytes 393224 | tf_op jit(solution)/shard_map/ppermute | solution.py:112
  19.8 34.9 %collective-permute-start.24 = (bf16[1,512,512]{2,1,0:T(8,128)(2,1)S(1)}, bf16[1,512,512]{2,1,0:T(8,128)(2,1)S(1)}, u32[]{:S(2)}, u32[]{:S(2)}) collective-permute-start(bf16[1,512,512]{2,1,0:T(8,128)(2,1)S(1)} %get-tuple-element.62), channel_id=1, source_target_pairs={{0,1},{1,0},{2,3},{3,2},{4,5},{5,4},{6,7},{7,6},{8,9},{9,8},{10,11... | collective-permute-start | bytes 1572872 | tf_op jit(solution)/shard_map/ppermute | solution.py:112
  41.1 14.6 %collective-permute-start.16 = (bf16[1,512,512]{2,1,0:T(8,128)(2,1)S(1)}, bf16[1,512,512]{2,1,0:T(8,128)(2,1)S(1)}, u32[]{:S(2)}, u32[]{:S(2)}) collective-permute-start(bf16[1,512,512]{2,1,0:T(8,128)(2,1)S(1)} %get-tuple-element.54), channel_id=1, source_target_pairs={{0,1},{1,0},{2,3},{3,2},{4,5},{5,4},{6,7},{7,6},{8,9},{9,8},{10,11... | collective-permute-start | bytes 1572872 | tf_op jit(solution)/shard_map/ppermute | solution.py:112
  47.4 10.2 %collective-permute-start = (bf16[1,512,512]{2,1,0:T(8,128)(2,1)S(1)}, bf16[1,512,512]{2,1,0:T(8,128)(2,1)S(1)}, u32[]{:S(2)}, u32[]{:S(2)}) collective-permute-start(bf16[1,512,512]{2,1,0:T(8,128)(2,1)S(1)} %get-tuple-element.38), channel_id=1, source_target_pairs={{0,1},{1,0},{2,3},{3,2},{4,5},{5,4},{6,7},{7,6},{8,9},{9,8},{10,11... | collective-permute-start | bytes 1572872 | tf_op jit(solution)/shard_map/ppermute | solution.py:112
  55.4 10.5 %collective-permute-start.25 = (bf16[1,256,512]{2,1,0:T(8,128)(2,1)S(1)}, bf16[1,256,512]{2,1,0:T(8,128)(2,1)S(1)}, u32[]{:S(2)}, u32[]{:S(2)}) collective-permute-start(bf16[1,256,512]{2,1,0:T(8,128)(2,1)S(1)} %get-tuple-element.64), channel_id=1, source_target_pairs={{0,2},{1,3},{2,0},{3,1},{4,6},{5,7},{6,4},{7,5},{8,10},{9,11},{10,... | collective-permute-start | bytes 786440 | tf_op jit(solution)/shard_map/ppermute | solution.py:112
  56.4 15.1 %collective-permute-start.17 = (bf16[1,256,512]{2,1,0:T(8,128)(2,1)S(1)}, bf16[1,256,512]{2,1,0:T(8,128)(2,1)S(1)}, u32[]{:S(2)}, u32[]{:S(2)}) collective-permute-start(bf16[1,256,512]{2,1,0:T(8,128)(2,1)S(1)} %get-tuple-element.56), channel_id=1, source_target_pairs={{0,2},{1,3},{2,0},{3,1},{4,6},{5,7},{6,4},{7,5},{8,10},{9,11},{10,... | collective-permute-start | bytes 786440 | tf_op jit(solution)/shard_map/ppermute | solution.py:112
  58.3 18.8 %collective-permute-start.1 = (bf16[1,256,512]{2,1,0:T(8,128)(2,1)S(1)}, bf16[1,256,512]{2,1,0:T(8,128)(2,1)S(1)}, u32[]{:S(2)}, u32[]{:S(2)}) collective-permute-start(bf16[1,256,512]{2,1,0:T(8,128)(2,1)S(1)} %get-tuple-element.40), channel_id=1, source_target_pairs={{0,2},{1,3},{2,0},{3,1},{4,6},{5,7},{6,4},{7,5},{8,10},{9,11},{10,... | collective-permute-start | bytes 786440 | tf_op jit(solution)/shard_map/ppermute | solution.py:112
  60.4 28.2 %collective-permute-start.15 = (bf16[8,1,64,512]{3,2,0,1:T(8,128)(2,1)S(1)}, bf16[8,1,64,512]{3,2,0,1:T(8,128)(2,1)S(1)}, u32[]{:S(2)}, u32[]{:S(2)}) collective-permute-start(bf16[8,1,64,512]{3,2,0,1:T(8,128)(2,1)S(1)} %get-tuple-element.73), channel_id=1, source_target_pairs={{0,1},{1,0},{2,3},{3,2},{4,5},{5,4},{6,7},{7,6},{8,9},{9,8},{10,11... | collective-permute-start | bytes 1572872 | tf_op jit(solution)/shard_map/ppermute | solution.py:112
  66.5 12.1 %collective-permute-start.26 = (bf16[1,128,512]{2,1,0:T(8,128)(2,1)S(1)}, bf16[1,128,512]{2,1,0:T(8,128)(2,1)S(1)}, u32[]{:S(2)}, u32[]{:S(2)}) collective-permute-start(bf16[1,128,512]{2,1,0:T(8,128)(2,1)S(1)} %get-tuple-element.66), channel_id=1, source_target_pairs={{0,4},{1,5},{2,6},{3,7},{4,0},{5,1},{6,2},{7,3},{8,12},{9,13},{10,... | collective-permute-start | bytes 393224 | tf_op jit(solution)/shard_map/ppermute | solution.py:112
  72.1 9.1 %collective-permute-start.18 = (bf16[1,128,512]{2,1,0:T(8,128)(2,1)S(1)}, bf16[1,128,512]{2,1,0:T(8,128)(2,1)S(1)}, u32[]{:S(2)}, u32[]{:S(2)}) collective-permute-start(bf16[1,128,512]{2,1,0:T(8,128)(2,1)S(1)} %get-tuple-element.58), channel_id=1, source_target_pairs={{0,4},{1,5},{2,6},{3,7},{4,0},{5,1},{6,2},{7,3},{8,12},{9,13},{10,... | collective-permute-start | bytes 393224 | tf_op jit(solution)/shard_map/ppermute | solution.py:112
  81.8 20.2 %collective-permute-start.19 = (bf16[1,64,512]{2,1,0:T(8,128)(2,1)S(1)}, bf16[1,64,512]{2,1,0:T(8,128)(2,1)S(1)}, u32[]{:S(2)}, u32[]{:S(2)}) collective-permute-start(bf16[1,64,512]{2,1,0:T(8,128)(2,1)S(1)} %get-tuple-element.60), channel_id=1, source_target_pairs={{0,8},{1,9},{2,10},{3,11},{4,12},{5,13},{6,14},{7,15},{8,0},{9,1},... | collective-permute-start | bytes 196616 | tf_op jit(solution)/shard_map/ppermute | solution.py:112
  82.9 21.7 %collective-permute-start.3 = (bf16[1,64,512]{2,1,0:T(8,128)(2,1)S(1)}, bf16[1,64,512]{2,1,0:T(8,128)(2,1)S(1)}, u32[]{:S(2)}, u32[]{:S(2)}) collective-permute-start(bf16[1,64,512]{2,1,0:T(8,128)(2,1)S(1)} %get-tuple-element.44), channel_id=1, source_target_pairs={{0,8},{1,9},{2,10},{3,11},{4,12},{5,13},{6,14},{7,15},{8,0},{9,1},... | collective-permute-start | bytes 196616 | tf_op jit(solution)/shard_map/ppermute | solution.py:112
  84.9 19.3 %collective-permute-start.28 = (bf16[1,1,64,512]{3,2,0,1:T(8,128)(2,1)S(1)}, bf16[1,1,64,512]{3,2,0,1:T(8,128)(2,1)S(1)}, u32[]{:S(2)}, u32[]{:S(2)}) collective-permute-start(bf16[1,1,64,512]{3,2,0,1:T(8,128)(2,1)S(1)} %fusion.3), channel_id=1, source_target_pairs={{0,8},{1,9},{2,10},{3,11},{4,12},{5,13},{6,14},{7,15},{8,0},{9,1},... | collective-permute-start | bytes 196616 | tf_op jit(solution)/shard_map/ppermute | solution.py:112
  91.4 64.5 %all-to-all-start.1 = ((bf16[16,32,1024]{2,1,0:T(8,128)(2,1)}), bf16[16,32,1024]{2,1,0:T(8,128)(2,1)S(1)}, u32[]{:S(2)}, u32[]{:S(2)}) async-start(bf16[16,32,1024]{2,1,0:T(8,128)(2,1)} %bitcast.8), calls=%async_computation.1 | async-start | bytes 2097152 | tf_op jit(solution)/shard_map/all_to_all | solution.py:297
  102.0 26.9 %collective-permute-start.20 = (bf16[1,1,64,512]{3,2,0,1:T(8,128)(2,1)S(1)}, bf16[1,1,64,512]{3,2,0,1:T(8,128)(2,1)S(1)}, u32[]{:S(2)}, u32[]{:S(2)}) collective-permute-start(bf16[1,1,64,512]{3,2,0,1:T(8,128)(2,1)S(1)} %fusion.2), channel_id=1, source_target_pairs={{0,8},{1,9},{2,10},{3,11},{4,12},{5,13},{6,14},{7,15},{8,0},{9,1},... | collective-permute-start | bytes 196616 | tf_op jit(solution)/shard_map/ppermute | solution.py:112
  104.2 28.0 %collective-permute-start.29 = (bf16[2,1,64,512]{3,2,0,1:T(8,128)(2,1)S(1)}, bf16[2,1,64,512]{3,2,0,1:T(8,128)(2,1)S(1)}, u32[]{:S(2)}, u32[]{:S(2)}) collective-permute-start(bf16[2,1,64,512]{3,2,0,1:T(8,128)(2,1)S(1)} %pad_maximum_fusion.11), channel_id=1, source_target_pairs={{0,4},{1,5},{2,6},{3,7},{4,0},{5,1},{6,2},{7,3},{8,12},{9,13},{10,... | collective-permute-start | bytes 393224 | tf_op jit(solution)/shard_map/ppermute | solution.py:112
  104.6 28.9 %collective-permute-start.4 = (bf16[1,1,64,512]{3,2,0,1:T(8,128)(2,1)S(1)}, bf16[1,1,64,512]{3,2,0,1:T(8,128)(2,1)S(1)}, u32[]{:S(2)}, u32[]{:S(2)}) collective-permute-start(bf16[1,1,64,512]{3,2,0,1:T(8,128)(2,1)S(1)} %fusion), channel_id=1, source_target_pairs={{0,8},{1,9},{2,10},{3,11},{4,12},{5,13},{6,14},{7,15},{8,0},{9,1},... | collective-permute-start | bytes 196616 | tf_op jit(solution)/shard_map/ppermute | solution.py:112
  132.2 6.9 %collective-permute-start.30 = (bf16[4,1,64,512]{3,2,0,1:T(8,128)(2,1)S(1)}, bf16[4,1,64,512]{3,2,0,1:T(8,128)(2,1)S(1)}, u32[]{:S(2)}, u32[]{:S(2)}) collective-permute-start(bf16[4,1,64,512]{3,2,0,1:T(8,128)(2,1)S(1)} %pad_maximum_fusion.7), channel_id=1, source_target_pairs={{0,2},{1,3},{2,0},{3,1},{4,6},{5,7},{6,4},{7,5},{8,10},{9,11},{10,... | collective-permute-start | bytes 786440 | tf_op jit(solution)/shard_map/ppermute | solution.py:112
  134.6 9.5 %collective-permute-start.22 = (bf16[4,1,64,512]{3,2,0,1:T(8,128)(2,1)S(1)}, bf16[4,1,64,512]{3,2,0,1:T(8,128)(2,1)S(1)}, u32[]{:S(2)}, u32[]{:S(2)}) collective-permute-start(bf16[4,1,64,512]{3,2,0,1:T(8,128)(2,1)S(1)} %pad_maximum_fusion.6), channel_id=1, source_target_pairs={{0,2},{1,3},{2,0},{3,1},{4,6},{5,7},{6,4},{7,5},{8,10},{9,11},{10,... | collective-permute-start | bytes 786440 | tf_op jit(solution)/shard_map/ppermute | solution.py:112
  137.8 11.9 %collective-permute-start.6 = (bf16[4,1,64,512]{3,2,0,1:T(8,128)(2,1)S(1)}, bf16[4,1,64,512]{3,2,0,1:T(8,128)(2,1)S(1)}, u32[]{:S(2)}, u32[]{:S(2)}) collective-permute-start(bf16[4,1,64,512]{3,2,0,1:T(8,128)(2,1)S(1)} %pad_maximum_fusion.4), channel_id=1, source_target_pairs={{0,2},{1,3},{2,0},{3,1},{4,6},{5,7},{6,4},{7,5},{8,10},{9,11},{10,... | collective-permute-start | bytes 786440 | tf_op jit(solution)/shard_map/ppermute | solution.py:112
  139.1 14.0 %collective-permute-start.31 = (bf16[8,1,64,512]{3,2,0,1:T(8,128)(2,1)S(1)}, bf16[8,1,64,512]{3,2,0,1:T(8,128)(2,1)S(1)}, u32[]{:S(2)}, u32[]{:S(2)}) collective-permute-start(bf16[8,1,64,512]{3,2,0,1:T(8,128)(2,1)S(1)} %get-tuple-element.69), channel_id=1, source_target_pairs={{0,1},{1,0},{2,3},{3,2},{4,5},{5,4},{6,7},{7,6},{8,9},{9,8},{10,11... | collective-permute-start | bytes 1572872 | tf_op jit(solution)/shard_map/ppermute | solution.py:112
  144.1 9.0 %collective-permute-start.23 = (bf16[8,1,64,512]{3,2,0,1:T(8,128)(2,1)S(1)}, bf16[8,1,64,512]{3,2,0,1:T(8,128)(2,1)S(1)}, u32[]{:S(2)}, u32[]{:S(2)}) collective-permute-start(bf16[8,1,64,512]{3,2,0,1:T(8,128)(2,1)S(1)} %get-tuple-element.71), channel_id=1, source_target_pairs={{0,1},{1,0},{2,3},{3,2},{4,5},{5,4},{6,7},{7,6},{8,9},{9,8},{10,11... | collective-permute-start | bytes 1572872 | tf_op jit(solution)/shard_map/ppermute | solution.py:112
  (14 other events, 54.8 us)

commit v2 on v0

v2 whole, which is shorter than its diff:
```python
import functools

import jax
import jax.numpy as jnp
from jax import lax
from jax.experimental import pallas as pl
from jax.experimental.pallas import tpu as pltpu
from jax.sharding import PartitionSpec as P

VMEM_LIMIT = 48 << 20
TILE = 256
bf16, f32 = jnp.bfloat16, jnp.float32

SMEM_SPEC = pl.BlockSpec(memory_space=pltpu.SMEM)
VMEM_SPEC = pl.BlockSpec(memory_space=pltpu.VMEM)
ANY_SPEC = pl.BlockSpec(memory_space=pl.ANY)


class Chain:
    def __init__(self, meta):
        self.meta, self.last = meta, None

    def __call__(self, body, shapes, in_specs, operands, scratch=(), out_specs=None):
        many = isinstance(shapes, (tuple, list))
        shapes = tuple(shapes) if many else (shapes,)
        specs, extra = [SMEM_SPEC] + list(in_specs), []
        if self.last is not None:
            specs, extra = specs + [ANY_SPEC], [self.last]
        count = len(specs)

        def kernel(*refs):
            body(*refs[: len(in_specs) + 1], *refs[count:])

        out = pl.pallas_call(
            kernel,
            out_shape=shapes,
            in_specs=specs,
            out_specs=tuple(out_specs or [VMEM_SPEC] * len(shapes)),
            scratch_shapes=list(scratch),
            compiler_params=pltpu.CompilerParams(vmem_limit_bytes=VMEM_LIMIT),
            cost_estimate=pl.CostEstimate(flops=0, bytes_accessed=1024, transcendentals=0),
        )(self.meta, *operands, *extra)
        self.last = out[0]
        return out if many else out[0]


def shaped(shape, dtype=bf16):
    return jax.ShapeDtypeStruct(shape, dtype)


def tdot(a, b):
    return lax.dot_general(a, b, (((0,), (0,)), ((), ())), preferred_element_type=f32)


def dot(a, b):
    return jnp.dot(a, b, preferred_element_type=f32)


def reversed_bits(value, bits):
    found = 0
    for at in range(bits):
        found = found + ((value >> at) & 1) * (1 << (bits - 1 - at))
    return found


def block_of(meta, blocks):
    return reversed_bits(meta[0] >> 1, blocks.bit_length() - 1)


def leaf_body(branch, meta, left, right, keep, send, lhs, rhs, both, sems):
    depth, width = left.shape[2], left.shape[4]
    core = meta[0] & 1
    first, second = (right, left) if branch % 2 == 0 else (left, right)
    copies = []
    for which, (ref, buf) in enumerate(((second, rhs), (first, lhs))):
        flat = ref.reshape(ref.shape[0], ref.shape[1], 2 * depth, width)
        copies.append(pltpu.make_async_copy(flat.at[branch, meta[1 + branch]], buf, sems.at[which]))
        copies[-1].start()
    rows = lax.broadcasted_iota(jnp.int32, (2 * depth // 8, 8, width), 1)
    is_real = (rows & 1) == 0
    copies[0].wait()
    wide = rhs[...].astype(f32).reshape(2 * depth // 8, 8, width)
    signed = jnp.where(is_real, wide, -wide)
    swapped = jnp.where(is_real, pltpu.roll(wide, 7, 1), pltpu.roll(wide, 1, 1))
    both[core] = signed.reshape(2 * depth, width).astype(bf16)
    both[1 - core] = swapped.reshape(2 * depth, width).astype(bf16)
    copies[1].wait()
    send[...] = tdot(lhs[...], both[1]).astype(bf16)
    keep[...] = tdot(lhs[...], both[0])


def leaf_partial(chain, left, right, branch):
    depth, width = left.shape[2], left.shape[4]
    return chain(
        functools.partial(leaf_body, branch),
        (shaped((width, width), f32), shaped((width, width))),
        [ANY_SPEC, ANY_SPEC],
        (left, right),
        [
            pltpu.VMEM((2 * depth, width), bf16),
            pltpu.VMEM((2 * depth, width), bf16),
            pltpu.VMEM((2, 2 * depth, width), bf16),
            pltpu.SemaphoreType.DMA((2,)),
        ],
    )


def half_body(shift, meta, keep, recv, keep_out, send_out):
    half = keep_out.shape[0]
    bit = (meta[0] >> shift) & 1
    mine = pl.multiple_of(bit * half, half)
    other = pl.multiple_of((1 - bit) * half, half)
    send_out[...] = (keep[pl.ds(other, half)] + recv[pl.ds(other, half)].astype(f32)).astype(bf16)
    keep_out[...] = keep[pl.ds(mine, half)] + recv[pl.ds(mine, half)].astype(f32)


def halve(chain, keep, recv, shift):
    rows, width = keep.shape
    half = rows // 2
    if half % 16:
        total = (keep + recv.astype(f32)).reshape(2, half, width)
        bit = (chain.meta[0] >> shift) & 1
        return total[bit], total[1 - bit].astype(bf16)
    return chain(
        functools.partial(half_body, shift),
        (shaped((half, width), f32), shaped((half, width))),
        [VMEM_SPEC] * 2,
        (keep, recv),
    )


def spread_body(shift, meta, keep, recv, keep_out, *sends):
    rows = keep_out.shape[0]
    blocks = len(sends) + 1
    me = reversed_bits(meta[0] >> shift, blocks.bit_length() - 1)
    for t in range(blocks):
        at = pl.ds(pl.multiple_of((me ^ t) * rows, rows), rows)
        value = keep[at] + recv[at].astype(f32)
        if t:
            sends[t - 1][...] = value.astype(bf16)
        else:
            keep_out[...] = value


def spread(chain, keep, recv, shift, blocks):
    rows, width = keep.shape[0] // blocks, keep.shape[1]
    return chain(
        functools.partial(spread_body, shift),
        (shaped((rows, width), f32),) + (shaped((rows, width)),) * (blocks - 1),
        [VMEM_SPEC] * 2,
        (keep, recv),
    )


def finish_body(meta, keep, *rest):
    total = keep[...]
    for recv in rest[:-1]:
        total = total + recv[...].astype(f32)
    rest[-1][0] = total.astype(bf16)


def finish(chain, keep, recvs):
    rows, width = keep.shape
    if rows % 16:
        return (keep + sum(recv.astype(f32) for recv in recvs)).astype(bf16)[None]
    return chain(finish_body, shaped((1, rows, width)), [VMEM_SPEC] * (1 + len(recvs)), (keep, *recvs))


def join_body(meta, *refs):
    at = 0
    for ref in refs[:-1]:
        refs[-1][at : at + ref.shape[0]] = ref[...]
        at += ref.shape[0]


def join(chain, parts):
    blocks, rows, width = sum(part.shape[0] for part in parts), *parts[0].shape[1:]
    if rows % 16:
        return jnp.concatenate(parts, axis=0)
    return chain(join_body, shaped((blocks, rows, width)), [VMEM_SPEC] * len(parts), parts)


def swap_with(x, mask, size):
    return lax.ppermute(x, "outer", [(i, i ^ mask) for i in range(size)])


def prepare_body(meta, stem, out, wide):
    count, width = stem.shape[0], stem.shape[2]
    core = meta[0] & 1
    flat = stem[...].reshape(2 * count, width)
    for at in range(width // 128):
        wide[at] = flat[:, at * 128 : (at + 1) * 128].astype(f32)
    for at in range(width // 128):
        here = slice(at * 128, (at + 1) * 128)
        there = slice(width + at * 128, width + (at + 1) * 128)
        real = wide[at, pl.ds(0, count, stride=2), :]
        imag = wide[at, pl.ds(1, count, stride=2), :]
        out[core, :, here] = real.astype(bf16)
        out[core, :, there] = imag.astype(bf16)
        out[1 - core, :, here] = (-imag).astype(bf16)
        out[1 - core, :, there] = real.astype(bf16)


def prepare(chain, stem):
    count, _, width = stem.shape
    return chain(
        prepare_body,
        shaped((2, count, 2 * width)),
        [VMEM_SPEC],
        (stem,),
        [pltpu.VMEM((width // 128, 2 * count, 128), f32)],
    )


def rows_of(refs, width):
    return jnp.concatenate([ref[...].reshape(-1, width) for ref in refs], axis=0)


def layout(planes):
    return sum(part.shape[0] for part in planes), *planes[0].shape[1:]


def first_body(parts, meta, *refs):
    own, other, (right, out) = refs[:parts], refs[parts : 2 * parts], refs[2 * parts :]
    blocks, rows, columns = out.shape
    me = block_of(meta, blocks)
    mine, theirs = rows_of(own, columns // 2), rows_of(other, columns // 2)
    for at in range(columns // TILE):
        here = slice(at * TILE, (at + 1) * TILE)
        value = dot(mine, right[0, :, here]) + dot(theirs, right[1, :, here])
        value = value.astype(bf16).reshape(blocks, rows, TILE)
        for t in range(blocks):
            out[me ^ t, :, here] = value[t]


def first_product(chain, branch, right):
    own, other = branch
    blocks, rows, width = layout(own)
    return chain(
        functools.partial(first_body, len(own)),
        shaped((blocks, rows, 2 * width)),
        [VMEM_SPEC] * (2 * len(own) + 1),
        (*own, *other, right),
    )


def joined_body(parts, meta, *refs):
    own0, other0, own1, other1 = (refs[at * parts : (at + 1) * parts] for at in range(4))
    out, right = refs[4 * parts :]
    _, blocks, rows, columns = out.shape
    width = columns // 2
    me = block_of(meta, blocks)
    core = meta[0] & 1
    t = 0
    for own_ref, other_ref in zip(own1, other1, strict=True):
        for at in range(own_ref.shape[0]):
            own, other = own_ref[at], other_ref[at]
            real = jnp.where(core == 0, own, other)
            imag = jnp.where(core == 0, other, own)
            right[core, me ^ t, :, :width] = real
            right[core, me ^ t, :, width:] = imag
            right[1 - core, me ^ t, :, :width] = -imag
            right[1 - core, me ^ t, :, width:] = real
            t += 1
    mine, theirs = rows_of(own0, width), rows_of(other0, width)
    for at in range(columns // TILE):
        here = slice(at * TILE, (at + 1) * TILE)
        there = slice((at * TILE + width) % columns, (at * TILE + width) % columns + TILE)
        first = right[0, :, :, here].reshape(blocks * rows, TILE)
        second = right[1, :, :, here].reshape(blocks * rows, TILE)
        value = dot(mine, first) + dot(theirs, second)
        turned = value if at * TILE < width else -value
        value = value.astype(bf16).reshape(blocks, rows, TILE)
        turned = turned.astype(bf16).reshape(blocks, rows, TILE)
        for t in range(blocks):
            out[0, me ^ t, :, here] = value[t]
            out[1, me ^ t, :, there] = turned[t]


def joined_right(chain, first, second):
    blocks, rows, width = layout(first[0])
    parts = len(first[0])
    return chain(
        functools.partial(joined_body, parts),
        shaped((2, blocks, rows, 2 * width)),
        [VMEM_SPEC] * (4 * parts),
        (*first[0], *first[1], *second[0], *second[1]),
        [pltpu.VMEM((2, blocks, rows, 2 * width), bf16)],
    )


def last_body(parts, meta, *refs):
    own, other = refs[:parts], refs[parts : 2 * parts]
    stem, factor, out, left, given, both, right, middle, wide, done, sems = refs[2 * parts :]
    _, blocks, rows, width = left.shape
    total = blocks * rows
    core = meta[0] & 1
    me = block_of(meta, blocks)
    copies = [pltpu.make_async_copy(stem, given, sems.at[0]), pltpu.make_async_copy(factor, both, sems.at[1])]
    for plane, refs_of in enumerate((own, other)):
        at = 0
        for ref in refs_of:
            size = ref.shape[0]
            copies.append(pltpu.make_async_copy(ref, left.at[plane, pl.ds(at, size)], sems.at[len(copies)]))
            at += size
    for copy in copies:
        copy.start()
    copies[0].wait()
    value = given[...]
    right[core] = value
    right[1 - core, :, :width] = -value[:, width:]
    right[1 - core, :, width:] = value[:, :width]
    for copy in copies[2:]:
        copy.wait()
    mine = left[0].reshape(total, width)
    theirs = left[1].reshape(total, width)
    for at in range(2 * width // TILE):
        here = slice(at * TILE, (at + 1) * TILE)
        middle[:, here] = (dot(mine, right[0, :, here]) + dot(theirs, right[1, :, here])).astype(bf16)
    copies[1].wait()
    for at in range(width // TILE):
        for part in range(2):
            here = slice(part * width + at * TILE, part * width + (at + 1) * TILE)
            value = dot(middle[:, :width], both[0, :, here]) + dot(middle[:, width:], both[1, :, here])
            for sub in range(TILE // 128):
                wide[at * (TILE // 128) + sub, pl.ds(part, total, stride=2), :] = value[:, sub * 128 : (sub + 1) * 128]
    target = out.reshape(blocks, 2 * rows, width)
    writes = []
    for t in range(blocks):
        for at in range(width // 128):
            piece = wide[at, 2 * rows * t : 2 * rows * (t + 1), :]
            done[t, :, at * 128 : (at + 1) * 128] = piece.astype(bf16)
        writes.append(pltpu.make_async_copy(done.at[t], target.at[me ^ t], sems.at[len(copies) + t]))
        writes[-1].start()
    for copy in writes:
        copy.wait()


def last_product(chain, branch, stem, factor, shape):
    own, other = branch
    blocks, rows, width = layout(own)
    count = stem.shape[0]
    return chain(
        functools.partial(last_body, len(own)),
        shaped(shape),
        [ANY_SPEC] * (2 * len(own) + 2),
        (*own, *other, stem, factor),
        [
            pltpu.VMEM((2, blocks, rows, width), bf16),
            pltpu.VMEM((count, 2 * width), bf16),
            pltpu.VMEM((2, width, 2 * width), bf16),
            pltpu.VMEM((2, count, 2 * width), bf16),
            pltpu.VMEM((blocks * rows, 2 * width), bf16),
            pltpu.VMEM((width // 128, 2 * blocks * rows, 128), f32),
            pltpu.VMEM((blocks, 2 * rows, width), bf16),
            pltpu.SemaphoreType.DMA((2 + 2 * len(own) + blocks,)),
        ],
        [ANY_SPEC],
    )


def exchange(x):
    return lax.all_to_all(x, "outer", split_axis=0, concat_axis=0, tiled=True)


class Sum:
    def __init__(self, chain, left, right, branch, size, direct):
        self.chain, self.size, self.direct = chain, size, direct
        self.levels = size.bit_length() - 1
        self.keep, send = leaf_partial(chain, left, right, branch)
        self.recv = self.swap(send, 0)

    def swap(self, x, shift):
        return swap_with(x, 1 << shift, self.size)

    def steps(self):
        levels = self.levels
        direct = 1 << (levels - 2) if self.direct else 1
        stop = 2 if self.direct else levels
        for shift in range(1, stop):
            self.keep, send = halve(self.chain, self.keep, self.recv, shift)
            self.recv = self.swap(send, shift)
            yield
        masks = [reversed_bits(t, levels - 2) << 2 for t in range(1, direct)]
        if self.direct:
            self.keep, *sends = spread(self.chain, self.keep, self.recv, 2, direct)
            recvs = [swap_with(x, mask, self.size) for x, mask in zip(sends, masks, strict=True)]
            yield
        else:
            recvs = [self.recv]
        total = finish(self.chain, self.keep, recvs)
        if self.direct:
            recvs = [swap_with(total, mask, self.size) for mask in masks]
            yield
            total = join(self.chain, (total, *recvs))
        else:
            for shift in reversed(range(2, levels)):
                recv = self.swap(total, shift)
                yield
                total = join(self.chain, (total, recv))
        across = self.swap(total, 1)
        own = (total, across)
        other = (self.swap(total, 0), self.swap(across, 0))
        rows, width = total.shape[1:]
        if rows % 16:
            blocks = 1 << (levels - 1)
            order = block_of(self.chain.meta, blocks) ^ jnp.arange(blocks)
            own, other = (
                (jnp.concatenate(x, axis=0)[order].reshape(1, blocks * rows, width),) for x in (own, other)
            )
        self.result = own, other


def on_device(size, stem_tensor, leaf_left, leaf_right, slice_bits):
    width = stem_tensor.shape[1]
    place = lax.axis_index("outer").astype(jnp.int32)
    chain = Chain(jnp.concatenate([place[None], slice_bits.astype(jnp.int32)]))
    fine = width // size * 2 % 16 == 0
    given = exchange(stem_tensor[0])

    sums, runs = {}, {}

    def begin(j):
        sums[j] = Sum(chain, leaf_left, leaf_right, j, size, fine and j == 0)
        runs[j] = sums[j].steps()

    def step(*order):
        for j in order:
            next(runs[j], None)

    def end(j):
        for _ in runs[j]:
            pass
        return sums[j].result

    begin(0)
    begin(2)
    step(0)
    begin(1)
    step(2)
    begin(3)
    step(0)
    step(1, 3)
    step(0)
    step(2)
    right = prepare(chain, given)
    step(0)
    step(1, 2, 3, 1)
    end(0)
    state = first_product(chain, sums[0].result, right).reshape(width, 2 * width)
    state = exchange(state)
    step(2, 3, 1, 2, 3, 1, 2, 3, 1)
    end(1)
    end(3)
    end(2)
    factor = joined_right(chain, sums[1].result, sums[3].result).reshape(2, width, 2 * width)
    return last_product(chain, sums[2].result, state, factor, stem_tensor.shape)


def solution(mesh):
    return jax.shard_map(
        functools.partial(on_device, mesh.shape["outer"]),
        mesh=mesh,
        in_specs=(
            P(("cuts", "outer"), None, None, None),
            P(None, None, "outer", None, None),
            P(None, None, "outer", None, None),
            P("cuts"),
        ),
        out_specs=P(("cuts", "outer"), None, None, None),
        check_vma=False,
    )
```

time: 343 us -> 165 us (0.48)
  blocking collectives: 182 us -> 0 us
  local copies, waits for them, and re-layouts: 69.2 us -> 4.28 us
  starting transfers between devices: 10.9 us -> 73.3 us
  Pallas kernels: 0 us -> 39.1 us
  matrix products: 16.1 us -> 0 us
  other arithmetic: 8.63 us -> 0.73 us
  between operations: 7.62 us -> 0.55 us
    psum x1 -> x0, blocking collectives: 182 us -> none  [on_device(): lax.psum((leaf_term(leaves[0][0], leaves[0][1], width), leaf_term(leaves[...]
    ppermute x0 -> x38, starting transfers between devices: none -> 57.4 us  [swap_with(): return lax.ppermute(x, 'outer', [(i, i ^ mask) for i in range(size)])]
    all_to_all x2, waiting for transfers between devices: 47.1 us -> 0.01 us  [exchange(): return lax.all_to_all(x, 'outer', split_axis=0, concat_axis=0, tiled=True)]
    ppermute x0 -> x38, waiting for transfers between devices: none -> 44.1 us  [swap_with(): return lax.ppermute(x, 'outer', [(i, i ^ mask) for i in range(size)])]
    pallas_call x0 -> x30, Pallas kernels: none -> 39.1 us  [__call__(): pl.pallas_call(kernel, out_shape=shapes, in_specs=specs, out_specs=tuple(...]
    unnamed x21 -> x12, local copies, waits for them, and re-layouts: 25.6 us -> 4.28 us
    slice x3 -> x0, local copies, waits for them, and re-layouts: 19.2 us -> none  [the longest x1 8.94 us: on_device(): leaf_left[branch_index]]
    dot_general x12 -> x0, matrix products: 16.1 us -> none  [the longest x4 10.3 us: leaf_term(): lax.dot_general(left_leaf.reshape(depth, 2 * row_count), right_leaf.resha...]
  transfers between devices with their start and end apart: 2 -> 40, of which waited for: 2 -> 11; matrix products, arithmetic and copies ran while one was open for 1% -> 0% of each run, Pallas kernels for 0% -> 19%
where the time goes in v2:
time: 165 us; the launch traced here: 162 us
  starting transfers between devices  73.3 us (44%)
  waiting for transfers between devices  44.1 us (27%)
  Pallas kernels  39.1 us (24%)
  local copies, waits for them, and re-layouts  4.28 us (3%)
    ppermute x38, starting transfers between devices, swap_with(): return lax.ppermute(x, 'outer', [(i, i ^ mask) for i in range(size)])  57.4 us
    ppermute x38, waiting for transfers between devices, swap_with(): return lax.ppermute(x, 'outer', [(i, i ^ mask) for i in range(size)])  44.1 us
    pallas_call x30, Pallas kernels, __call__(): pl.pallas_call(kernel, out_shape=shapes, in_specs=specs, out_specs=tuple(...  39.1 us
    all_to_all x2, starting transfers between devices, exchange(): return lax.all_to_all(x, 'outer', split_axis=0, concat_axis=0, tiled=True)  15.9 us
    unnamed x12, local copies, waits for them, and re-layouts  4.28 us
  transfers between devices with their start and end apart: 40, of which 11 were waited for; matrix products, arithmetic and copies ran while one was open for 0% of the time, Pallas kernels for 19%

profile of v2, /device:TPU:11, one launch (start us, length us, event | category | flops | bytes accessed | tf_op | source)
XLA Modules:
  0.0 162.1 jit_solution(8162661735330404376)
XLA Ops:
  0.0 6.6 %all-to-all-start = ((bf16[512,2,512]{2,1,0:T(2,128)(2,1)}), bf16[512,2,512]{2,1,0:T(2,128)(2,1)S(1)}, u32[]{:S(2)}, u32[]{:S(2)}) async-start(bf16[512,2,512]{2,1,0:T(2,128)(2,1)} %bitcast.7), calls=%async_computation | async-start | bytes 2097152 | tf_op jit(solution)/shard_map/all_to_all | solution.py:363
  7.3 3.6 %shard_map.46 = (f32[512,512]{1,0:T(8,128)S(1)}, bf16[512,512]{1,0:T(8,128)(2,1)S(1)}) custom-call(s32[5]{0:T(128)S(1)} %pad_add_fusion.refs_0_, bf16[4,2,512,2,512]{4,3,2,1,0:T(2,128)(2,1)} %refs_1_.7, bf16[4,2,512,2,512]{4,3,2,1,0:T(2,128)(2,1)} %refs_2_.7), custom_call_target="tpu_custom_call" | custom-call | bytes 1024 | tf_op jit(solution)/shard_map/pallas_call | solution.py:34
  11.3 3.6 %shard_map.47 = (f32[512,512]{1,0:T(8,128)S(1)}, bf16[512,512]{1,0:T(8,128)(2,1)S(1)}) custom-call(s32[5]{0:T(128)S(1)} %pad_add_fusion.refs_0_, bf16[4,2,512,2,512]{4,3,2,1,0:T(2,128)(2,1)} %refs_1_.7, bf16[4,2,512,2,512]{4,3,2,1,0:T(2,128)(2,1)} %refs_2_.7, f32[512,512]{1,0:T(8,128)S(1)} %get-tuple-element.37.refs_3_.refs_1_), custom_call_target="tpu_custom_call" | custom-call | bytes 1024 | tf_op jit(solution)/shard_map/pallas_call | solution.py:34
  15.7 3.6 %shard_map.49 = (f32[512,512]{1,0:T(8,128)S(1)}, bf16[512,512]{1,0:T(8,128)(2,1)S(1)}) custom-call(s32[5]{0:T(128)S(1)} %pad_add_fusion.refs_0_, bf16[4,2,512,2,512]{4,3,2,1,0:T(2,128)(2,1)} %refs_1_.7, bf16[4,2,512,2,512]{4,3,2,1,0:T(2,128)(2,1)} %refs_2_.7, f32[256,512]{1,0:T(8,128)S(1)} %get-tuple-element.41.refs_3_.refs_1_), custom_call_target="tpu_custom_call" | custom-call | bytes 1024 | tf_op jit(solution)/shard_map/pallas_call | solution.py:34
  20.4 3.6 %shard_map.51 = (f32[512,512]{1,0:T(8,128)S(1)}, bf16[512,512]{1,0:T(8,128)(2,1)S(1)}) custom-call(s32[5]{0:T(128)S(1)} %pad_add_fusion.refs_0_, bf16[4,2,512,2,512]{4,3,2,1,0:T(2,128)(2,1)} %refs_1_.7, bf16[4,2,512,2,512]{4,3,2,1,0:T(2,128)(2,1)} %refs_2_.7, f32[256,512]{1,0:T(8,128)S(1)} %get-tuple-element.43.refs_3_.refs_1_), custom_call_target="tpu_custom_call" | custom-call | bytes 1024 | tf_op jit(solution)/shard_map/pallas_call | solution.py:34
  25.6 7.4 %collective-permute-done.3.refs_2_ = bf16[256,512]{1,0:T(8,128)(2,1)S(1)} collective-permute-done((bf16[256,512]{1,0:T(8,128)(2,1)S(1)}, bf16[256,512]{1,0:T(8,128)(2,1)S(1)}, u32[]{:S(2)}, u32[]{:S(2)}) %collective-permute-start.3) | collective-permute-done | bytes 262176 | tf_op jit(solution)/shard_map/ppermute | solution.py:184
  33.7 2.5 %collective-permute-start.4 = (bf16[64,512]{1,0:T(8,128)(2,1)S(1)}, bf16[64,512]{1,0:T(8,128)(2,1)S(1)}, u32[]{:S(2)}, u32[]{:S(2)}) collective-permute-start(bf16[64,512]{1,0:T(8,128)(2,1)S(1)} %get-tuple-element.48), channel_id=1, source_target_pairs={{0,8},{1,9},{2,10},{3,11},{4,12},{5,13},{6,14},{7,15},{8,0},{9,1},... | collective-permute-start | bytes 196616 | tf_op jit(solution)/shard_map/ppermute | solution.py:184
  40.5 3.6 %collective-permute-start.11 = (bf16[1,64,512]{2,1,0:T(8,128)(2,1)S(1)}, bf16[1,64,512]{2,1,0:T(8,128)(2,1)S(1)}, u32[]{:S(2)}, u32[]{:S(2)}) collective-permute-start(bf16[1,64,512]{2,1,0:T(8,128)(2,1)S(1)} %shard_map.55.refs_3_.refs_1_), channel_id=1, source_target_pairs={{0,8},{1,9},{2,10},{3,11},{4,12},{5,13},{6,14},{7,15},{8,0},{9,1},... | collective-permute-start | bytes 196616 | tf_op jit(solution)/shard_map/ppermute | solution.py:184
  45.5 2.7 %shard_map.57.refs_5_ = bf16[2,512,1024]{2,1,0:T(8,128)(2,1)S(1)} custom-call(s32[5]{0:T(128)S(1)} %pad_add_fusion.refs_0_, bf16[512,2,512]{2,1,0:T(2,128)(2,1)S(1)} %all-to-all-done.refs_1_, f32[128,512]{1,0:T(8,128)S(1)} %get-tuple-element.55.refs_2_.refs_1_), custom_call_target="tpu_custom_call" | custom-call | bytes 1024 | tf_op jit(solution)/shard_map/pallas_call | solution.py:34
  51.6 4.2 %collective-permute-start.16 = (bf16[4,64,512]{2,1,0:T(8,128)(2,1)S(1)}, bf16[4,64,512]{2,1,0:T(8,128)(2,1)S(1)}, u32[]{:S(2)}, u32[]{:S(2)}) collective-permute-start(bf16[4,64,512]{2,1,0:T(8,128)(2,1)S(1)} %shard_map.58.refs_3_.refs_1_), channel_id=1, source_target_pairs={{0,1},{1,0},{2,3},{3,2},{4,5},{5,4},{6,7},{7,6},{8,9},{9,8},{10,11... | collective-permute-start | bytes 786440 | tf_op jit(solution)/shard_map/ppermute | solution.py:184
  55.8 5.4 %collective-permute-start.17 = (bf16[4,64,512]{2,1,0:T(8,128)(2,1)S(1)}, bf16[4,64,512]{2,1,0:T(8,128)(2,1)S(1)}, u32[]{:S(2)}, u32[]{:S(2)}) collective-permute-start(bf16[4,64,512]{2,1,0:T(8,128)(2,1)S(1)} %collective-permute-done.15.refs_2_), channel_id=1, source_target_pairs={{0,1},{1,0},{2,3},{3,2},{4,5},{5,4},{6,7},{7,6},{8,9},{9,8},{10,11... | collective-permute-start | bytes 786440 | tf_op jit(solution)/shard_map/ppermute | solution.py:184
  61.3 2.8 %collective-permute-start.9 = (bf16[128,512]{1,0:T(8,128)(2,1)S(1)}, bf16[128,512]{1,0:T(8,128)(2,1)S(1)}, u32[]{:S(2)}, u32[]{:S(2)}) collective-permute-start(bf16[128,512]{1,0:T(8,128)(2,1)S(1)} %get-tuple-element.56), channel_id=1, source_target_pairs={{0,4},{1,5},{2,6},{3,7},{4,0},{5,1},{6,2},{7,3},{8,12},{9,13},{10,... | collective-permute-start | bytes 393224 | tf_op jit(solution)/shard_map/ppermute | solution.py:184
  64.8 3.2 %collective-permute-done.9.refs_2_ = bf16[128,512]{1,0:T(8,128)(2,1)S(1)} collective-permute-done((bf16[128,512]{1,0:T(8,128)(2,1)S(1)}, bf16[128,512]{1,0:T(8,128)(2,1)S(1)}, u32[]{:S(2)}, u32[]{:S(2)}) %collective-permute-start.9) | collective-permute-done | bytes 131104 | tf_op jit(solution)/shard_map/ppermute | solution.py:184
  69.9 2.8 %shard_map.63.refs_3_ = bf16[8,64,1024]{2,1,0:T(8,128)(2,1)} custom-call(s32[5]{0:T(128)S(1)} %pad_add_fusion.refs_0_, bf16[4,64,512]{2,1,0:T(8,128)(2,1)S(1)} %shard_map.58.refs_3_.refs_1_, bf16[4,64,512]{2,1,0:T(8,128)(2,1)S(1)} %collective-permute-done.15.refs_2_, bf16[4,64,512]{2,1,0:T(8,128)(2,1)S(1)} %collective-permute-done.16.refs_3_, ...), custom_call_target="tpu_custom_call" | custom-call | bytes 1024 | tf_op jit(solution)/shard_map/pallas_call | solution.py:34
  72.7 9.3 %all-to-all-start.1 = ((bf16[16,32,1024]{2,1,0:T(8,128)(2,1)}), bf16[16,32,1024]{2,1,0:T(8,128)(2,1)S(1)}, u32[]{:S(2)}, u32[]{:S(2)}) async-start(bf16[16,32,1024]{2,1,0:T(8,128)(2,1)} %bitcast.2), calls=%async_computation.1 | async-start | bytes 2097152 | tf_op jit(solution)/shard_map/all_to_all | solution.py:363
  84.6 24.4 %collective-permute-done.14.refs_2_ = bf16[64,512]{1,0:T(8,128)(2,1)S(1)} collective-permute-done((bf16[64,512]{1,0:T(8,128)(2,1)S(1)}, bf16[64,512]{1,0:T(8,128)(2,1)S(1)}, u32[]{:S(2)}, u32[]{:S(2)}) %collective-permute-start.14) | collective-permute-done | bytes 65568 | tf_op jit(solution)/shard_map/ppermute | solution.py:184
  109.5 3.2 %collective-permute-start.20 = (bf16[1,64,512]{2,1,0:T(8,128)(2,1)S(1)}, bf16[1,64,512]{2,1,0:T(8,128)(2,1)S(1)}, u32[]{:S(2)}, u32[]{:S(2)}) collective-permute-start(bf16[1,64,512]{2,1,0:T(8,128)(2,1)S(1)} %shard_map.64.refs_3_.refs_1_), channel_id=1, source_target_pairs={{0,8},{1,9},{2,10},{3,11},{4,12},{5,13},{6,14},{7,15},{8,0},{9,1},... | collective-permute-start | bytes 196616 | tf_op jit(solution)/shard_map/ppermute | solution.py:184
  114.9 3.1 %collective-permute-start.23 = (bf16[2,64,512]{2,1,0:T(8,128)(2,1)S(1)}, bf16[2,64,512]{2,1,0:T(8,128)(2,1)S(1)}, u32[]{:S(2)}, u32[]{:S(2)}) collective-permute-start(bf16[2,64,512]{2,1,0:T(8,128)(2,1)S(1)} %shard_map.67.refs_3_.refs_1_), channel_id=1, source_target_pairs={{0,4},{1,5},{2,6},{3,7},{4,0},{5,1},{6,2},{7,3},{8,12},{9,13},{10,... | collective-permute-start | bytes 393224 | tf_op jit(solution)/shard_map/ppermute | solution.py:184
  118.1 2.4 %collective-permute-start.24 = (bf16[1,64,512]{2,1,0:T(8,128)(2,1)S(1)}, bf16[1,64,512]{2,1,0:T(8,128)(2,1)S(1)}, u32[]{:S(2)}, u32[]{:S(2)}) collective-permute-start(bf16[1,64,512]{2,1,0:T(8,128)(2,1)S(1)} %shard_map.66.refs_3_.refs_1_), channel_id=1, source_target_pairs={{0,8},{1,9},{2,10},{3,11},{4,12},{5,13},{6,14},{7,15},{8,0},{9,1},... | collective-permute-start | bytes 196616 | tf_op jit(solution)/shard_map/ppermute | solution.py:184
  135.0 4.6 %collective-permute-start.32 = (bf16[4,64,512]{2,1,0:T(8,128)(2,1)S(1)}, bf16[4,64,512]{2,1,0:T(8,128)(2,1)S(1)}, u32[]{:S(2)}, u32[]{:S(2)}) collective-permute-start(bf16[4,64,512]{2,1,0:T(8,128)(2,1)S(1)} %shard_map.72.refs_3_.refs_1_), channel_id=1, source_target_pairs={{0,1},{1,0},{2,3},{3,2},{4,5},{5,4},{6,7},{7,6},{8,9},{9,8},{10,11... | collective-permute-start | bytes 786440 | tf_op jit(solution)/shard_map/ppermute | solution.py:184
  140.1 2.4 %collective-permute-start.33 = (bf16[4,64,512]{2,1,0:T(8,128)(2,1)S(1)}, bf16[4,64,512]{2,1,0:T(8,128)(2,1)S(1)}, u32[]{:S(2)}, u32[]{:S(2)}) collective-permute-start(bf16[4,64,512]{2,1,0:T(8,128)(2,1)S(1)} %collective-permute-done.31.refs_2_), channel_id=1, source_target_pairs={{0,1},{1,0},{2,3},{3,2},{4,5},{5,4},{6,7},{7,6},{8,9},{9,8},{10,11... | collective-permute-start | bytes 786440 | tf_op jit(solution)/shard_map/ppermute | solution.py:184
  142.5 5.4 %collective-permute-start.37 = (bf16[4,64,512]{2,1,0:T(8,128)(2,1)S(1)}, bf16[4,64,512]{2,1,0:T(8,128)(2,1)S(1)}, u32[]{:S(2)}, u32[]{:S(2)}) collective-permute-start(bf16[4,64,512]{2,1,0:T(8,128)(2,1)S(1)} %collective-permute-done.35.refs_6_), channel_id=1, source_target_pairs={{0,1},{1,0},{2,3},{3,2},{4,5},{5,4},{6,7},{7,6},{8,9},{9,8},{10,11... | collective-permute-start | bytes 786440 | tf_op jit(solution)/shard_map/ppermute | solution.py:184
  148.0 3.0 %collective-permute-start.28 = (bf16[4,64,512]{2,1,0:T(8,128)(2,1)S(1)}, bf16[4,64,512]{2,1,0:T(8,128)(2,1)S(1)}, u32[]{:S(2)}, u32[]{:S(2)}) collective-permute-start(bf16[4,64,512]{2,1,0:T(8,128)(2,1)S(1)} %collective-permute-done.26.refs_2_), channel_id=1, source_target_pairs={{0,1},{1,0},{2,3},{3,2},{4,5},{5,4},{6,7},{7,6},{8,9},{9,8},{10,11... | collective-permute-start | bytes 786440 | tf_op jit(solution)/shard_map/ppermute | solution.py:184
  157.3 4.6 %shard_map.75 = bf16[1,512,2,512]{3,2,1,0:T(2,128)(2,1)} custom-call(s32[5]{0:T(128)S(1)} %pad_add_fusion.refs_0_, bf16[4,64,512]{2,1,0:T(8,128)(2,1)S(1)} %shard_map.70.refs_3_.refs_1_, bf16[4,64,512]{2,1,0:T(8,128)(2,1)S(1)} %copy-done.1, bf16[4,64,512]{2,1,0:T(8,128)(2,1)S(1)} %copy-done.3, bf16[4,64,512]{2,1,0:T(8,128)(2,1)S(1)} %copy-done.5, ...), custom_call_target="tpu_custom_call" | custom-call | bytes 1024 | tf_op jit(solution)/shard_map/pallas_call | solution.py:34
  (99 shorter events, 43.6 us)
Async XLA Ops:
  0.0 45.5 %all-to-all-start = ((bf16[512,2,512]{2,1,0:T(2,128)(2,1)}), bf16[512,2,512]{2,1,0:T(2,128)(2,1)S(1)}, u32[]{:S(2)}, u32[]{:S(2)}) async-start(bf16[512,2,512]{2,1,0:T(2,128)(2,1)} %bitcast.7), calls=%async_computation | async-start | bytes 2097152 | tf_op jit(solution)/shard_map/all_to_all | solution.py:363
  19.3 16.8 %collective-permute-start.8 = (bf16[512,512]{1,0:T(8,128)(2,1)S(1)}, bf16[512,512]{1,0:T(8,128)(2,1)S(1)}, u32[]{:S(2)}, u32[]{:S(2)}) collective-permute-start(bf16[512,512]{1,0:T(8,128)(2,1)S(1)} %get-tuple-element.52), channel_id=1, source_target_pairs={{0,1},{1,0},{2,3},{3,2},{4,5},{5,4},{6,7},{7,6},{8,9},{9,8},{10,11... | collective-permute-start | bytes 1572872 | tf_op jit(solution)/shard_map/ppermute | solution.py:184
  24.0 13.4 %collective-permute-start.7 = (bf16[512,512]{1,0:T(8,128)(2,1)S(1)}, bf16[512,512]{1,0:T(8,128)(2,1)S(1)}, u32[]{:S(2)}, u32[]{:S(2)}) collective-permute-start(bf16[512,512]{1,0:T(8,128)(2,1)S(1)} %get-tuple-element.51), channel_id=1, source_target_pairs={{0,1},{1,0},{2,3},{3,2},{4,5},{5,4},{6,7},{7,6},{8,9},{9,8},{10,11... | collective-permute-start | bytes 1572872 | tf_op jit(solution)/shard_map/ppermute | solution.py:184
  24.2 8.9 %collective-permute-start.3 = (bf16[256,512]{1,0:T(8,128)(2,1)S(1)}, bf16[256,512]{1,0:T(8,128)(2,1)S(1)}, u32[]{:S(2)}, u32[]{:S(2)}) collective-permute-start(bf16[256,512]{1,0:T(8,128)(2,1)S(1)} %get-tuple-element.45), channel_id=1, source_target_pairs={{0,2},{1,3},{2,0},{3,1},{4,6},{5,7},{6,4},{7,5},{8,10},{9,11},{10,... | collective-permute-start | bytes 786440 | tf_op jit(solution)/shard_map/ppermute | solution.py:184
  25.3 19.6 %collective-permute-start.2 = (bf16[256,512]{1,0:T(8,128)(2,1)S(1)}, bf16[256,512]{1,0:T(8,128)(2,1)S(1)}, u32[]{:S(2)}, u32[]{:S(2)}) collective-permute-start(bf16[256,512]{1,0:T(8,128)(2,1)S(1)} %get-tuple-element.44), channel_id=1, source_target_pairs={{0,2},{1,3},{2,0},{3,1},{4,6},{5,7},{6,4},{7,5},{8,10},{9,11},{10,... | collective-permute-start | bytes 786440 | tf_op jit(solution)/shard_map/ppermute | solution.py:184
  40.5 7.8 %collective-permute-start.11 = (bf16[1,64,512]{2,1,0:T(8,128)(2,1)S(1)}, bf16[1,64,512]{2,1,0:T(8,128)(2,1)S(1)}, u32[]{:S(2)}, u32[]{:S(2)}) collective-permute-start(bf16[1,64,512]{2,1,0:T(8,128)(2,1)S(1)} %shard_map.55.refs_3_.refs_1_), channel_id=1, source_target_pairs={{0,8},{1,9},{2,10},{3,11},{4,12},{5,13},{6,14},{7,15},{8,0},{9,1},... | collective-permute-start | bytes 196616 | tf_op jit(solution)/shard_map/ppermute | solution.py:184
  48.9 7.0 %collective-permute-start.15 = (bf16[4,64,512]{2,1,0:T(8,128)(2,1)S(1)}, bf16[4,64,512]{2,1,0:T(8,128)(2,1)S(1)}, u32[]{:S(2)}, u32[]{:S(2)}) collective-permute-start(bf16[4,64,512]{2,1,0:T(8,128)(2,1)S(1)} %shard_map.58.refs_3_.refs_1_), channel_id=1, source_target_pairs={{0,2},{1,3},{2,0},{3,1},{4,6},{5,7},{6,4},{7,5},{8,10},{9,11},{10,... | collective-permute-start | bytes 786440 | tf_op jit(solution)/shard_map/ppermute | solution.py:184
  50.1 14.0 %collective-permute-start.10 = (bf16[256,512]{1,0:T(8,128)(2,1)S(1)}, bf16[256,512]{1,0:T(8,128)(2,1)S(1)}, u32[]{:S(2)}, u32[]{:S(2)}) collective-permute-start(bf16[256,512]{1,0:T(8,128)(2,1)S(1)} %get-tuple-element.57), channel_id=1, source_target_pairs={{0,2},{1,3},{2,0},{3,1},{4,6},{5,7},{6,4},{7,5},{8,10},{9,11},{10,... | collective-permute-start | bytes 786440 | tf_op jit(solution)/shard_map/ppermute | solution.py:184
  50.4 18.2 %collective-permute-start.19 = (bf16[256,512]{1,0:T(8,128)(2,1)S(1)}, bf16[256,512]{1,0:T(8,128)(2,1)S(1)}, u32[]{:S(2)}, u32[]{:S(2)}) collective-permute-start(bf16[256,512]{1,0:T(8,128)(2,1)S(1)} %get-tuple-element.62), channel_id=1, source_target_pairs={{0,2},{1,3},{2,0},{3,1},{4,6},{5,7},{6,4},{7,5},{8,10},{9,11},{10,... | collective-permute-start | bytes 786440 | tf_op jit(solution)/shard_map/ppermute | solution.py:184
  51.6 18.3 %collective-permute-start.16 = (bf16[4,64,512]{2,1,0:T(8,128)(2,1)S(1)}, bf16[4,64,512]{2,1,0:T(8,128)(2,1)S(1)}, u32[]{:S(2)}, u32[]{:S(2)}) collective-permute-start(bf16[4,64,512]{2,1,0:T(8,128)(2,1)S(1)} %shard_map.58.refs_3_.refs_1_), channel_id=1, source_target_pairs={{0,1},{1,0},{2,3},{3,2},{4,5},{5,4},{6,7},{7,6},{8,9},{9,8},{10,11... | collective-permute-start | bytes 786440 | tf_op jit(solution)/shard_map/ppermute | solution.py:184
  55.8 14.0 %collective-permute-start.17 = (bf16[4,64,512]{2,1,0:T(8,128)(2,1)S(1)}, bf16[4,64,512]{2,1,0:T(8,128)(2,1)S(1)}, u32[]{:S(2)}, u32[]{:S(2)}) collective-permute-start(bf16[4,64,512]{2,1,0:T(8,128)(2,1)S(1)} %collective-permute-done.15.refs_2_), channel_id=1, source_target_pairs={{0,1},{1,0},{2,3},{3,2},{4,5},{5,4},{6,7},{7,6},{8,9},{9,8},{10,11... | collective-permute-start | bytes 786440 | tf_op jit(solution)/shard_map/ppermute | solution.py:184
  61.3 6.7 %collective-permute-start.9 = (bf16[128,512]{1,0:T(8,128)(2,1)S(1)}, bf16[128,512]{1,0:T(8,128)(2,1)S(1)}, u32[]{:S(2)}, u32[]{:S(2)}) collective-permute-start(bf16[128,512]{1,0:T(8,128)(2,1)S(1)} %get-tuple-element.56), channel_id=1, source_target_pairs={{0,4},{1,5},{2,6},{3,7},{4,0},{5,1},{6,2},{7,3},{8,12},{9,13},{10,... | collective-permute-start | bytes 393224 | tf_op jit(solution)/shard_map/ppermute | solution.py:184
  72.7 81.8 %all-to-all-start.1 = ((bf16[16,32,1024]{2,1,0:T(8,128)(2,1)}), bf16[16,32,1024]{2,1,0:T(8,128)(2,1)S(1)}, u32[]{:S(2)}, u32[]{:S(2)}) async-start(bf16[16,32,1024]{2,1,0:T(8,128)(2,1)} %bitcast.2), calls=%async_computation.1 | async-start | bytes 2097152 | tf_op jit(solution)/shard_map/all_to_all | solution.py:363
  82.0 30.7 %collective-permute-start.22 = (bf16[128,512]{1,0:T(8,128)(2,1)S(1)}, bf16[128,512]{1,0:T(8,128)(2,1)S(1)}, u32[]{:S(2)}, u32[]{:S(2)}) collective-permute-start(bf16[128,512]{1,0:T(8,128)(2,1)S(1)} %get-tuple-element.66), channel_id=1, source_target_pairs={{0,4},{1,5},{2,6},{3,7},{4,0},{5,1},{6,2},{7,3},{8,12},{9,13},{10,... | collective-permute-start | bytes 393224 | tf_op jit(solution)/shard_map/ppermute | solution.py:184
  82.2 26.8 %collective-permute-start.14 = (bf16[64,512]{1,0:T(8,128)(2,1)S(1)}, bf16[64,512]{1,0:T(8,128)(2,1)S(1)}, u32[]{:S(2)}, u32[]{:S(2)}) collective-permute-start(bf16[64,512]{1,0:T(8,128)(2,1)S(1)} %get-tuple-element.60), channel_id=1, source_target_pairs={{0,8},{1,9},{2,10},{3,11},{4,12},{5,13},{6,14},{7,15},{8,0},{9,1},... | collective-permute-start | bytes 196616 | tf_op jit(solution)/shard_map/ppermute | solution.py:184
  84.4 28.8 %collective-permute-start.21 = (bf16[64,512]{1,0:T(8,128)(2,1)S(1)}, bf16[64,512]{1,0:T(8,128)(2,1)S(1)}, u32[]{:S(2)}, u32[]{:S(2)}) collective-permute-start(bf16[64,512]{1,0:T(8,128)(2,1)S(1)} %get-tuple-element.65), channel_id=1, source_target_pairs={{0,8},{1,9},{2,10},{3,11},{4,12},{5,13},{6,14},{7,15},{8,0},{9,1},... | collective-permute-start | bytes 196616 | tf_op jit(solution)/shard_map/ppermute | solution.py:184
  114.9 10.2 %collective-permute-start.23 = (bf16[2,64,512]{2,1,0:T(8,128)(2,1)S(1)}, bf16[2,64,512]{2,1,0:T(8,128)(2,1)S(1)}, u32[]{:S(2)}, u32[]{:S(2)}) collective-permute-start(bf16[2,64,512]{2,1,0:T(8,128)(2,1)S(1)} %shard_map.67.refs_3_.refs_1_), channel_id=1, source_target_pairs={{0,4},{1,5},{2,6},{3,7},{4,0},{5,1},{6,2},{7,3},{8,12},{9,13},{10,... | collective-permute-start | bytes 393224 | tf_op jit(solution)/shard_map/ppermute | solution.py:184
  130.3 9.9 %collective-permute-start.31 = (bf16[4,64,512]{2,1,0:T(8,128)(2,1)S(1)}, bf16[4,64,512]{2,1,0:T(8,128)(2,1)S(1)}, u32[]{:S(2)}, u32[]{:S(2)}) collective-permute-start(bf16[4,64,512]{2,1,0:T(8,128)(2,1)S(1)} %shard_map.72.refs_3_.refs_1_), channel_id=1, source_target_pairs={{0,2},{1,3},{2,0},{3,1},{4,6},{5,7},{6,4},{7,5},{8,10},{9,11},{10,... | collective-permute-start | bytes 786440 | tf_op jit(solution)/shard_map/ppermute | solution.py:184
  133.8 8.8 %collective-permute-start.35 = (bf16[4,64,512]{2,1,0:T(8,128)(2,1)S(1)}, bf16[4,64,512]{2,1,0:T(8,128)(2,1)S(1)}, u32[]{:S(2)}, u32[]{:S(2)}) collective-permute-start(bf16[4,64,512]{2,1,0:T(8,128)(2,1)S(1)} %shard_map.73.refs_5_.refs_9_), channel_id=1, source_target_pairs={{0,2},{1,3},{2,0},{3,1},{4,6},{5,7},{6,4},{7,5},{8,10},{9,11},{10,... | collective-permute-start | bytes 786440 | tf_op jit(solution)/shard_map/ppermute | solution.py:184
  135.0 12.9 %collective-permute-start.32 = (bf16[4,64,512]{2,1,0:T(8,128)(2,1)S(1)}, bf16[4,64,512]{2,1,0:T(8,128)(2,1)S(1)}, u32[]{:S(2)}, u32[]{:S(2)}) collective-permute-start(bf16[4,64,512]{2,1,0:T(8,128)(2,1)S(1)} %shard_map.72.refs_3_.refs_1_), channel_id=1, source_target_pairs={{0,1},{1,0},{2,3},{3,2},{4,5},{5,4},{6,7},{7,6},{8,9},{9,8},{10,11... | collective-permute-start | bytes 786440 | tf_op jit(solution)/shard_map/ppermute | solution.py:184
  139.6 8.4 %collective-permute-start.26 = (bf16[4,64,512]{2,1,0:T(8,128)(2,1)S(1)}, bf16[4,64,512]{2,1,0:T(8,128)(2,1)S(1)}, u32[]{:S(2)}, u32[]{:S(2)}) collective-permute-start(bf16[4,64,512]{2,1,0:T(8,128)(2,1)S(1)} %shard_map.70.refs_3_.refs_1_), channel_id=1, source_target_pairs={{0,2},{1,3},{2,0},{3,1},{4,6},{5,7},{6,4},{7,5},{8,10},{9,11},{10,... | collective-permute-start | bytes 786440 | tf_op jit(solution)/shard_map/ppermute | solution.py:184
  139.8 11.1 %collective-permute-start.36 = (bf16[4,64,512]{2,1,0:T(8,128)(2,1)S(1)}, bf16[4,64,512]{2,1,0:T(8,128)(2,1)S(1)}, u32[]{:S(2)}, u32[]{:S(2)}) collective-permute-start(bf16[4,64,512]{2,1,0:T(8,128)(2,1)S(1)} %shard_map.73.refs_5_.refs_9_), channel_id=1, source_target_pairs={{0,1},{1,0},{2,3},{3,2},{4,5},{5,4},{6,7},{7,6},{8,9},{9,8},{10,11... | collective-permute-start | bytes 786440 | tf_op jit(solution)/shard_map/ppermute | solution.py:184
  140.1 10.8 %collective-permute-start.33 = (bf16[4,64,512]{2,1,0:T(8,128)(2,1)S(1)}, bf16[4,64,512]{2,1,0:T(8,128)(2,1)S(1)}, u32[]{:S(2)}, u32[]{:S(2)}) collective-permute-start(bf16[4,64,512]{2,1,0:T(8,128)(2,1)S(1)} %collective-permute-done.31.refs_2_), channel_id=1, source_target_pairs={{0,1},{1,0},{2,3},{3,2},{4,5},{5,4},{6,7},{7,6},{8,9},{9,8},{10,11... | collective-permute-start | bytes 786440 | tf_op jit(solution)/shard_map/ppermute | solution.py:184
  142.5 8.4 %collective-permute-start.37 = (bf16[4,64,512]{2,1,0:T(8,128)(2,1)S(1)}, bf16[4,64,512]{2,1,0:T(8,128)(2,1)S(1)}, u32[]{:S(2)}, u32[]{:S(2)}) collective-permute-start(bf16[4,64,512]{2,1,0:T(8,128)(2,1)S(1)} %collective-permute-done.35.refs_6_), channel_id=1, source_target_pairs={{0,1},{1,0},{2,3},{3,2},{4,5},{5,4},{6,7},{7,6},{8,9},{9,8},{10,11... | collective-permute-start | bytes 786440 | tf_op jit(solution)/shard_map/ppermute | solution.py:184
  (22 other events, 83.6 us)

commit v3 on v2

--- a/solution.py
+++ b/solution.py
@@ -7,7 +7,7 @@
 from jax.experimental.pallas import tpu as pltpu
 from jax.sharding import PartitionSpec as P
 
-VMEM_LIMIT = 48 << 20
+VMEM_LIMIT = 24 << 20
 TILE = 256
 bf16, f32 = jnp.bfloat16, jnp.float32
 
@@ -20,7 +20,7 @@
     def __init__(self, meta):
         self.meta, self.last = meta, None
 
-    def __call__(self, body, shapes, in_specs, operands, scratch=(), out_specs=None):
+    def __call__(self, body, shapes, in_specs, operands, scratch=(), out_specs=None, us=1.0):
         many = isinstance(shapes, (tuple, list))
         shapes = tuple(shapes) if many else (shapes,)
         specs, extra = [SMEM_SPEC] + list(in_specs), []
@@ -38,7 +38,7 @@
             out_specs=tuple(out_specs or [VMEM_SPEC] * len(shapes)),
             scratch_shapes=list(scratch),
             compiler_params=pltpu.CompilerParams(vmem_limit_bytes=VMEM_LIMIT),
-            cost_estimate=pl.CostEstimate(flops=0, bytes_accessed=1024, transcendentals=0),
+            cost_estimate=pl.CostEstimate(flops=int(us * 1e9), bytes_accessed=1024, transcendentals=0),
         )(self.meta, *operands, *extra)
         self.last = out[0]
         return out if many else out[0]
@@ -102,40 +102,45 @@
             pltpu.VMEM((2, 2 * depth, width), bf16),
             pltpu.SemaphoreType.DMA((2,)),
         ],
-    )
-
-
-def half_body(shift, meta, keep, recv, keep_out, send_out):
-    half = keep_out.shape[0]
+        us=3.5,
+    )
+
+
+def half_body(count, shift, meta, *refs):
+    keeps, recvs, (keep_out, send_out) = refs[:count], refs[count : 2 * count], refs[2 * count :]
+    half = keep_out.shape[1]
     bit = (meta[0] >> shift) & 1
-    mine = pl.multiple_of(bit * half, half)
-    other = pl.multiple_of((1 - bit) * half, half)
-    send_out[...] = (keep[pl.ds(other, half)] + recv[pl.ds(other, half)].astype(f32)).astype(bf16)
-    keep_out[...] = keep[pl.ds(mine, half)] + recv[pl.ds(mine, half)].astype(f32)
-
-
-def halve(chain, keep, recv, shift):
-    rows, width = keep.shape
+    mine = pl.ds(pl.multiple_of(bit * half, half), half)
+    other = pl.ds(pl.multiple_of((1 - bit) * half, half), half)
+    for at, (keep, recv) in enumerate(zip(keeps, recvs, strict=True)):
+        send_out[at] = (keep[other] + recv[other].astype(f32)).astype(bf16)
+        keep_out[at] = keep[mine] + recv[mine].astype(f32)
+
+
+def halve(chain, keeps, recvs, shift):
+    count, (rows, width) = len(keeps), keeps[0].shape
     half = rows // 2
     if half % 16:
-        total = (keep + recv.astype(f32)).reshape(2, half, width)
+        total = jnp.stack([keep + recv.astype(f32) for keep, recv in zip(keeps, recvs, strict=True)])
+        total = total.reshape(count, 2, half, width)
         bit = (chain.meta[0] >> shift) & 1
-        return total[bit], total[1 - bit].astype(bf16)
-    return chain(
-        functools.partial(half_body, shift),
-        (shaped((half, width), f32), shaped((half, width))),
-        [VMEM_SPEC] * 2,
-        (keep, recv),
+        return total[:, bit], total[:, 1 - bit].astype(bf16)
+    return chain(
+        functools.partial(half_body, count, shift),
+        (shaped((count, half, width), f32), shaped((count, half, width))),
+        [VMEM_SPEC] * (2 * count),
+        (*keeps, *recvs),
+        us=0.6 * count,
     )
 
 
 def spread_body(shift, meta, keep, recv, keep_out, *sends):
-    rows = keep_out.shape[0]
+    rows = keep_out.shape[1]
     blocks = len(sends) + 1
     me = reversed_bits(meta[0] >> shift, blocks.bit_length() - 1)
     for t in range(blocks):
         at = pl.ds(pl.multiple_of((me ^ t) * rows, rows), rows)
-        value = keep[at] + recv[at].astype(f32)
+        value = keep[:, at] + recv[:, at].astype(f32)
         if t:
             sends[t - 1][...] = value.astype(bf16)
         else:
@@ -143,12 +148,13 @@
 
 
 def spread(chain, keep, recv, shift, blocks):
-    rows, width = keep.shape[0] // blocks, keep.shape[1]
+    count, rows, width = keep.shape[0], keep.shape[1] // blocks, keep.shape[2]
     return chain(
         functools.partial(spread_body, shift),
-        (shaped((rows, width), f32),) + (shaped((rows, width)),) * (blocks - 1),
+        (shaped((count, rows, width), f32),) + (shaped((count, rows, width)),) * (blocks - 1),
         [VMEM_SPEC] * 2,
         (keep, recv),
+        us=0.6 * count,
     )
 
 
@@ -160,10 +166,9 @@
 
 
 def finish(chain, keep, recvs):
-    rows, width = keep.shape
-    if rows % 16:
+    if keep.shape[1] % 16:
         return (keep + sum(recv.astype(f32) for recv in recvs)).astype(bf16)[None]
-    return chain(finish_body, shaped((1, rows, width)), [VMEM_SPEC] * (1 + len(recvs)), (keep, *recvs))
+    return chain(finish_body, shaped((1, *keep.shape)), [VMEM_SPEC] * (1 + len(recvs)), (keep, *recvs), us=0.6)
 
 
 def join_body(meta, *refs):
@@ -174,10 +179,10 @@
 
 
 def join(chain, parts):
-    blocks, rows, width = sum(part.shape[0] for part in parts), *parts[0].shape[1:]
-    if rows % 16:
+    blocks, shape = sum(part.shape[0] for part in parts), parts[0].shape[1:]
+    if shape[1] % 16:
         return jnp.concatenate(parts, axis=0)
-    return chain(join_body, shaped((blocks, rows, width)), [VMEM_SPEC] * len(parts), parts)
+    return chain(join_body, shaped((blocks, *shape)), [VMEM_SPEC] * len(parts), parts, us=0.6)
 
 
 def swap_with(x, mask, size):
@@ -212,19 +217,23 @@
     )
 
 
-def rows_of(refs, width):
-    return jnp.concatenate([ref[...].reshape(-1, width) for ref in refs], axis=0)
-
-
-def layout(planes):
-    return sum(part.shape[0] for part in planes), *planes[0].shape[1:]
-
-
-def first_body(parts, meta, *refs):
+class Summed:
+    def __init__(self, own, other, at):
+        self.own, self.other, self.at = own, other, at
+        self.parts = len(own)
+        self.blocks, (self.rows, self.width) = sum(part.shape[0] for part in own), own[0].shape[2:]
+        self.operands = (*own, *other)
+
+
+def rows_of(refs, at):
+    return jnp.concatenate([ref[:, at].reshape(-1, ref.shape[3]) for ref in refs], axis=0)
+
+
+def first_body(parts, at_branch, meta, *refs):
     own, other, (right, out) = refs[:parts], refs[parts : 2 * parts], refs[2 * parts :]
     blocks, rows, columns = out.shape
     me = block_of(meta, blocks)
-    mine, theirs = rows_of(own, columns // 2), rows_of(other, columns // 2)
+    mine, theirs = rows_of(own, at_branch), rows_of(other, at_branch)
     for at in range(columns // TILE):
         here = slice(at * TILE, (at + 1) * TILE)
         value = dot(mine, right[0, :, here]) + dot(theirs, right[1, :, here])
@@ -234,17 +243,16 @@
 
 
 def first_product(chain, branch, right):
-    own, other = branch
-    blocks, rows, width = layout(own)
-    return chain(
-        functools.partial(first_body, len(own)),
-        shaped((blocks, rows, 2 * width)),
-        [VMEM_SPEC] * (2 * len(own) + 1),
-        (*own, *other, right),
-    )
-
-
-def joined_body(parts, meta, *refs):
+    return chain(
+        functools.partial(first_body, branch.parts, branch.at),
+        shaped((branch.blocks, branch.rows, 2 * branch.width)),
+        [VMEM_SPEC] * (2 * branch.parts + 1),
+        (*branch.operands, right),
+        us=2.8,
+    )
+
+
+def joined_body(parts, at0, at1, meta, *refs):
     own0, other0, own1, other1 = (refs[at * parts : (at + 1) * parts] for at in range(4))
     out, right = refs[4 * parts :]
     _, blocks, rows, columns = out.shape
@@ -254,7 +262,7 @@
     t = 0
     for own_ref, other_ref in zip(own1, other1, strict=True):
         for at in range(own_ref.shape[0]):
-            own, other = own_ref[at], other_ref[at]
+            own, other = own_ref[at, at1], other_ref[at, at1]
             real = jnp.where(core == 0, own, other)
             imag = jnp.where(core == 0, other, own)
             right[core, me ^ t, :, :width] = real
@@ -262,7 +270,7 @@
             right[1 - core, me ^ t, :, :width] = -imag
             right[1 - core, me ^ t, :, width:] = real
             t += 1
-    mine, theirs = rows_of(own0, width), rows_of(other0, width)
+    mine, theirs = rows_of(own0, at0), rows_of(other0, at0)
     for at in range(columns // TILE):
         here = slice(at * TILE, (at + 1) * TILE)
         there = slice((at * TILE + width) % columns, (at * TILE + width) % columns + TILE)
@@ -278,18 +286,18 @@
 
 
 def joined_right(chain, first, second):
-    blocks, rows, width = layout(first[0])
-    parts = len(first[0])
-    return chain(
-        functools.partial(joined_body, parts),
+    blocks, rows, width = first.blocks, first.rows, first.width
+    return chain(
+        functools.partial(joined_body, first.parts, first.at, second.at),
         shaped((2, blocks, rows, 2 * width)),
-        [VMEM_SPEC] * (4 * parts),
-        (*first[0], *first[1], *second[0], *second[1]),
+        [VMEM_SPEC] * (4 * first.parts),
+        (*first.operands, *second.operands),
         [pltpu.VMEM((2, blocks, rows, 2 * width), bf16)],
-    )
-
-
-def last_body(parts, meta, *refs):
+        us=2.0,
+    )
+
+
+def last_body(parts, at_branch, meta, *refs):
     own, other = refs[:parts], refs[parts : 2 * parts]
     stem, factor, out, left, given, both, right, middle, wide, done, sems = refs[2 * parts :]
     _, blocks, rows, width = left.shape
@@ -301,7 +309,11 @@
         at = 0
         for ref in refs_of:
             size = ref.shape[0]
-            copies.append(pltpu.make_async_copy(ref, left.at[plane, pl.ds(at, size)], sems.at[len(copies)]))
+            copies.append(
+                pltpu.make_async_copy(
+                    ref.at[:, at_branch], left.at[plane, pl.ds(at, size)], sems.at[len(copies)]
+                )
+            )
             at += size
     for copy in copies:
         copy.start()
@@ -337,14 +349,13 @@
 
 
 def last_product(chain, branch, stem, factor, shape):
-    own, other = branch
-    blocks, rows, width = layout(own)
+    blocks, rows, width = branch.blocks, branch.rows, branch.width
     count = stem.shape[0]
     return chain(
-        functools.partial(last_body, len(own)),
+        functools.partial(last_body, branch.parts, branch.at),
         shaped(shape),
-        [ANY_SPEC] * (2 * len(own) + 2),
-        (*own, *other, stem, factor),
+        [ANY_SPEC] * (2 * branch.parts + 2),
+        (*branch.operands, stem, factor),
         [
             pltpu.VMEM((2, blocks, rows, width), bf16),
             pltpu.VMEM((count, 2 * width), bf16),
@@ -353,9 +364,10 @@
             pltpu.VMEM((blocks * rows, 2 * width), bf16),
             pltpu.VMEM((width // 128, 2 * blocks * rows, 128), f32),
             pltpu.VMEM((blocks, 2 * rows, width), bf16),
-            pltpu.SemaphoreType.DMA((2 + 2 * len(own) + blocks,)),
+            pltpu.SemaphoreType.DMA((2 + 2 * branch.parts + blocks,)),
         ],
         [ANY_SPEC],
+        us=5.0,
     )
 
 
@@ -364,97 +376,81 @@
 
 
 class Sum:
-    def __init__(self, chain, left, right, branch, size, direct):
-        self.chain, self.size, self.direct = chain, size, direct
+    def __init__(self, chain, size):
+        self.chain, self.size = chain, size
         self.levels = size.bit_length() - 1
-        self.keep, send = leaf_partial(chain, left, right, branch)
-        self.recv = self.swap(send, 0)
+        self.keeps, self.recvs = [], []
+
+    def add(self, left, right, branch):
+        keep, send = leaf_partial(self.chain, left, right, branch)
+        self.keeps.append(keep)
+        self.recvs.append(self.swap(send, 0))
 
     def swap(self, x, shift):
         return swap_with(x, 1 << shift, self.size)
 
     def steps(self):
-        levels = self.levels
-        direct = 1 << (levels - 2) if self.direct else 1
-        stop = 2 if self.direct else levels
-        for shift in range(1, stop):
-            self.keep, send = halve(self.chain, self.keep, self.recv, shift)
-            self.recv = self.swap(send, shift)
-            yield
-        masks = [reversed_bits(t, levels - 2) << 2 for t in range(1, direct)]
-        if self.direct:
-            self.keep, *sends = spread(self.chain, self.keep, self.recv, 2, direct)
+        levels, chain = self.levels, self.chain
+        blocks = 1 << (levels - 2)
+        rows = self.keeps[0].shape[0] // (2 * blocks)
+        keep, send = halve(chain, self.keeps, self.recvs, 1)
+        recv = self.swap(send, 1)
+        yield
+        if rows % 16:
+            for shift in range(2, levels):
+                keep, send = halve(chain, list(keep), list(recv), shift)
+                recv = self.swap(send, shift)
+            total = finish(chain, keep, [recv])
+            for shift in reversed(range(2, levels)):
+                total = join(chain, (total, self.swap(total, shift)))
+        else:
+            masks = [reversed_bits(t, levels - 2) << 2 for t in range(1, blocks)]
+            keep, *sends = spread(chain, keep, recv, 2, blocks)
             recvs = [swap_with(x, mask, self.size) for x, mask in zip(sends, masks, strict=True)]
             yield
-        else:
-            recvs = [self.recv]
-        total = finish(self.chain, self.keep, recvs)
-        if self.direct:
+            total = finish(chain, keep, recvs)
             recvs = [swap_with(total, mask, self.size) for mask in masks]
             yield
-            total = join(self.chain, (total, *recvs))
-        else:
-            for shift in reversed(range(2, levels)):
-                recv = self.swap(total, shift)
-                yield
-                total = join(self.chain, (total, recv))
+            total = join(chain, (total, *recvs))
         across = self.swap(total, 1)
-        own = (total, across)
-        other = (self.swap(total, 0), self.swap(across, 0))
-        rows, width = total.shape[1:]
+        self.own, self.other = (total, across), (self.swap(total, 0), self.swap(across, 0))
         if rows % 16:
-            blocks = 1 << (levels - 1)
-            order = block_of(self.chain.meta, blocks) ^ jnp.arange(blocks)
-            own, other = (
-                (jnp.concatenate(x, axis=0)[order].reshape(1, blocks * rows, width),) for x in (own, other)
+            order = block_of(chain.meta, 2 * blocks) ^ jnp.arange(2 * blocks)
+            self.own, self.other = (
+                (jnp.swapaxes(jnp.concatenate(x, axis=0)[order], 0, 1).reshape(1, keep.shape[0], -1, keep.shape[2]),)
+                for x in (self.own, self.other)
             )
-        self.result = own, other
+        yield
+
+    def result(self, at):
+        return Summed(self.own, self.other, at)
 
 
 def on_device(size, stem_tensor, leaf_left, leaf_right, slice_bits):
     width = stem_tensor.shape[1]
     place = lax.axis_index("outer").astype(jnp.int32)
     chain = Chain(jnp.concatenate([place[None], slice_bits.astype(jnp.int32)]))
-    fine = width // size * 2 % 16 == 0
     given = exchange(stem_tensor[0])
-
-    sums, runs = {}, {}
-
-    def begin(j):
-        sums[j] = Sum(chain, leaf_left, leaf_right, j, size, fine and j == 0)
-        runs[j] = sums[j].steps()
-
-    def step(*order):
-        for j in order:
-            next(runs[j], None)
-
-    def end(j):
-        for _ in runs[j]:
-            pass
-        return sums[j].result
-
-    begin(0)
-    begin(2)
-    step(0)
-    begin(1)
-    step(2)
-    begin(3)
-    step(0)
-    step(1, 3)
-    step(0)
-    step(2)
+    early, late = Sum(chain, size), Sum(chain, size)
+    early.add(leaf_left, leaf_right, 0)
+    late.add(leaf_left, leaf_right, 2)
+    first = early.steps()
+    next(first)
+    late.add(leaf_left, leaf_right, 1)
+    late.add(leaf_left, leaf_right, 3)
+    second = late.steps()
+    next(second)
+    next(first)
     right = prepare(chain, given)
-    step(0)
-    step(1, 2, 3, 1)
-    end(0)
-    state = first_product(chain, sums[0].result, right).reshape(width, 2 * width)
+    next(first, None)
+    next(second, None)
+    next(first, None)
+    next(second, None)
+    state = first_product(chain, early.result(0), right).reshape(width, 2 * width)
     state = exchange(state)
-    step(2, 3, 1, 2, 3, 1, 2, 3, 1)
-    end(1)
-    end(3)
-    end(2)
-    factor = joined_right(chain, sums[1].result, sums[3].result).reshape(2, width, 2 * width)
-    return last_product(chain, sums[2].result, state, factor, stem_tensor.shape)
+    next(second, None)
+    factor = joined_right(chain, late.result(1), late.result(2)).reshape(2, width, 2 * width)
+    return last_product(chain, late.result(0), state, factor, stem_tensor.shape)
 
 
 def solution(mesh):

time: 165 us -> 181 us (1.097); the launches traced: 162 us -> 181 us
  waiting for transfers between devices: 44.1 us -> 87.4 us
  starting transfers between devices: 73.3 us -> 38.2 us
  local copies, waits for them, and re-layouts: 4.28 us -> 18.7 us
  Pallas kernels: 39.1 us -> 35.4 us
    ppermute x38 -> x24, waiting for transfers between devices: 44.1 us -> 87.4 us  [swap_with(): return lax.ppermute(x, 'outer', [(i, i ^ mask) for i in range(size)])]
    ppermute x38 -> x24, starting transfers between devices: 57.4 us -> 23.1 us  [swap_with(): return lax.ppermute(x, 'outer', [(i, i ^ mask) for i in range(size)])]
    unnamed x12 -> x18, local copies, waits for them, and re-layouts: 4.28 us -> 18.7 us
    pallas_call x30 -> x16, Pallas kernels: 39.1 us -> 35.4 us  [__call__(): pl.pallas_call(kernel, out_shape=shapes, in_specs=specs, out_specs=tuple(...]
  transfers between devices with their start and end apart: 40 -> 26, of which waited for: 11 -> 13; matrix products, arithmetic and copies ran while one was open for 0% -> 0% of each run, Pallas kernels for 19% -> 14%
where the time goes in v3:
time: 181 us
  waiting for transfers between devices  87.4 us (48%)
  starting transfers between devices  38.2 us (21%)
  Pallas kernels  35.4 us (20%)
  local copies, waits for them, and re-layouts  18.7 us (10%)
    ppermute x24, waiting for transfers between devices, swap_with(): return lax.ppermute(x, 'outer', [(i, i ^ mask) for i in range(size)])  87.4 us
    pallas_call x16, Pallas kernels, __call__(): pl.pallas_call(kernel, out_shape=shapes, in_specs=specs, out_specs=tuple(...  35.4 us
    ppermute x24, starting transfers between devices, swap_with(): return lax.ppermute(x, 'outer', [(i, i ^ mask) for i in range(size)])  23.1 us
    unnamed x18, local copies, waits for them, and re-layouts  18.7 us
    all_to_all x2, starting transfers between devices, exchange(): return lax.all_to_all(x, 'outer', split_axis=0, concat_axis=0, tiled=True)  15.1 us
  transfers between devices with their start and end apart: 26, of which 13 were waited for; matrix products, arithmetic and copies ran while one was open for 0% of the time, Pallas kernels for 14%

profile of v3, /device:TPU:11, one launch (start us, length us, event | category | flops | bytes accessed | tf_op | source)
XLA Modules:
  0.0 180.8 jit_solution(5255625391957983218)
XLA Ops:
  0.7 3.4 %copy-done = bf16[4,2,512,2,512]{4,3,2,1,0:T(2,128)(2,1)S(1)} copy-done((bf16[4,2,512,2,512]{4,3,2,1,0:T(2,128)(2,1)S(1)}, bf16[4,2,512,2,512]{4,3,2,1,0:T(2,128)(2,1)}, u32[]{:S(2)}) %copy-start) | copy-done | bytes 8388632
  4.1 3.4 %copy-done.2 = bf16[4,2,512,2,512]{4,3,2,1,0:T(2,128)(2,1)S(1)} copy-done((bf16[4,2,512,2,512]{4,3,2,1,0:T(2,128)(2,1)S(1)}, bf16[4,2,512,2,512]{4,3,2,1,0:T(2,128)(2,1)}, u32[]{:S(2)}) %copy-start.2) | copy-done | bytes 8388632
  7.5 4.1 %shard_map.46 = (f32[512,512]{1,0:T(8,128)S(1)}, bf16[512,512]{1,0:T(8,128)(2,1)}) custom-call(s32[5]{0:T(128)S(1)} %pad_add_fusion.refs_0_, bf16[4,2,512,2,512]{4,3,2,1,0:T(2,128)(2,1)S(1)} %copy-done, bf16[4,2,512,2,512]{4,3,2,1,0:T(2,128)(2,1)S(1)} %copy-done.2), custom_call_target="tpu_custom_call" | custom-call | flops 3500000000 | bytes 1024 | tf_op jit(solution)/shard_map/pallas_call | solution.py:34
  12.3 4.1 %shard_map.47 = (f32[512,512]{1,0:T(8,128)S(1)}, bf16[512,512]{1,0:T(8,128)(2,1)}) custom-call(s32[5]{0:T(128)S(1)} %pad_add_fusion.refs_0_, bf16[4,2,512,2,512]{4,3,2,1,0:T(2,128)(2,1)S(1)} %copy-done, bf16[4,2,512,2,512]{4,3,2,1,0:T(2,128)(2,1)S(1)} %copy-done.2, f32[512,512]{1,0:T(8,128)S(1)} %get-tuple-element.25.refs_3_.refs_1_), custom_call_target="tpu_custom_call" | custom-call | flops 3500000000 | bytes 1024 | tf_op jit(solution)/shard_map/pallas_call | solution.py:34
  17.4 6.4 %all-to-all-start = ((bf16[512,2,512]{2,1,0:T(2,128)(2,1)}), bf16[512,2,512]{2,1,0:T(2,128)(2,1)S(1)}, u32[]{:S(2)}, u32[]{:S(2)}) async-start(bf16[512,2,512]{2,1,0:T(2,128)(2,1)} %bitcast.6), calls=%async_computation | async-start | bytes 2097152 | tf_op jit(solution)/shard_map/all_to_all | solution.py:375
  25.7 3.4 %copy-done.1 = bf16[4,2,512,2,512]{4,3,2,1,0:T(2,128)(2,1)S(1)} copy-done((bf16[4,2,512,2,512]{4,3,2,1,0:T(2,128)(2,1)S(1)}, bf16[4,2,512,2,512]{4,3,2,1,0:T(2,128)(2,1)}, u32[]{:S(2)}) %copy-start.1) | copy-done | bytes 8388632
  29.1 3.4 %copy-done.3 = bf16[4,2,512,2,512]{4,3,2,1,0:T(2,128)(2,1)S(1)} copy-done((bf16[4,2,512,2,512]{4,3,2,1,0:T(2,128)(2,1)S(1)}, bf16[4,2,512,2,512]{4,3,2,1,0:T(2,128)(2,1)}, u32[]{:S(2)}) %copy-start.3) | copy-done | bytes 8388632
  32.5 3.8 %shard_map.49 = (f32[512,512]{1,0:T(8,128)S(1)}, bf16[512,512]{1,0:T(8,128)(2,1)S(1)}) custom-call(s32[5]{0:T(128)S(1)} %pad_add_fusion.refs_0_, bf16[4,2,512,2,512]{4,3,2,1,0:T(2,128)(2,1)S(1)} %copy-done.1, bf16[4,2,512,2,512]{4,3,2,1,0:T(2,128)(2,1)S(1)} %copy-done.3, f32[1,256,512]{2,1,0:T(8,128)S(1)} %get-tuple-element.28.refs_3_.refs_1_), custom_call_target="tpu_custom_call" | custom-call | flops 3500000000 | bytes 1024 | tf_op jit(solution)/shard_map/pallas_call | solution.py:34
  36.3 3.8 %shard_map.50 = (f32[512,512]{1,0:T(8,128)S(1)}, bf16[512,512]{1,0:T(8,128)(2,1)S(1)}) custom-call(s32[5]{0:T(128)S(1)} %pad_add_fusion.refs_0_, bf16[4,2,512,2,512]{4,3,2,1,0:T(2,128)(2,1)S(1)} %copy-done.1, bf16[4,2,512,2,512]{4,3,2,1,0:T(2,128)(2,1)S(1)} %copy-done.3, f32[512,512]{1,0:T(8,128)S(1)} %get-tuple-element.29.refs_3_.refs_2_), custom_call_target="tpu_custom_call" | custom-call | flops 3500000000 | bytes 1024 | tf_op jit(solution)/shard_map/pallas_call | solution.py:34
  46.0 24.7 %collective-permute-done.5.refs_2_ = bf16[1,256,512]{2,1,0:T(8,128)(2,1)S(1)} collective-permute-done((bf16[1,256,512]{2,1,0:T(8,128)(2,1)S(1)}, bf16[1,256,512]{2,1,0:T(8,128)(2,1)S(1)}, u32[]{:S(2)}, u32[]{:S(2)}) %collective-permute-start.5) | collective-permute-done | bytes 262176 | tf_op jit(solution)/shard_map/ppermute | solution.py:189
  74.1 2.7 %shard_map.53.refs_5_ = bf16[2,512,1024]{2,1,0:T(8,128)(2,1)S(1)} custom-call(s32[5]{0:T(128)S(1)} %pad_add_fusion.refs_0_, bf16[512,2,512]{2,1,0:T(2,128)(2,1)S(1)} %all-to-all-done.refs_1_, f32[1,64,512]{2,1,0:T(8,128)S(1)} %get-tuple-element.37.refs_2_.refs_1_), custom_call_target="tpu_custom_call" | custom-call | flops 1000000000 | bytes 1024 | tf_op jit(solution)/shard_map/pallas_call | solution.py:34
  84.0 2.9 %collective-permute-done.14.refs_4_ = bf16[1,1,64,512]{3,2,1,0:T(8,128)(2,1)S(1)} collective-permute-done((bf16[1,1,64,512]{3,2,1,0:T(8,128)(2,1)S(1)}, bf16[1,1,64,512]{3,2,1,0:T(8,128)(2,1)S(1)}, u32[]{:S(2)}, u32[]{:S(2)}) %collective-permute-start.14) | collective-permute-done | bytes 65568 | tf_op jit(solution)/shard_map/ppermute | solution.py:189
  90.1 3.9 %collective-permute-done.18.refs_2_ = bf16[4,1,64,512]{3,2,1,0:T(8,128)(2,1)S(1)} collective-permute-done((bf16[4,1,64,512]{3,2,1,0:T(8,128)(2,1)S(1)}, bf16[4,1,64,512]{3,2,1,0:T(8,128)(2,1)S(1)}, u32[]{:S(2)}, u32[]{:S(2)}) %collective-permute-start.18) | collective-permute-done | bytes 262176 | tf_op jit(solution)/shard_map/ppermute | solution.py:189
  94.0 2.3 %collective-permute-start.20 = (bf16[4,1,64,512]{3,2,1,0:T(8,128)(2,1)S(1)}, bf16[4,1,64,512]{3,2,1,0:T(8,128)(2,1)S(1)}, u32[]{:S(2)}, u32[]{:S(2)}) collective-permute-start(bf16[4,1,64,512]{3,2,1,0:T(8,128)(2,1)S(1)} %collective-permute-done.18.refs_2_), channel_id=1, source_target_pairs={{0,1},{1,0},{2,3},{3,2},{4,5},{5,4},{6,7},{7,6},{8,9},{9,8},{10,11... | collective-permute-start | bytes 786440 | tf_op jit(solution)/shard_map/ppermute | solution.py:189
  99.9 3.0 %collective-permute-done.10.refs_3_ = bf16[3,64,512]{2,1,0:T(8,128)(2,1)S(1)} collective-permute-done((bf16[3,64,512]{2,1,0:T(8,128)(2,1)S(1)}, bf16[3,64,512]{2,1,0:T(8,128)(2,1)S(1)}, u32[]{:S(2)}, u32[]{:S(2)}) %collective-permute-start.10) | collective-permute-done | bytes 196640 | tf_op jit(solution)/shard_map/ppermute | solution.py:189
  102.8 9.4 %collective-permute-done.11.refs_4_ = bf16[3,64,512]{2,1,0:T(8,128)(2,1)S(1)} collective-permute-done((bf16[3,64,512]{2,1,0:T(8,128)(2,1)S(1)}, bf16[3,64,512]{2,1,0:T(8,128)(2,1)S(1)}, u32[]{:S(2)}, u32[]{:S(2)}) %collective-permute-start.11) | collective-permute-done | bytes 196640 | tf_op jit(solution)/shard_map/ppermute | solution.py:189
  112.3 2.5 %collective-permute-done.9.refs_2_ = bf16[3,64,512]{2,1,0:T(8,128)(2,1)S(1)} collective-permute-done((bf16[3,64,512]{2,1,0:T(8,128)(2,1)S(1)}, bf16[3,64,512]{2,1,0:T(8,128)(2,1)S(1)}, u32[]{:S(2)}, u32[]{:S(2)}) %collective-permute-start.9) | collective-permute-done | bytes 196640 | tf_op jit(solution)/shard_map/ppermute | solution.py:189
  115.4 3.2 %collective-permute-start.15 = (bf16[1,3,64,512]{3,2,1,0:T(8,128)(2,1)S(1)}, bf16[1,3,64,512]{3,2,1,0:T(8,128)(2,1)S(1)}, u32[]{:S(2)}, u32[]{:S(2)}) collective-permute-start(bf16[1,3,64,512]{3,2,1,0:T(8,128)(2,1)S(1)} %shard_map.57.refs_6_.refs_1_), channel_id=1, source_target_pairs={{0,8},{1,9},{2,10},{3,11},{4,12},{5,13},{6,14},{7,15},{8,0},{9,1},... | collective-permute-start | bytes 589832 | tf_op jit(solution)/shard_map/ppermute | solution.py:189
  119.6 2.8 %shard_map.58.refs_5_ = bf16[8,64,1024]{2,1,0:T(8,128)(2,1)} custom-call(s32[5]{0:T(128)S(1)} %pad_add_fusion.refs_0_, bf16[4,1,64,512]{3,2,1,0:T(8,128)(2,1)S(1)} %shard_map.56.refs_5_.refs_1_, bf16[4,1,64,512]{3,2,1,0:T(8,128)(2,1)S(1)} %collective-permute-done.18.refs_2_, bf16[4,1,64,512]{3,2,1,0:T(8,128)(2,1)S(1)} %collective-permute-done.19.refs_3_, ...), custom_call_target="tpu_custom_call" | custom-call | flops 2800000000 | bytes 1024 | tf_op jit(solution)/shard_map/pallas_call | solution.py:34
  122.4 8.7 %all-to-all-start.1 = ((bf16[16,32,1024]{2,1,0:T(8,128)(2,1)}), bf16[16,32,1024]{2,1,0:T(8,128)(2,1)}, u32[]{:S(2)}, u32[]{:S(2)}) async-start(bf16[16,32,1024]{2,1,0:T(8,128)(2,1)} %bitcast.2), calls=%async_computation.1 | async-start | bytes 2097152 | tf_op jit(solution)/shard_map/all_to_all | solution.py:375
  131.1 11.3 %collective-permute-done.17.refs_4_ = bf16[1,3,64,512]{3,2,1,0:T(8,128)(2,1)S(1)} collective-permute-done((bf16[1,3,64,512]{3,2,1,0:T(8,128)(2,1)S(1)}, bf16[1,3,64,512]{3,2,1,0:T(8,128)(2,1)S(1)}, u32[]{:S(2)}, u32[]{:S(2)}) %collective-permute-start.17) | collective-permute-done | bytes 196640 | tf_op jit(solution)/shard_map/ppermute | solution.py:189
  144.5 23.1 %collective-permute-done.21.refs_2_.refs_6_ = bf16[4,3,64,512]{3,2,1,0:T(8,128)(2,1)S(1)} collective-permute-done((bf16[4,3,64,512]{3,2,1,0:T(8,128)(2,1)S(1)}, bf16[4,3,64,512]{3,2,1,0:T(8,128)(2,1)S(1)}, u32[]{:S(2)}, u32[]{:S(2)}) %collective-permute-start.21) | collective-permute-done | bytes 786464 | tf_op jit(solution)/shard_map/ppermute | solution.py:189
  170.2 2.0 %shard_map.60.refs_7_ = bf16[2,8,64,1024]{3,2,1,0:T(8,128)(2,1)S(1)} custom-call(s32[5]{0:T(128)S(1)} %pad_add_fusion.refs_0_, bf16[4,3,64,512]{3,2,1,0:T(8,128)(2,1)S(1)} %shard_map.59.refs_1_.refs_5_.refs_9_, bf16[4,3,64,512]{3,2,1,0:T(8,128)(2,1)S(1)} %collective-permute-done.21.refs_2_.refs_6_, ...), custom_call_target="tpu_custom_call" | custom-call | flops 2000000000 | bytes 1024 | tf_op jit(solution)/shard_map/pallas_call | solution.py:34
  175.1 5.5 %shard_map.61 = bf16[1,512,2,512]{3,2,1,0:T(2,128)(2,1)} custom-call(s32[5]{0:T(128)S(1)} %pad_add_fusion.refs_0_, bf16[4,3,64,512]{3,2,1,0:T(8,128)(2,1)S(1)} %shard_map.59.refs_1_.refs_5_.refs_9_, bf16[4,3,64,512]{3,2,1,0:T(8,128)(2,1)S(1)} %collective-permute-done.21.refs_2_.refs_6_, bf16[4,3,64,512]{3,2,1,0:T(8,128)(2,1)S(1)} %collective-permute-done.22.refs_3_.refs_7_, ...), custom_call_target="tpu_custom_call" | custom-call | flops 5000000000 | bytes 1024 | tf_op jit(solution)/shard_map/pallas_call | solution.py:34
  (63 shorter events, 36.6 us)
Async XLA Ops:
  11.6 12.3 %collective-permute-start = (bf16[512,512]{1,0:T(8,128)(2,1)}, bf16[512,512]{1,0:T(8,128)(2,1)S(1)}, u32[]{:S(2)}, u32[]{:S(2)}) collective-permute-start(bf16[512,512]{1,0:T(8,128)(2,1)} %get-tuple-element.27), channel_id=1, source_target_pairs={{0,1},{1,0},{2,3},{3,2},{4,5},{5,4},{6,7},{7,6},{8,9},{9,8},{10,11... | collective-permute-start | bytes 1572872 | tf_op jit(solution)/shard_map/ppermute | solution.py:189
  17.4 23.3 %collective-permute-start.1 = (bf16[512,512]{1,0:T(8,128)(2,1)}, bf16[512,512]{1,0:T(8,128)(2,1)S(1)}, u32[]{:S(2)}, u32[]{:S(2)}) collective-permute-start(bf16[512,512]{1,0:T(8,128)(2,1)} %get-tuple-element.31), channel_id=1, source_target_pairs={{0,1},{1,0},{2,3},{3,2},{4,5},{5,4},{6,7},{7,6},{8,9},{9,8},{10,11... | collective-permute-start | bytes 1572872 | tf_op jit(solution)/shard_map/ppermute | solution.py:189
  17.4 56.6 %all-to-all-start = ((bf16[512,2,512]{2,1,0:T(2,128)(2,1)}), bf16[512,2,512]{2,1,0:T(2,128)(2,1)S(1)}, u32[]{:S(2)}, u32[]{:S(2)}) async-start(bf16[512,2,512]{2,1,0:T(2,128)(2,1)} %bitcast.6), calls=%async_computation | async-start | bytes 2097152 | tf_op jit(solution)/shard_map/all_to_all | solution.py:375
  44.5 37.2 %collective-permute-start.4 = (bf16[3,256,512]{2,1,0:T(8,128)(2,1)}, bf16[3,256,512]{2,1,0:T(8,128)(2,1)}, u32[]{:S(2)}, u32[]{:S(2)}) collective-permute-start(bf16[3,256,512]{2,1,0:T(8,128)(2,1)} %get-tuple-element.35), channel_id=1, source_target_pairs={{0,2},{1,3},{2,0},{3,1},{4,6},{5,7},{6,4},{7,5},{8,10},{9,11},{10,... | collective-permute-start | bytes 2359304 | tf_op jit(solution)/shard_map/ppermute | solution.py:189
  45.7 25.0 %collective-permute-start.5 = (bf16[1,256,512]{2,1,0:T(8,128)(2,1)S(1)}, bf16[1,256,512]{2,1,0:T(8,128)(2,1)S(1)}, u32[]{:S(2)}, u32[]{:S(2)}) collective-permute-start(bf16[1,256,512]{2,1,0:T(8,128)(2,1)S(1)} %get-tuple-element.36), channel_id=1, source_target_pairs={{0,2},{1,3},{2,0},{3,1},{4,6},{5,7},{6,4},{7,5},{8,10},{9,11},{10,... | collective-permute-start | bytes 786440 | tf_op jit(solution)/shard_map/ppermute | solution.py:189
  71.3 5.5 %collective-permute-start.6 = (bf16[1,64,512]{2,1,0:T(8,128)(2,1)S(1)}, bf16[1,64,512]{2,1,0:T(8,128)(2,1)S(1)}, u32[]{:S(2)}, u32[]{:S(2)}) collective-permute-start(bf16[1,64,512]{2,1,0:T(8,128)(2,1)S(1)} %get-tuple-element.38), channel_id=1, source_target_pairs={{0,8},{1,9},{2,10},{3,11},{4,12},{5,13},{6,14},{7,15},{8,0},{9,1},... | collective-permute-start | bytes 196616 | tf_op jit(solution)/shard_map/ppermute | solution.py:189
  72.1 4.7 %collective-permute-start.7 = (bf16[1,64,512]{2,1,0:T(8,128)(2,1)S(1)}, bf16[1,64,512]{2,1,0:T(8,128)(2,1)S(1)}, u32[]{:S(2)}, u32[]{:S(2)}) collective-permute-start(bf16[1,64,512]{2,1,0:T(8,128)(2,1)S(1)} %get-tuple-element.39), channel_id=1, source_target_pairs={{0,4},{1,5},{2,6},{3,7},{4,0},{5,1},{6,2},{7,3},{8,12},{9,13},{10,... | collective-permute-start | bytes 196616 | tf_op jit(solution)/shard_map/ppermute | solution.py:189
  73.8 4.4 %collective-permute-start.8 = (bf16[1,64,512]{2,1,0:T(8,128)(2,1)S(1)}, bf16[1,64,512]{2,1,0:T(8,128)(2,1)S(1)}, u32[]{:S(2)}, u32[]{:S(2)}) collective-permute-start(bf16[1,64,512]{2,1,0:T(8,128)(2,1)S(1)} %get-tuple-element.40), channel_id=1, source_target_pairs={{0,12},{1,13},{2,14},{3,15},{4,8},{5,9},{6,10},{7,11},{8,4},{9,5},... | collective-permute-start | bytes 196616 | tf_op jit(solution)/shard_map/ppermute | solution.py:189
  78.8 4.2 %collective-permute-start.12 = (bf16[1,1,64,512]{3,2,1,0:T(8,128)(2,1)S(1)}, bf16[1,1,64,512]{3,2,1,0:T(8,128)(2,1)S(1)}, u32[]{:S(2)}, u32[]{:S(2)}) collective-permute-start(bf16[1,1,64,512]{3,2,1,0:T(8,128)(2,1)S(1)} %shard_map.54.refs_3_.refs_1_), channel_id=1, source_target_pairs={{0,8},{1,9},{2,10},{3,11},{4,12},{5,13},{6,14},{7,15},{8,0},{9,1},... | collective-permute-start | bytes 196616 | tf_op jit(solution)/shard_map/ppermute | solution.py:189
  80.5 3.5 %collective-permute-start.13 = (bf16[1,1,64,512]{3,2,1,0:T(8,128)(2,1)S(1)}, bf16[1,1,64,512]{3,2,1,0:T(8,128)(2,1)S(1)}, u32[]{:S(2)}, u32[]{:S(2)}) collective-permute-start(bf16[1,1,64,512]{3,2,1,0:T(8,128)(2,1)S(1)} %shard_map.54.refs_3_.refs_1_), channel_id=1, source_target_pairs={{0,4},{1,5},{2,6},{3,7},{4,0},{5,1},{6,2},{7,3},{8,12},{9,13},{10,... | collective-permute-start | bytes 196616 | tf_op jit(solution)/shard_map/ppermute | solution.py:189
  81.7 5.3 %collective-permute-start.14 = (bf16[1,1,64,512]{3,2,1,0:T(8,128)(2,1)S(1)}, bf16[1,1,64,512]{3,2,1,0:T(8,128)(2,1)S(1)}, u32[]{:S(2)}, u32[]{:S(2)}) collective-permute-start(bf16[1,1,64,512]{3,2,1,0:T(8,128)(2,1)S(1)} %shard_map.54.refs_3_.refs_1_), channel_id=1, source_target_pairs={{0,12},{1,13},{2,14},{3,15},{4,8},{5,9},{6,10},{7,11},{8,4},{9,5},... | collective-permute-start | bytes 196616 | tf_op jit(solution)/shard_map/ppermute | solution.py:189
  87.5 6.5 %collective-permute-start.18 = (bf16[4,1,64,512]{3,2,1,0:T(8,128)(2,1)S(1)}, bf16[4,1,64,512]{3,2,1,0:T(8,128)(2,1)S(1)}, u32[]{:S(2)}, u32[]{:S(2)}) collective-permute-start(bf16[4,1,64,512]{3,2,1,0:T(8,128)(2,1)S(1)} %shard_map.56.refs_5_.refs_1_), channel_id=1, source_target_pairs={{0,2},{1,3},{2,0},{3,1},{4,6},{5,7},{6,4},{7,5},{8,10},{9,11},{10,... | collective-permute-start | bytes 786440 | tf_op jit(solution)/shard_map/ppermute | solution.py:189
  88.3 31.3 %collective-permute-start.19 = (bf16[4,1,64,512]{3,2,1,0:T(8,128)(2,1)S(1)}, bf16[4,1,64,512]{3,2,1,0:T(8,128)(2,1)S(1)}, u32[]{:S(2)}, u32[]{:S(2)}) collective-permute-start(bf16[4,1,64,512]{3,2,1,0:T(8,128)(2,1)S(1)} %shard_map.56.refs_5_.refs_1_), channel_id=1, source_target_pairs={{0,1},{1,0},{2,3},{3,2},{4,5},{5,4},{6,7},{7,6},{8,9},{9,8},{10,11... | collective-permute-start | bytes 786440 | tf_op jit(solution)/shard_map/ppermute | solution.py:189
  94.0 25.5 %collective-permute-start.20 = (bf16[4,1,64,512]{3,2,1,0:T(8,128)(2,1)S(1)}, bf16[4,1,64,512]{3,2,1,0:T(8,128)(2,1)S(1)}, u32[]{:S(2)}, u32[]{:S(2)}) collective-permute-start(bf16[4,1,64,512]{3,2,1,0:T(8,128)(2,1)S(1)} %collective-permute-done.18.refs_2_), channel_id=1, source_target_pairs={{0,1},{1,0},{2,3},{3,2},{4,5},{5,4},{6,7},{7,6},{8,9},{9,8},{10,11... | collective-permute-start | bytes 786440 | tf_op jit(solution)/shard_map/ppermute | solution.py:189
  96.3 6.5 %collective-permute-start.10 = (bf16[3,64,512]{2,1,0:T(8,128)(2,1)S(1)}, bf16[3,64,512]{2,1,0:T(8,128)(2,1)S(1)}, u32[]{:S(2)}, u32[]{:S(2)}) collective-permute-start(bf16[3,64,512]{2,1,0:T(8,128)(2,1)S(1)} %get-tuple-element.43), channel_id=1, source_target_pairs={{0,4},{1,5},{2,6},{3,7},{4,0},{5,1},{6,2},{7,3},{8,12},{9,13},{10,... | collective-permute-start | bytes 589832 | tf_op jit(solution)/shard_map/ppermute | solution.py:189
  97.6 14.6 %collective-permute-start.11 = (bf16[3,64,512]{2,1,0:T(8,128)(2,1)S(1)}, bf16[3,64,512]{2,1,0:T(8,128)(2,1)S(1)}, u32[]{:S(2)}, u32[]{:S(2)}) collective-permute-start(bf16[3,64,512]{2,1,0:T(8,128)(2,1)S(1)} %get-tuple-element.44), channel_id=1, source_target_pairs={{0,12},{1,13},{2,14},{3,15},{4,8},{5,9},{6,10},{7,11},{8,4},{9,5},... | collective-permute-start | bytes 589832 | tf_op jit(solution)/shard_map/ppermute | solution.py:189
  98.2 16.7 %collective-permute-start.9 = (bf16[3,64,512]{2,1,0:T(8,128)(2,1)S(1)}, bf16[3,64,512]{2,1,0:T(8,128)(2,1)S(1)}, u32[]{:S(2)}, u32[]{:S(2)}) collective-permute-start(bf16[3,64,512]{2,1,0:T(8,128)(2,1)S(1)} %get-tuple-element.42), channel_id=1, source_target_pairs={{0,8},{1,9},{2,10},{3,11},{4,12},{5,13},{6,14},{7,15},{8,0},{9,1},... | collective-permute-start | bytes 589832 | tf_op jit(solution)/shard_map/ppermute | solution.py:189
  115.4 15.6 %collective-permute-start.15 = (bf16[1,3,64,512]{3,2,1,0:T(8,128)(2,1)S(1)}, bf16[1,3,64,512]{3,2,1,0:T(8,128)(2,1)S(1)}, u32[]{:S(2)}, u32[]{:S(2)}) collective-permute-start(bf16[1,3,64,512]{3,2,1,0:T(8,128)(2,1)S(1)} %shard_map.57.refs_6_.refs_1_), channel_id=1, source_target_pairs={{0,8},{1,9},{2,10},{3,11},{4,12},{5,13},{6,14},{7,15},{8,0},{9,1},... | collective-permute-start | bytes 589832 | tf_op jit(solution)/shard_map/ppermute | solution.py:189
  118.6 12.5 %collective-permute-start.16 = (bf16[1,3,64,512]{3,2,1,0:T(8,128)(2,1)S(1)}, bf16[1,3,64,512]{3,2,1,0:T(8,128)(2,1)S(1)}, u32[]{:S(2)}, u32[]{:S(2)}) collective-permute-start(bf16[1,3,64,512]{3,2,1,0:T(8,128)(2,1)S(1)} %shard_map.57.refs_6_.refs_1_), channel_id=1, source_target_pairs={{0,4},{1,5},{2,6},{3,7},{4,0},{5,1},{6,2},{7,3},{8,12},{9,13},{10,... | collective-permute-start | bytes 589832 | tf_op jit(solution)/shard_map/ppermute | solution.py:189
  118.6 23.8 %collective-permute-start.17 = (bf16[1,3,64,512]{3,2,1,0:T(8,128)(2,1)S(1)}, bf16[1,3,64,512]{3,2,1,0:T(8,128)(2,1)S(1)}, u32[]{:S(2)}, u32[]{:S(2)}) collective-permute-start(bf16[1,3,64,512]{3,2,1,0:T(8,128)(2,1)S(1)} %shard_map.57.refs_6_.refs_1_), channel_id=1, source_target_pairs={{0,12},{1,13},{2,14},{3,15},{4,8},{5,9},{6,10},{7,11},{8,4},{9,5},... | collective-permute-start | bytes 589832 | tf_op jit(solution)/shard_map/ppermute | solution.py:189
  122.4 51.1 %all-to-all-start.1 = ((bf16[16,32,1024]{2,1,0:T(8,128)(2,1)}), bf16[16,32,1024]{2,1,0:T(8,128)(2,1)}, u32[]{:S(2)}, u32[]{:S(2)}) async-start(bf16[16,32,1024]{2,1,0:T(8,128)(2,1)} %bitcast.2), calls=%async_computation.1 | async-start | bytes 2097152 | tf_op jit(solution)/shard_map/all_to_all | solution.py:375
  143.0 24.6 %collective-permute-start.21 = (bf16[4,3,64,512]{3,2,1,0:T(8,128)(2,1)S(1)}, bf16[4,3,64,512]{3,2,1,0:T(8,128)(2,1)S(1)}, u32[]{:S(2)}, u32[]{:S(2)}) collective-permute-start(bf16[4,3,64,512]{3,2,1,0:T(8,128)(2,1)S(1)} %shard_map.59.refs_1_.refs_5_.refs_9_), channel_id=1, source_target_pairs={{0,2},{1,3},{2,0},{3,1},{4,6},{5,7},{6,4},{7,5},{8,10},{9,11},{10,... | collective-permute-start | bytes 2359304 | tf_op jit(solution)/shard_map/ppermute | solution.py:189
  143.6 24.7 %collective-permute-start.22 = (bf16[4,3,64,512]{3,2,1,0:T(8,128)(2,1)S(1)}, bf16[4,3,64,512]{3,2,1,0:T(8,128)(2,1)S(1)}, u32[]{:S(2)}, u32[]{:S(2)}) collective-permute-start(bf16[4,3,64,512]{3,2,1,0:T(8,128)(2,1)S(1)} %shard_map.59.refs_1_.refs_5_.refs_9_), channel_id=1, source_target_pairs={{0,1},{1,0},{2,3},{3,2},{4,5},{5,4},{6,7},{7,6},{8,9},{9,8},{10,11... | collective-permute-start | bytes 2359304 | tf_op jit(solution)/shard_map/ppermute | solution.py:189
  167.6 2.6 %collective-permute-start.23 = (bf16[4,3,64,512]{3,2,1,0:T(8,128)(2,1)S(1)}, bf16[4,3,64,512]{3,2,1,0:T(8,128)(2,1)S(1)}, u32[]{:S(2)}, u32[]{:S(2)}) collective-permute-start(bf16[4,3,64,512]{3,2,1,0:T(8,128)(2,1)S(1)} %collective-permute-done.21.refs_2_.refs_6_), channel_id=1, source_target_pairs={{0,1},{1,0},{2,3},{3,2},{4,5},{5,4},{6,7},{7,6},{8,9},{9,8},{10,11... | collective-permute-start | bytes 2359304 | tf_op jit(solution)/shard_map/ppermute | solution.py:189
  (11 other events, 29.5 us)

commit v4 on v3

--- a/solution.py
+++ b/solution.py
@@ -8,24 +8,27 @@
 from jax.sharding import PartitionSpec as P
 
 VMEM_LIMIT = 24 << 20
+LEAF_LIMIT = 48 << 20
+LEAF, HALVE, SPREAD, FINISH, JOIN = 0.1, 2.0, 10.0, 10.0, 10.0
+PREPARE, FIRST, JOINED, LAST = 1.0, 2.8, 2.0, 5.0
 TILE = 256
 bf16, f32 = jnp.bfloat16, jnp.float32
 
 SMEM_SPEC = pl.BlockSpec(memory_space=pltpu.SMEM)
 VMEM_SPEC = pl.BlockSpec(memory_space=pltpu.VMEM)
 ANY_SPEC = pl.BlockSpec(memory_space=pl.ANY)
-
-
-class Chain:
+HBM_SPEC = pl.BlockSpec(memory_space=pltpu.HBM)
+
+
+class Calls:
     def __init__(self, meta):
-        self.meta, self.last = meta, None
-
-    def __call__(self, body, shapes, in_specs, operands, scratch=(), out_specs=None, us=1.0):
+        self.meta, self.last = meta, ()
+
+    def __call__(self, body, shapes, in_specs, operands, scratch=(), out_specs=None, us=1.0, limit=VMEM_LIMIT):
         many = isinstance(shapes, (tuple, list))
         shapes = tuple(shapes) if many else (shapes,)
-        specs, extra = [SMEM_SPEC] + list(in_specs), []
-        if self.last is not None:
-            specs, extra = specs + [ANY_SPEC], [self.last]
+        after = self.last
+        specs = [SMEM_SPEC] + list(in_specs) + [ANY_SPEC] * len(after)
         count = len(specs)
 
         def kernel(*refs):
@@ -37,10 +40,10 @@
             in_specs=specs,
             out_specs=tuple(out_specs or [VMEM_SPEC] * len(shapes)),
             scratch_shapes=list(scratch),
-            compiler_params=pltpu.CompilerParams(vmem_limit_bytes=VMEM_LIMIT),
+            compiler_params=pltpu.CompilerParams(vmem_limit_bytes=limit),
             cost_estimate=pl.CostEstimate(flops=int(us * 1e9), bytes_accessed=1024, transcendentals=0),
-        )(self.meta, *operands, *extra)
-        self.last = out[0]
+        )(self.meta, *operands, *after)
+        self.last = (out[0],)
         return out if many else out[0]
 
 
@@ -67,70 +70,83 @@
     return reversed_bits(meta[0] >> 1, blocks.bit_length() - 1)
 
 
-def leaf_body(branch, meta, left, right, keep, send, lhs, rhs, both, sems):
+def leaf_body(groups, meta, left, right, *refs):
+    outs, (lhs, rhs, both, sems) = refs[:-4], refs[-4:]
     depth, width = left.shape[2], left.shape[4]
     core = meta[0] & 1
-    first, second = (right, left) if branch % 2 == 0 else (left, right)
+    keep_at = pl.ds(pl.multiple_of(core * width, width), width)
+    send_at = pl.ds(pl.multiple_of((1 - core) * width, width), width)
+    branches = [branch for group in groups for branch in group]
     copies = []
-    for which, (ref, buf) in enumerate(((second, rhs), (first, lhs))):
-        flat = ref.reshape(ref.shape[0], ref.shape[1], 2 * depth, width)
-        copies.append(pltpu.make_async_copy(flat.at[branch, meta[1 + branch]], buf, sems.at[which]))
-        copies[-1].start()
+    for at, branch in enumerate(branches):
+        first, second = (right, left) if branch % 2 == 0 else (left, right)
+        for which, (ref, buf) in enumerate(((second, rhs), (first, lhs))):
+            flat = ref.reshape(ref.shape[0], ref.shape[1], 2 * depth, width)
+            copies.append(
+                pltpu.make_async_copy(flat.at[branch, meta[1 + branch]], buf.at[at], sems.at[at, which])
+            )
+            copies[-1].start()
     rows = lax.broadcasted_iota(jnp.int32, (2 * depth // 8, 8, width), 1)
     is_real = (rows & 1) == 0
-    copies[0].wait()
-    wide = rhs[...].astype(f32).reshape(2 * depth // 8, 8, width)
-    signed = jnp.where(is_real, wide, -wide)
-    swapped = jnp.where(is_real, pltpu.roll(wide, 7, 1), pltpu.roll(wide, 1, 1))
-    both[core] = signed.reshape(2 * depth, width).astype(bf16)
-    both[1 - core] = swapped.reshape(2 * depth, width).astype(bf16)
-    copies[1].wait()
-    send[...] = tdot(lhs[...], both[1]).astype(bf16)
-    keep[...] = tdot(lhs[...], both[0])
-
-
-def leaf_partial(chain, left, right, branch):
+    at = 0
+    for group, keep, send in zip(groups, outs[0::2], outs[1::2], strict=True):
+        for inside in range(len(group)):
+            copies[2 * at].wait()
+            wide = rhs[at].astype(f32).reshape(2 * depth // 8, 8, width)
+            signed = jnp.where(is_real, wide, -wide)
+            swapped = jnp.where(is_real, pltpu.roll(wide, 7, 1), pltpu.roll(wide, 1, 1))
+            both[at % 2, :, keep_at] = signed.reshape(2 * depth, width).astype(bf16)
+            both[at % 2, :, send_at] = swapped.reshape(2 * depth, width).astype(bf16)
+            copies[2 * at + 1].wait()
+            value = tdot(lhs[at], both[at % 2])
+            keep[inside] = value[:, :width]
+            send[inside] = value[:, width:].astype(bf16)
+            at += 1
+
+
+def leaf_partials(chain, left, right, groups):
     depth, width = left.shape[2], left.shape[4]
-    return chain(
-        functools.partial(leaf_body, branch),
-        (shaped((width, width), f32), shaped((width, width))),
+    count = sum(len(group) for group in groups)
+    shapes = [shaped((len(group), width, width), dtype) for group in groups for dtype in (f32, bf16)]
+    outs = chain(
+        functools.partial(leaf_body, groups),
+        shapes,
         [ANY_SPEC, ANY_SPEC],
         (left, right),
         [
-            pltpu.VMEM((2 * depth, width), bf16),
-            pltpu.VMEM((2 * depth, width), bf16),
-            pltpu.VMEM((2, 2 * depth, width), bf16),
-            pltpu.SemaphoreType.DMA((2,)),
+            pltpu.VMEM((count, 2 * depth, width), bf16),
+            pltpu.VMEM((count, 2 * depth, width), bf16),
+            pltpu.VMEM((2, 2 * depth, 2 * width), bf16),
+            pltpu.SemaphoreType.DMA((count, 2)),
         ],
-        us=3.5,
-    )
-
-
-def half_body(count, shift, meta, *refs):
-    keeps, recvs, (keep_out, send_out) = refs[:count], refs[count : 2 * count], refs[2 * count :]
+        us=LEAF,
+        limit=LEAF_LIMIT,
+    )
+    return list(zip(outs[0::2], outs[1::2], strict=True))
+
+
+def half_body(shift, meta, keep, recv, keep_out, send_out):
     half = keep_out.shape[1]
     bit = (meta[0] >> shift) & 1
     mine = pl.ds(pl.multiple_of(bit * half, half), half)
     other = pl.ds(pl.multiple_of((1 - bit) * half, half), half)
-    for at, (keep, recv) in enumerate(zip(keeps, recvs, strict=True)):
-        send_out[at] = (keep[other] + recv[other].astype(f32)).astype(bf16)
-        keep_out[at] = keep[mine] + recv[mine].astype(f32)
-
-
-def halve(chain, keeps, recvs, shift):
-    count, (rows, width) = len(keeps), keeps[0].shape
+    send_out[...] = (keep[:, other] + recv[:, other].astype(f32)).astype(bf16)
+    keep_out[...] = keep[:, mine] + recv[:, mine].astype(f32)
+
+
+def halve(chain, keep, recv, shift):
+    count, rows, width = keep.shape
     half = rows // 2
     if half % 16:
-        total = jnp.stack([keep + recv.astype(f32) for keep, recv in zip(keeps, recvs, strict=True)])
-        total = total.reshape(count, 2, half, width)
+        total = (keep + recv.astype(f32)).reshape(count, 2, half, width)
         bit = (chain.meta[0] >> shift) & 1
         return total[:, bit], total[:, 1 - bit].astype(bf16)
     return chain(
-        functools.partial(half_body, count, shift),
+        functools.partial(half_body, shift),
         (shaped((count, half, width), f32), shaped((count, half, width))),
-        [VMEM_SPEC] * (2 * count),
-        (*keeps, *recvs),
-        us=0.6 * count,
+        [VMEM_SPEC] * 2,
+        (keep, recv),
+        us=HALVE,
     )
 
 
@@ -154,7 +170,7 @@
         (shaped((count, rows, width), f32),) + (shaped((count, rows, width)),) * (blocks - 1),
         [VMEM_SPEC] * 2,
         (keep, recv),
-        us=0.6 * count,
+        us=SPREAD,
     )
 
 
@@ -168,7 +184,7 @@
 def finish(chain, keep, recvs):
     if keep.shape[1] % 16:
         return (keep + sum(recv.astype(f32) for recv in recvs)).astype(bf16)[None]
-    return chain(finish_body, shaped((1, *keep.shape)), [VMEM_SPEC] * (1 + len(recvs)), (keep, *recvs), us=0.6)
+    return chain(finish_body, shaped((1, *keep.shape)), [VMEM_SPEC] * (1 + len(recvs)), (keep, *recvs), us=FINISH)
 
 
 def join_body(meta, *refs):
@@ -182,7 +198,7 @@
     blocks, shape = sum(part.shape[0] for part in parts), parts[0].shape[1:]
     if shape[1] % 16:
         return jnp.concatenate(parts, axis=0)
-    return chain(join_body, shaped((blocks, *shape)), [VMEM_SPEC] * len(parts), parts, us=0.6)
+    return chain(join_body, shaped((blocks, *shape)), [VMEM_SPEC] * len(parts), parts, us=JOIN)
 
 
 def swap_with(x, mask, size):
@@ -214,6 +230,7 @@
         [VMEM_SPEC],
         (stem,),
         [pltpu.VMEM((width // 128, 2 * count, 128), f32)],
+        us=PREPARE,
     )
 
 
@@ -248,14 +265,24 @@
         shaped((branch.blocks, branch.rows, 2 * branch.width)),
         [VMEM_SPEC] * (2 * branch.parts + 1),
         (*branch.operands, right),
-        us=2.8,
-    )
-
-
-def joined_body(parts, at0, at1, meta, *refs):
-    own0, other0, own1, other1 = (refs[at * parts : (at + 1) * parts] for at in range(4))
-    out, right = refs[4 * parts :]
-    _, blocks, rows, columns = out.shape
+        us=FIRST,
+    )
+
+
+def joined_body(parts, at0, at1, at2, meta, *refs):
+    own0, other0, own1, other1, own2, other2 = (refs[at * parts : (at + 1) * parts] for at in range(6))
+    result, moved, right, out, sems = refs[-5:]
+    copies = []
+    for plane, refs_of in enumerate((own2, other2)):
+        at = 0
+        for ref in refs_of:
+            size = ref.shape[0]
+            copies.append(
+                pltpu.make_async_copy(ref.at[:, at2], moved.at[plane, pl.ds(at, size)], sems.at[len(copies)])
+            )
+            copies[-1].start()
+            at += size
+    blocks, rows, columns = out.shape
     width = columns // 2
     me = block_of(meta, blocks)
     core = meta[0] & 1
@@ -273,48 +300,44 @@
     mine, theirs = rows_of(own0, at0), rows_of(other0, at0)
     for at in range(columns // TILE):
         here = slice(at * TILE, (at + 1) * TILE)
-        there = slice((at * TILE + width) % columns, (at * TILE + width) % columns + TILE)
         first = right[0, :, :, here].reshape(blocks * rows, TILE)
         second = right[1, :, :, here].reshape(blocks * rows, TILE)
         value = dot(mine, first) + dot(theirs, second)
-        turned = value if at * TILE < width else -value
         value = value.astype(bf16).reshape(blocks, rows, TILE)
-        turned = turned.astype(bf16).reshape(blocks, rows, TILE)
         for t in range(blocks):
-            out[0, me ^ t, :, here] = value[t]
-            out[1, me ^ t, :, there] = turned[t]
-
-
-def joined_right(chain, first, second):
+            out[me ^ t, :, here] = value[t]
+    copies.append(pltpu.make_async_copy(out, result, sems.at[len(copies)]))
+    copies[-1].start()
+    for copy in copies:
+        copy.wait()
+
+
+def joined_right(chain, first, second, third):
     blocks, rows, width = first.blocks, first.rows, first.width
     return chain(
-        functools.partial(joined_body, first.parts, first.at, second.at),
-        shaped((2, blocks, rows, 2 * width)),
-        [VMEM_SPEC] * (4 * first.parts),
-        (*first.operands, *second.operands),
-        [pltpu.VMEM((2, blocks, rows, 2 * width), bf16)],
-        us=2.0,
-    )
-
-
-def last_body(parts, at_branch, meta, *refs):
-    own, other = refs[:parts], refs[parts : 2 * parts]
-    stem, factor, out, left, given, both, right, middle, wide, done, sems = refs[2 * parts :]
+        functools.partial(joined_body, first.parts, first.at, second.at, third.at),
+        (shaped((blocks, rows, 2 * width)), shaped((2, blocks, rows, width))),
+        [VMEM_SPEC] * (4 * first.parts) + [ANY_SPEC] * (2 * first.parts),
+        (*first.operands, *second.operands, *third.operands),
+        [
+            pltpu.VMEM((2, blocks, rows, 2 * width), bf16),
+            pltpu.VMEM((blocks, rows, 2 * width), bf16),
+            pltpu.SemaphoreType.DMA((1 + 2 * first.parts,)),
+        ],
+        [HBM_SPEC] * 2,
+        us=JOINED,
+    )
+
+
+def last_body(meta, planes, stem, factor, out, left, given, both, right, middle, wide, done, sems):
     _, blocks, rows, width = left.shape
     total = blocks * rows
     core = meta[0] & 1
     me = block_of(meta, blocks)
-    copies = [pltpu.make_async_copy(stem, given, sems.at[0]), pltpu.make_async_copy(factor, both, sems.at[1])]
-    for plane, refs_of in enumerate((own, other)):
-        at = 0
-        for ref in refs_of:
-            size = ref.shape[0]
-            copies.append(
-                pltpu.make_async_copy(
-                    ref.at[:, at_branch], left.at[plane, pl.ds(at, size)], sems.at[len(copies)]
-                )
-            )
-            at += size
+    copies = [
+        pltpu.make_async_copy(source, target, sems.at[at])
+        for at, (source, target) in enumerate(((stem, given), (factor, both.at[0]), (planes, left)))
+    ]
     for copy in copies:
         copy.start()
     copies[0].wait()
@@ -330,6 +353,9 @@
         here = slice(at * TILE, (at + 1) * TILE)
         middle[:, here] = (dot(mine, right[0, :, here]) + dot(theirs, right[1, :, here])).astype(bf16)
     copies[1].wait()
+    value = both[0]
+    both[1, :, :width] = -value[:, width:]
+    both[1, :, width:] = value[:, :width]
     for at in range(width // TILE):
         for part in range(2):
             here = slice(part * width + at * TILE, part * width + (at + 1) * TILE)
@@ -348,14 +374,14 @@
         copy.wait()
 
 
-def last_product(chain, branch, stem, factor, shape):
-    blocks, rows, width = branch.blocks, branch.rows, branch.width
+def last_product(chain, planes, stem, factor, shape):
+    _, blocks, rows, width = planes.shape
     count = stem.shape[0]
     return chain(
-        functools.partial(last_body, branch.parts, branch.at),
+        last_body,
         shaped(shape),
-        [ANY_SPEC] * (2 * branch.parts + 2),
-        (*branch.operands, stem, factor),
+        [HBM_SPEC, ANY_SPEC, HBM_SPEC],
+        (planes, stem, factor),
         [
             pltpu.VMEM((2, blocks, rows, width), bf16),
             pltpu.VMEM((count, 2 * width), bf16),
@@ -364,10 +390,10 @@
             pltpu.VMEM((blocks * rows, 2 * width), bf16),
             pltpu.VMEM((width // 128, 2 * blocks * rows, 128), f32),
             pltpu.VMEM((blocks, 2 * rows, width), bf16),
-            pltpu.SemaphoreType.DMA((2 + 2 * branch.parts + blocks,)),
+            pltpu.SemaphoreType.DMA((3 + blocks,)),
         ],
         [ANY_SPEC],
-        us=5.0,
+        us=LAST,
     )
 
 
@@ -376,15 +402,10 @@
 
 
 class Sum:
-    def __init__(self, chain, size):
+    def __init__(self, chain, size, keep, send):
         self.chain, self.size = chain, size
         self.levels = size.bit_length() - 1
-        self.keeps, self.recvs = [], []
-
-    def add(self, left, right, branch):
-        keep, send = leaf_partial(self.chain, left, right, branch)
-        self.keeps.append(keep)
-        self.recvs.append(self.swap(send, 0))
+        self.keep, self.recv = keep, self.swap(send, 0)
 
     def swap(self, x, shift):
         return swap_with(x, 1 << shift, self.size)
@@ -392,13 +413,13 @@
     def steps(self):
         levels, chain = self.levels, self.chain
         blocks = 1 << (levels - 2)
-        rows = self.keeps[0].shape[0] // (2 * blocks)
-        keep, send = halve(chain, self.keeps, self.recvs, 1)
+        rows = self.keep.shape[1] // (2 * blocks)
+        keep, send = halve(chain, self.keep, self.recv, 1)
         recv = self.swap(send, 1)
         yield
         if rows % 16:
             for shift in range(2, levels):
-                keep, send = halve(chain, list(keep), list(recv), shift)
+                keep, send = halve(chain, keep, recv, shift)
                 recv = self.swap(send, shift)
             total = finish(chain, keep, [recv])
             for shift in reversed(range(2, levels)):
@@ -429,28 +450,28 @@
 def on_device(size, stem_tensor, leaf_left, leaf_right, slice_bits):
     width = stem_tensor.shape[1]
     place = lax.axis_index("outer").astype(jnp.int32)
-    chain = Chain(jnp.concatenate([place[None], slice_bits.astype(jnp.int32)]))
+    chain = Calls(jnp.concatenate([place[None], slice_bits.astype(jnp.int32)]))
     given = exchange(stem_tensor[0])
-    early, late = Sum(chain, size), Sum(chain, size)
-    early.add(leaf_left, leaf_right, 0)
-    late.add(leaf_left, leaf_right, 2)
-    first = early.steps()
-    next(first)
-    late.add(leaf_left, leaf_right, 1)
-    late.add(leaf_left, leaf_right, 3)
-    second = late.steps()
-    next(second)
-    next(first)
+    groups = (0,), (2,), (1, 3)
+    sums = [Sum(chain, size, *parts) for parts in leaf_partials(chain, leaf_left, leaf_right, groups)]
+    p0, p1, q = (total.steps() for total in sums)
+    next(p0, None)
+    next(p1, None)
+    next(q, None)
     right = prepare(chain, given)
-    next(first, None)
-    next(second, None)
-    next(first, None)
-    next(second, None)
-    state = first_product(chain, early.result(0), right).reshape(width, 2 * width)
+    next(p0, None)
+    next(p1, None)
+    next(p0, None)
+    next(p1, None)
+    next(q, None)
+    next(p0, None)
+    next(p1, None)
+    next(q, None)
+    state = first_product(chain, sums[0].result(0), right).reshape(width, 2 * width)
     state = exchange(state)
-    next(second, None)
-    factor = joined_right(chain, late.result(1), late.result(2)).reshape(2, width, 2 * width)
-    return last_product(chain, late.result(0), state, factor, stem_tensor.shape)
+    next(q, None)
+    factor, planes = joined_right(chain, sums[2].result(0), sums[2].result(1), sums[1].result(0))
+    return last_product(chain, planes, state, factor.reshape(width, 2 * width), stem_tensor.shape)
 
 
 def solution(mesh):

time: 181 us -> 129 us (0.71)
  waiting for transfers between devices: 87.4 us -> 39.4 us
  local copies, waits for them, and re-layouts: 18.7 us -> 3.31 us
  starting transfers between devices: 38.2 us -> 52.9 us
  Pallas kernels: 35.4 us -> 31 us
    ppermute x24 -> x33, waiting for transfers between devices: 87.4 us -> 34.6 us  [swap_with(): return lax.ppermute(x, 'outer', [(i, i ^ mask) for i in range(size)])]
    ppermute x24 -> x33, starting transfers between devices: 23.1 us -> 39.2 us  [swap_with(): return lax.ppermute(x, 'outer', [(i, i ^ mask) for i in range(size)])]
    unnamed x18 -> x14, local copies, waits for them, and re-layouts: 18.7 us -> 3.31 us
    all_to_all x2, waiting for transfers between devices: 0.01 us -> 4.81 us  [exchange(): return lax.all_to_all(x, 'outer', split_axis=0, concat_axis=0, tiled=True)]
    pallas_call x16 -> x17, Pallas kernels: 35.4 us -> 31 us  [__call__(): pl.pallas_call(kernel, out_shape=shapes, in_specs=specs, out_specs=tuple(...]
  transfers between devices with their start and end apart: 26 -> 35, of which waited for: 13 -> 10; matrix products, arithmetic and copies ran while one was open for 0% -> 1% of each run, Pallas kernels for 14% -> 21%
where the time goes in v4:
time: 129 us; the launch traced here: 128 us
  starting transfers between devices  52.9 us (41%)
  waiting for transfers between devices  39.4 us (31%)
  Pallas kernels  31 us (24%)
  local copies, waits for them, and re-layouts  3.31 us (3%)
    ppermute x33, starting transfers between devices, swap_with(): return lax.ppermute(x, 'outer', [(i, i ^ mask) for i in range(size)])  39.2 us
    ppermute x33, waiting for transfers between devices, swap_with(): return lax.ppermute(x, 'outer', [(i, i ^ mask) for i in range(size)])  34.6 us
    pallas_call x17, Pallas kernels, __call__(): pl.pallas_call(kernel, out_shape=shapes, in_specs=specs, out_specs=tuple(...  31 us
    all_to_all x2, starting transfers between devices, exchange(): return lax.all_to_all(x, 'outer', split_axis=0, concat_axis=0, tiled=True)  13.7 us
    all_to_all x2, waiting for transfers between devices, exchange(): return lax.all_to_all(x, 'outer', split_axis=0, concat_axis=0, tiled=True)  4.81 us
    unnamed x14, local copies, waits for them, and re-layouts  3.31 us
  transfers between devices with their start and end apart: 35, of which 10 were waited for; matrix products, arithmetic and copies ran while one was open for 1% of the time, Pallas kernels for 21%

profile of v4, /device:TPU:11, one launch (start us, length us, event | category | flops | bytes accessed | tf_op | source)
XLA Modules:
  0.0 127.8 jit_solution(8991871123315972960)
XLA Ops:
  0.0 6.6 %all-to-all-start = ((bf16[512,2,512]{2,1,0:T(2,128)(2,1)}), bf16[512,2,512]{2,1,0:T(2,128)(2,1)S(1)}, u32[]{:S(2)}, u32[]{:S(2)}) async-start(bf16[512,2,512]{2,1,0:T(2,128)(2,1)} %bitcast.7), calls=%async_computation | async-start | bytes 2097152 | tf_op jit(solution)/shard_map/all_to_all | solution.py:401
  7.3 9.7 %shard_map.46 = (f32[1,512,512]{2,1,0:T(8,128)S(1)}, bf16[1,512,512]{2,1,0:T(8,128)(2,1)S(1)}, f32[1,512,512]{2,1,0:T(8,128)S(1)}, bf16[1,512,512]{2,1,0:T(8,128...) custom-call(s32[5]{0:T(128)S(1)} %pad_add_fusion.refs_0_, bf16[4,2,512,2,512]{4,3,2,1,0:T(2,128)(2,1)} %refs_1_.1, ...), custom_call_target="tpu_custom_call" | custom-call | flops 100000000 | bytes 1024 | tf_op jit(solution)/shard_map/pallas_call | solution.py:37
  18.0 2.5 %collective-permute-done.2.refs_2_ = bf16[1,512,512]{2,1,0:T(8,128)(2,1)S(1)} collective-permute-done((bf16[1,512,512]{2,1,0:T(8,128)(2,1)S(1)}, bf16[1,512,512]{2,1,0:T(8,128)(2,1)S(1)}, u32[]{:S(2)}, u32[]{:S(2)}) %collective-permute-start.2) | collective-permute-done | bytes 524320 | tf_op jit(solution)/shard_map/ppermute | solution.py:205
  26.7 4.8 %all-to-all-done.refs_1_ = bf16[512,2,512]{2,1,0:T(2,128)(2,1)S(1)} async-done(((bf16[512,2,512]{2,1,0:T(2,128)(2,1)}), bf16[512,2,512]{2,1,0:T(2,128)(2,1)S(1)}, u32[]{:S(2)}, u32[]{:S(2)}) %all-to-all-start) | async-done | bytes 1048608 | tf_op jit(solution)/shard_map/all_to_all | solution.py:401
  31.5 2.7 %shard_map.50.refs_3_.refs_5_ = bf16[2,512,1024]{2,1,0:T(8,128)(2,1)S(1)} custom-call(s32[5]{0:T(128)S(1)} %pad_add_fusion.refs_0_, bf16[512,2,512]{2,1,0:T(2,128)(2,1)S(1)} %all-to-all-done.refs_1_, f32[2,256,512]{2,1,0:T(8,128)S(1)} %get-tuple-element.39.refs_2_.refs_1_), custom_call_target="tpu_custom_call" | custom-call | flops 1000000000 | bytes 1024 | tf_op jit(solution)/shard_map/pallas_call | solution.py:37
  37.5 2.5 %collective-permute-start.9 = (bf16[1,64,512]{2,1,0:T(8,128)(2,1)S(1)}, bf16[1,64,512]{2,1,0:T(8,128)(2,1)S(1)}, u32[]{:S(2)}, u32[]{:S(2)}) collective-permute-start(bf16[1,64,512]{2,1,0:T(8,128)(2,1)S(1)} %get-tuple-element.48), channel_id=1, source_target_pairs={{0,8},{1,9},{2,10},{3,11},{4,12},{5,13},{6,14},{7,15},{8,0},{9,1},... | collective-permute-start | bytes 196616 | tf_op jit(solution)/shard_map/ppermute | solution.py:205
  40.6 2.2 %collective-permute-start.7 = (bf16[1,64,512]{2,1,0:T(8,128)(2,1)S(1)}, bf16[1,64,512]{2,1,0:T(8,128)(2,1)S(1)}, u32[]{:S(2)}, u32[]{:S(2)}) collective-permute-start(bf16[1,64,512]{2,1,0:T(8,128)(2,1)S(1)} %get-tuple-element.46), channel_id=1, source_target_pairs={{0,4},{1,5},{2,6},{3,7},{4,0},{5,1},{6,2},{7,3},{8,12},{9,13},{10,... | collective-permute-start | bytes 196616 | tf_op jit(solution)/shard_map/ppermute | solution.py:205
  43.3 1.7 %collective-permute-done.9.refs_2_ = bf16[1,64,512]{2,1,0:T(8,128)(2,1)S(1)} collective-permute-done((bf16[1,64,512]{2,1,0:T(8,128)(2,1)S(1)}, bf16[1,64,512]{2,1,0:T(8,128)(2,1)S(1)}, u32[]{:S(2)}, u32[]{:S(2)}) %collective-permute-start.9) | collective-permute-done | bytes 65568 | tf_op jit(solution)/shard_map/ppermute | solution.py:205
  45.6 3.2 %collective-permute-start.18 = (bf16[1,1,64,512]{3,2,1,0:T(8,128)(2,1)S(1)}, bf16[1,1,64,512]{3,2,1,0:T(8,128)(2,1)S(1)}, u32[]{:S(2)}, u32[]{:S(2)}) collective-permute-start(bf16[1,1,64,512]{3,2,1,0:T(8,128)(2,1)S(1)} %shard_map.53.refs_5_.refs_1_), channel_id=1, source_target_pairs={{0,8},{1,9},{2,10},{3,11},{4,12},{5,13},{6,14},{7,15},{8,0},{9,1},... | collective-permute-start | bytes 196616 | tf_op jit(solution)/shard_map/ppermute | solution.py:205
  48.8 1.5 %collective-permute-start.19 = (bf16[1,1,64,512]{3,2,1,0:T(8,128)(2,1)S(1)}, bf16[1,1,64,512]{3,2,1,0:T(8,128)(2,1)S(1)}, u32[]{:S(2)}, u32[]{:S(2)}) collective-permute-start(bf16[1,1,64,512]{3,2,1,0:T(8,128)(2,1)S(1)} %shard_map.53.refs_5_.refs_1_), channel_id=1, source_target_pairs={{0,4},{1,5},{2,6},{3,7},{4,0},{5,1},{6,2},{7,3},{8,12},{9,13},{10,... | collective-permute-start | bytes 196616 | tf_op jit(solution)/shard_map/ppermute | solution.py:205
  53.3 1.4 %collective-permute-start.16 = (bf16[1,1,64,512]{3,2,1,0:T(8,128)(2,1)S(1)}, bf16[1,1,64,512]{3,2,1,0:T(8,128)(2,1)S(1)}, u32[]{:S(2)}, u32[]{:S(2)}) collective-permute-start(bf16[1,1,64,512]{3,2,1,0:T(8,128)(2,1)S(1)} %shard_map.54.refs_3_.refs_1_), channel_id=1, source_target_pairs={{0,4},{1,5},{2,6},{3,7},{4,0},{5,1},{6,2},{7,3},{8,12},{9,13},{10,... | collective-permute-start | bytes 196616 | tf_op jit(solution)/shard_map/ppermute | solution.py:205
  59.9 1.6 %collective-permute-start.24 = (bf16[4,1,64,512]{3,2,1,0:T(8,128)(2,1)S(1)}, bf16[4,1,64,512]{3,2,1,0:T(8,128)(2,1)S(1)}, u32[]{:S(2)}, u32[]{:S(2)}) collective-permute-start(bf16[4,1,64,512]{3,2,1,0:T(8,128)(2,1)S(1)} %shard_map.56.refs_5_.refs_1_), channel_id=1, source_target_pairs={{0,2},{1,3},{2,0},{3,1},{4,6},{5,7},{6,4},{7,5},{8,10},{9,11},{10,... | collective-permute-start | bytes 786440 | tf_op jit(solution)/shard_map/ppermute | solution.py:205
  62.3 6.8 %collective-permute-start.25 = (bf16[4,1,64,512]{3,2,1,0:T(8,128)(2,1)S(1)}, bf16[4,1,64,512]{3,2,1,0:T(8,128)(2,1)S(1)}, u32[]{:S(2)}, u32[]{:S(2)}) collective-permute-start(bf16[4,1,64,512]{3,2,1,0:T(8,128)(2,1)S(1)} %shard_map.56.refs_5_.refs_1_), channel_id=1, source_target_pairs={{0,1},{1,0},{2,3},{3,2},{4,5},{5,4},{6,7},{7,6},{8,9},{9,8},{10,11... | collective-permute-start | bytes 786440 | tf_op jit(solution)/shard_map/ppermute | solution.py:205
  70.3 2.8 %collective-permute-done.14.refs_4_ = bf16[2,64,512]{2,1,0:T(8,128)(2,1)S(1)} collective-permute-done((bf16[2,64,512]{2,1,0:T(8,128)(2,1)S(1)}, bf16[2,64,512]{2,1,0:T(8,128)(2,1)S(1)}, u32[]{:S(2)}, u32[]{:S(2)}) %collective-permute-start.14) | collective-permute-done | bytes 131104 | tf_op jit(solution)/shard_map/ppermute | solution.py:205
  73.7 1.8 %collective-permute-start.21 = (bf16[1,2,64,512]{3,2,1,0:T(8,128)(2,1)S(1)}, bf16[1,2,64,512]{3,2,1,0:T(8,128)(2,1)S(1)}, u32[]{:S(2)}, u32[]{:S(2)}) collective-permute-start(bf16[1,2,64,512]{3,2,1,0:T(8,128)(2,1)S(1)} %shard_map.58.refs_6_.refs_1_), channel_id=1, source_target_pairs={{0,8},{1,9},{2,10},{3,11},{4,12},{5,13},{6,14},{7,15},{8,0},{9,1},... | collective-permute-start | bytes 393224 | tf_op jit(solution)/shard_map/ppermute | solution.py:205
  76.4 2.8 %shard_map.59.refs_5_ = bf16[8,64,1024]{2,1,0:T(8,128)(2,1)} custom-call(s32[5]{0:T(128)S(1)} %pad_add_fusion.refs_0_, bf16[4,1,64,512]{3,2,1,0:T(8,128)(2,1)S(1)} %shard_map.56.refs_5_.refs_1_, bf16[4,1,64,512]{3,2,1,0:T(8,128)(2,1)S(1)} %collective-permute-done.24.refs_2_, bf16[4,1,64,512]{3,2,1,0:T(8,128)(2,1)S(1)} %collective-permute-done.25.refs_3_, ...), custom_call_target="tpu_custom_call" | custom-call | flops 2800000000 | bytes 1024 | tf_op jit(solution)/shard_map/pallas_call | solution.py:37
  79.3 7.1 %all-to-all-start.1 = ((bf16[16,32,1024]{2,1,0:T(8,128)(2,1)}), bf16[16,32,1024]{2,1,0:T(8,128)(2,1)S(1)}, u32[]{:S(2)}, u32[]{:S(2)}) async-start(bf16[16,32,1024]{2,1,0:T(8,128)(2,1)} %bitcast.2), calls=%async_computation.1 | async-start | bytes 2097152 | tf_op jit(solution)/shard_map/all_to_all | solution.py:401
  87.6 1.4 %collective-permute-start.27 = (bf16[4,2,64,512]{3,2,1,0:T(8,128)(2,1)S(1)}, bf16[4,2,64,512]{3,2,1,0:T(8,128)(2,1)S(1)}, u32[]{:S(2)}, u32[]{:S(2)}) collective-permute-start(bf16[4,2,64,512]{3,2,1,0:T(8,128)(2,1)S(1)} %shard_map.60.refs_1_.refs_5_.refs_13_), channel_id=1, source_target_pairs={{0,2},{1,3},{2,0},{3,1},{4,6},{5,7},{6,4},{7,5},{8,10},{9,11},{10,... | collective-permute-start | bytes 1572872 | tf_op jit(solution)/shard_map/ppermute | solution.py:205
  89.2 1.6 %collective-permute-start.28 = (bf16[4,2,64,512]{3,2,1,0:T(8,128)(2,1)S(1)}, bf16[4,2,64,512]{3,2,1,0:T(8,128)(2,1)S(1)}, u32[]{:S(2)}, u32[]{:S(2)}) collective-permute-start(bf16[4,2,64,512]{3,2,1,0:T(8,128)(2,1)S(1)} %shard_map.60.refs_1_.refs_5_.refs_13_), channel_id=1, source_target_pairs={{0,1},{1,0},{2,3},{3,2},{4,5},{5,4},{6,7},{7,6},{8,9},{9,8},{10,11... | collective-permute-start | bytes 1572872 | tf_op jit(solution)/shard_map/ppermute | solution.py:205
  90.8 19.2 %collective-permute-done.27.refs_2_.refs_6_ = bf16[4,2,64,512]{3,2,1,0:T(8,128)(2,1)S(1)} collective-permute-done((bf16[4,2,64,512]{3,2,1,0:T(8,128)(2,1)S(1)}, bf16[4,2,64,512]{3,2,1,0:T(8,128)(2,1)S(1)}, u32[]{:S(2)}, u32[]{:S(2)}) %collective-permute-start.27) | collective-permute-done | bytes 524320 | tf_op jit(solution)/shard_map/ppermute | solution.py:205
  110.0 2.3 %collective-permute-start.29 = (bf16[4,2,64,512]{3,2,1,0:T(8,128)(2,1)S(1)}, bf16[4,2,64,512]{3,2,1,0:T(8,128)(2,1)S(1)}, u32[]{:S(2)}, u32[]{:S(2)}) collective-permute-start(bf16[4,2,64,512]{3,2,1,0:T(8,128)(2,1)S(1)} %collective-permute-done.27.refs_2_.refs_6_), channel_id=1, source_target_pairs={{0,1},{1,0},{2,3},{3,2},{4,5},{5,4},{6,7},{7,6},{8,9},{9,8},{10,11... | collective-permute-start | bytes 1572872 | tf_op jit(solution)/shard_map/ppermute | solution.py:205
  112.3 4.3 %collective-permute-done.30.refs_10_ = bf16[4,1,64,512]{3,2,1,0:T(8,128)(2,1)S(1)} collective-permute-done((bf16[4,1,64,512]{3,2,1,0:T(8,128)(2,1)S(1)}, bf16[4,1,64,512]{3,2,1,0:T(8,128)(2,1)S(1)}, u32[]{:S(2)}, u32[]{:S(2)}) %collective-permute-start.30) | collective-permute-done | bytes 262176 | tf_op jit(solution)/shard_map/ppermute | solution.py:205
  118.6 2.2 %shard_map.61 = (bf16[8,64,1024]{2,1,0:T(8,128)(2,1)S(1)}, bf16[2,8,64,512]{3,2,1,0:T(8,128)(2,1)S(1)}) custom-call(s32[5]{0:T(128)S(1)} %pad_add_fusion.refs_0_, bf16[4,2,64,512]{3,2,1,0:T(8,128)(2,1)S(1)} %shard_map.60.refs_1_.refs_5_.refs_13_, bf16[4,2,64,512]{3,2,1,0:T(8,128)(2,1)S(1)} %collective-permute-done.27.refs_2_.refs_6_, ...), custom_call_target="tpu_custom_call" | custom-call | flops 2000000000 | bytes 1024 | tf_op jit(solution)/shard_map/pallas_call | solution.py:37
  123.1 4.5 %shard_map.62 = bf16[1,512,2,512]{3,2,1,0:T(2,128)(2,1)} custom-call(s32[5]{0:T(128)S(1)} %pad_add_fusion.refs_0_, bf16[2,8,64,512]{3,2,1,0:T(8,128)(2,1)S(1)} %copy-done.2, bf16[512,1024]{1,0:T(8,128)(2,1)S(1)} %bitcast.5, bf16[512,1024]{1,0:T(8,128)(2,1)S(1)} %bitcast.6, bf16[8,64,1024]{2,1,0:T(8,128)(2,1)S(1)} %get-tuple-element.56.refs_4_), custom_call_target="tpu_custom_call" | custom-call | flops 5000000000 | bytes 1024 | tf_op jit(solution)/shard_map/pallas_call | solution.py:37
  (78 shorter events, 30.0 us)
Async XLA Ops:
  0.0 31.5 %all-to-all-start = ((bf16[512,2,512]{2,1,0:T(2,128)(2,1)}), bf16[512,2,512]{2,1,0:T(2,128)(2,1)S(1)}, u32[]{:S(2)}, u32[]{:S(2)}) async-start(bf16[512,2,512]{2,1,0:T(2,128)(2,1)} %bitcast.7), calls=%async_computation | async-start | bytes 2097152 | tf_op jit(solution)/shard_map/all_to_all | solution.py:401
  17.1 7.6 %collective-permute-start = (bf16[2,512,512]{2,1,0:T(8,128)(2,1)S(1)}, bf16[2,512,512]{2,1,0:T(8,128)(2,1)S(1)}, u32[]{:S(2)}, u32[]{:S(2)}) collective-permute-start(bf16[2,512,512]{2,1,0:T(8,128)(2,1)S(1)} %get-tuple-element.32), channel_id=1, source_target_pairs={{0,1},{1,0},{2,3},{3,2},{4,5},{5,4},{6,7},{7,6},{8,9},{9,8},{10,11... | collective-permute-start | bytes 3145736 | tf_op jit(solution)/shard_map/ppermute | solution.py:205
  21.9 12.3 %collective-permute-start.5 = (bf16[1,256,512]{2,1,0:T(8,128)(2,1)}, bf16[1,256,512]{2,1,0:T(8,128)(2,1)}, u32[]{:S(2)}, u32[]{:S(2)}) collective-permute-start(bf16[1,256,512]{2,1,0:T(8,128)(2,1)} %get-tuple-element.42), channel_id=1, source_target_pairs={{0,2},{1,3},{2,0},{3,1},{4,6},{5,7},{6,4},{7,5},{8,10},{9,11},{10,... | collective-permute-start | bytes 786440 | tf_op jit(solution)/shard_map/ppermute | solution.py:205
  24.4 15.6 %collective-permute-start.4 = (bf16[1,256,512]{2,1,0:T(8,128)(2,1)}, bf16[1,256,512]{2,1,0:T(8,128)(2,1)S(1)}, u32[]{:S(2)}, u32[]{:S(2)}) collective-permute-start(bf16[1,256,512]{2,1,0:T(8,128)(2,1)} %get-tuple-element.41), channel_id=1, source_target_pairs={{0,2},{1,3},{2,0},{3,1},{4,6},{5,7},{6,4},{7,5},{8,10},{9,11},{10,... | collective-permute-start | bytes 786440 | tf_op jit(solution)/shard_map/ppermute | solution.py:205
  25.4 27.9 %collective-permute-start.3 = (bf16[2,256,512]{2,1,0:T(8,128)(2,1)S(1)}, bf16[2,256,512]{2,1,0:T(8,128)(2,1)S(1)}, u32[]{:S(2)}, u32[]{:S(2)}) collective-permute-start(bf16[2,256,512]{2,1,0:T(8,128)(2,1)S(1)} %get-tuple-element.40), channel_id=1, source_target_pairs={{0,2},{1,3},{2,0},{3,1},{4,6},{5,7},{6,4},{7,5},{8,10},{9,11},{10,... | collective-permute-start | bytes 1572872 | tf_op jit(solution)/shard_map/ppermute | solution.py:205
  37.5 7.5 %collective-permute-start.9 = (bf16[1,64,512]{2,1,0:T(8,128)(2,1)S(1)}, bf16[1,64,512]{2,1,0:T(8,128)(2,1)S(1)}, u32[]{:S(2)}, u32[]{:S(2)}) collective-permute-start(bf16[1,64,512]{2,1,0:T(8,128)(2,1)S(1)} %get-tuple-element.48), channel_id=1, source_target_pairs={{0,8},{1,9},{2,10},{3,11},{4,12},{5,13},{6,14},{7,15},{8,0},{9,1},... | collective-permute-start | bytes 196616 | tf_op jit(solution)/shard_map/ppermute | solution.py:205
  40.6 8.2 %collective-permute-start.6 = (bf16[1,64,512]{2,1,0:T(8,128)(2,1)S(1)}, bf16[1,64,512]{2,1,0:T(8,128)(2,1)S(1)}, u32[]{:S(2)}, u32[]{:S(2)}) collective-permute-start(bf16[1,64,512]{2,1,0:T(8,128)(2,1)S(1)} %get-tuple-element.45), channel_id=1, source_target_pairs={{0,8},{1,9},{2,10},{3,11},{4,12},{5,13},{6,14},{7,15},{8,0},{9,1},... | collective-permute-start | bytes 196616 | tf_op jit(solution)/shard_map/ppermute | solution.py:205
  40.6 9.6 %collective-permute-start.7 = (bf16[1,64,512]{2,1,0:T(8,128)(2,1)S(1)}, bf16[1,64,512]{2,1,0:T(8,128)(2,1)S(1)}, u32[]{:S(2)}, u32[]{:S(2)}) collective-permute-start(bf16[1,64,512]{2,1,0:T(8,128)(2,1)S(1)} %get-tuple-element.46), channel_id=1, source_target_pairs={{0,4},{1,5},{2,6},{3,7},{4,0},{5,1},{6,2},{7,3},{8,12},{9,13},{10,... | collective-permute-start | bytes 196616 | tf_op jit(solution)/shard_map/ppermute | solution.py:205
  42.8 9.8 %collective-permute-start.8 = (bf16[1,64,512]{2,1,0:T(8,128)(2,1)S(1)}, bf16[1,64,512]{2,1,0:T(8,128)(2,1)S(1)}, u32[]{:S(2)}, u32[]{:S(2)}) collective-permute-start(bf16[1,64,512]{2,1,0:T(8,128)(2,1)S(1)} %get-tuple-element.47), channel_id=1, source_target_pairs={{0,12},{1,13},{2,14},{3,15},{4,8},{5,9},{6,10},{7,11},{8,4},{9,5},... | collective-permute-start | bytes 196616 | tf_op jit(solution)/shard_map/ppermute | solution.py:205
  45.6 9.7 %collective-permute-start.18 = (bf16[1,1,64,512]{3,2,1,0:T(8,128)(2,1)S(1)}, bf16[1,1,64,512]{3,2,1,0:T(8,128)(2,1)S(1)}, u32[]{:S(2)}, u32[]{:S(2)}) collective-permute-start(bf16[1,1,64,512]{3,2,1,0:T(8,128)(2,1)S(1)} %shard_map.53.refs_5_.refs_1_), channel_id=1, source_target_pairs={{0,8},{1,9},{2,10},{3,11},{4,12},{5,13},{6,14},{7,15},{8,0},{9,1},... | collective-permute-start | bytes 196616 | tf_op jit(solution)/shard_map/ppermute | solution.py:205
  48.8 7.9 %collective-permute-start.19 = (bf16[1,1,64,512]{3,2,1,0:T(8,128)(2,1)S(1)}, bf16[1,1,64,512]{3,2,1,0:T(8,128)(2,1)S(1)}, u32[]{:S(2)}, u32[]{:S(2)}) collective-permute-start(bf16[1,1,64,512]{3,2,1,0:T(8,128)(2,1)S(1)} %shard_map.53.refs_5_.refs_1_), channel_id=1, source_target_pairs={{0,4},{1,5},{2,6},{3,7},{4,0},{5,1},{6,2},{7,3},{8,12},{9,13},{10,... | collective-permute-start | bytes 196616 | tf_op jit(solution)/shard_map/ppermute | solution.py:205
  56.6 13.7 %collective-permute-start.12 = (bf16[2,64,512]{2,1,0:T(8,128)(2,1)S(1)}, bf16[2,64,512]{2,1,0:T(8,128)(2,1)S(1)}, u32[]{:S(2)}, u32[]{:S(2)}) collective-permute-start(bf16[2,64,512]{2,1,0:T(8,128)(2,1)S(1)} %get-tuple-element.52), channel_id=1, source_target_pairs={{0,8},{1,9},{2,10},{3,11},{4,12},{5,13},{6,14},{7,15},{8,0},{9,1},... | collective-permute-start | bytes 393224 | tf_op jit(solution)/shard_map/ppermute | solution.py:205
  57.6 12.7 %collective-permute-start.13 = (bf16[2,64,512]{2,1,0:T(8,128)(2,1)S(1)}, bf16[2,64,512]{2,1,0:T(8,128)(2,1)S(1)}, u32[]{:S(2)}, u32[]{:S(2)}) collective-permute-start(bf16[2,64,512]{2,1,0:T(8,128)(2,1)S(1)} %get-tuple-element.53), channel_id=1, source_target_pairs={{0,4},{1,5},{2,6},{3,7},{4,0},{5,1},{6,2},{7,3},{8,12},{9,13},{10,... | collective-permute-start | bytes 393224 | tf_op jit(solution)/shard_map/ppermute | solution.py:205
  58.6 14.5 %collective-permute-start.14 = (bf16[2,64,512]{2,1,0:T(8,128)(2,1)S(1)}, bf16[2,64,512]{2,1,0:T(8,128)(2,1)S(1)}, u32[]{:S(2)}, u32[]{:S(2)}) collective-permute-start(bf16[2,64,512]{2,1,0:T(8,128)(2,1)S(1)} %get-tuple-element.54), channel_id=1, source_target_pairs={{0,12},{1,13},{2,14},{3,15},{4,8},{5,9},{6,10},{7,11},{8,4},{9,5},... | collective-permute-start | bytes 393224 | tf_op jit(solution)/shard_map/ppermute | solution.py:205
  59.9 9.7 %collective-permute-start.24 = (bf16[4,1,64,512]{3,2,1,0:T(8,128)(2,1)S(1)}, bf16[4,1,64,512]{3,2,1,0:T(8,128)(2,1)S(1)}, u32[]{:S(2)}, u32[]{:S(2)}) collective-permute-start(bf16[4,1,64,512]{3,2,1,0:T(8,128)(2,1)S(1)} %shard_map.56.refs_5_.refs_1_), channel_id=1, source_target_pairs={{0,2},{1,3},{2,0},{3,1},{4,6},{5,7},{6,4},{7,5},{8,10},{9,11},{10,... | collective-permute-start | bytes 786440 | tf_op jit(solution)/shard_map/ppermute | solution.py:205
  62.3 14.2 %collective-permute-start.25 = (bf16[4,1,64,512]{3,2,1,0:T(8,128)(2,1)S(1)}, bf16[4,1,64,512]{3,2,1,0:T(8,128)(2,1)S(1)}, u32[]{:S(2)}, u32[]{:S(2)}) collective-permute-start(bf16[4,1,64,512]{3,2,1,0:T(8,128)(2,1)S(1)} %shard_map.56.refs_5_.refs_1_), channel_id=1, source_target_pairs={{0,1},{1,0},{2,3},{3,2},{4,5},{5,4},{6,7},{7,6},{8,9},{9,8},{10,11... | collective-permute-start | bytes 786440 | tf_op jit(solution)/shard_map/ppermute | solution.py:205
  73.7 12.7 %collective-permute-start.21 = (bf16[1,2,64,512]{3,2,1,0:T(8,128)(2,1)S(1)}, bf16[1,2,64,512]{3,2,1,0:T(8,128)(2,1)S(1)}, u32[]{:S(2)}, u32[]{:S(2)}) collective-permute-start(bf16[1,2,64,512]{3,2,1,0:T(8,128)(2,1)S(1)} %shard_map.58.refs_6_.refs_1_), channel_id=1, source_target_pairs={{0,8},{1,9},{2,10},{3,11},{4,12},{5,13},{6,14},{7,15},{8,0},{9,1},... | collective-permute-start | bytes 393224 | tf_op jit(solution)/shard_map/ppermute | solution.py:205
  75.5 10.8 %collective-permute-start.22 = (bf16[1,2,64,512]{3,2,1,0:T(8,128)(2,1)S(1)}, bf16[1,2,64,512]{3,2,1,0:T(8,128)(2,1)S(1)}, u32[]{:S(2)}, u32[]{:S(2)}) collective-permute-start(bf16[1,2,64,512]{3,2,1,0:T(8,128)(2,1)S(1)} %shard_map.58.refs_6_.refs_1_), channel_id=1, source_target_pairs={{0,4},{1,5},{2,6},{3,7},{4,0},{5,1},{6,2},{7,3},{8,12},{9,13},{10,... | collective-permute-start | bytes 393224 | tf_op jit(solution)/shard_map/ppermute | solution.py:205
  75.6 11.5 %collective-permute-start.23 = (bf16[1,2,64,512]{3,2,1,0:T(8,128)(2,1)S(1)}, bf16[1,2,64,512]{3,2,1,0:T(8,128)(2,1)S(1)}, u32[]{:S(2)}, u32[]{:S(2)}) collective-permute-start(bf16[1,2,64,512]{3,2,1,0:T(8,128)(2,1)S(1)} %shard_map.58.refs_6_.refs_1_), channel_id=1, source_target_pairs={{0,12},{1,13},{2,14},{3,15},{4,8},{5,9},{6,10},{7,11},{8,4},{9,5},... | collective-permute-start | bytes 393224 | tf_op jit(solution)/shard_map/ppermute | solution.py:205
  79.3 42.6 %all-to-all-start.1 = ((bf16[16,32,1024]{2,1,0:T(8,128)(2,1)}), bf16[16,32,1024]{2,1,0:T(8,128)(2,1)S(1)}, u32[]{:S(2)}, u32[]{:S(2)}) async-start(bf16[16,32,1024]{2,1,0:T(8,128)(2,1)} %bitcast.2), calls=%async_computation.1 | async-start | bytes 2097152 | tf_op jit(solution)/shard_map/all_to_all | solution.py:401
  87.6 22.4 %collective-permute-start.27 = (bf16[4,2,64,512]{3,2,1,0:T(8,128)(2,1)S(1)}, bf16[4,2,64,512]{3,2,1,0:T(8,128)(2,1)S(1)}, u32[]{:S(2)}, u32[]{:S(2)}) collective-permute-start(bf16[4,2,64,512]{3,2,1,0:T(8,128)(2,1)S(1)} %shard_map.60.refs_1_.refs_5_.refs_13_), channel_id=1, source_target_pairs={{0,2},{1,3},{2,0},{3,1},{4,6},{5,7},{6,4},{7,5},{8,10},{9,11},{10,... | collective-permute-start | bytes 1572872 | tf_op jit(solution)/shard_map/ppermute | solution.py:205
  89.1 27.5 %collective-permute-start.30 = (bf16[4,1,64,512]{3,2,1,0:T(8,128)(2,1)S(1)}, bf16[4,1,64,512]{3,2,1,0:T(8,128)(2,1)S(1)}, u32[]{:S(2)}, u32[]{:S(2)}) collective-permute-start(bf16[4,1,64,512]{3,2,1,0:T(8,128)(2,1)S(1)} %shard_map.57.refs_5_.refs_9_), channel_id=1, source_target_pairs={{0,2},{1,3},{2,0},{3,1},{4,6},{5,7},{6,4},{7,5},{8,10},{9,11},{10,... | collective-permute-start | bytes 786440 | tf_op jit(solution)/shard_map/ppermute | solution.py:205
  89.2 29.5 %collective-permute-start.28 = (bf16[4,2,64,512]{3,2,1,0:T(8,128)(2,1)S(1)}, bf16[4,2,64,512]{3,2,1,0:T(8,128)(2,1)S(1)}, u32[]{:S(2)}, u32[]{:S(2)}) collective-permute-start(bf16[4,2,64,512]{3,2,1,0:T(8,128)(2,1)S(1)} %shard_map.60.refs_1_.refs_5_.refs_13_), channel_id=1, source_target_pairs={{0,1},{1,0},{2,3},{3,2},{4,5},{5,4},{6,7},{7,6},{8,9},{9,8},{10,11... | collective-permute-start | bytes 1572872 | tf_op jit(solution)/shard_map/ppermute | solution.py:205
  110.0 8.6 %collective-permute-start.29 = (bf16[4,2,64,512]{3,2,1,0:T(8,128)(2,1)S(1)}, bf16[4,2,64,512]{3,2,1,0:T(8,128)(2,1)S(1)}, u32[]{:S(2)}, u32[]{:S(2)}) collective-permute-start(bf16[4,2,64,512]{3,2,1,0:T(8,128)(2,1)S(1)} %collective-permute-done.27.refs_2_.refs_6_), channel_id=1, source_target_pairs={{0,1},{1,0},{2,3},{3,2},{4,5},{5,4},{6,7},{7,6},{8,9},{9,8},{10,11... | collective-permute-start | bytes 1572872 | tf_op jit(solution)/shard_map/ppermute | solution.py:205
  (18 other events, 80.7 us)

commit v5 on v4

--- a/solution.py
+++ b/solution.py
@@ -9,8 +9,11 @@
 
 VMEM_LIMIT = 24 << 20
 LEAF_LIMIT = 48 << 20
-LEAF, HALVE, SPREAD, FINISH, JOIN = 0.1, 2.0, 10.0, 10.0, 10.0
-PREPARE, FIRST, JOINED, LAST = 1.0, 2.8, 2.0, 5.0
+DIRECT = True, True, True
+LEAVES = 0.1, 10.0
+STEPS = (1.0, 20.0, 20.0, 10.0), (2.0, 3.0, 20.0, 20.0), (3.0, 5.0, 10.0, 20.0)
+PREPARE, FIRST, JOINED, LAST = 5.0, 0.1, 2.0, 5.0
+RIGHT = 2.0
 TILE = 256
 bf16, f32 = jnp.bfloat16, jnp.float32
 
@@ -104,7 +107,7 @@
             at += 1
 
 
-def leaf_partials(chain, left, right, groups):
+def leaf_partials(chain, left, right, groups, us):
     depth, width = left.shape[2], left.shape[4]
     count = sum(len(group) for group in groups)
     shapes = [shaped((len(group), width, width), dtype) for group in groups for dtype in (f32, bf16)]
@@ -119,7 +122,7 @@
             pltpu.VMEM((2, 2 * depth, 2 * width), bf16),
             pltpu.SemaphoreType.DMA((count, 2)),
         ],
-        us=LEAF,
+        us=us,
         limit=LEAF_LIMIT,
     )
     return list(zip(outs[0::2], outs[1::2], strict=True))
@@ -134,7 +137,7 @@
     keep_out[...] = keep[:, mine] + recv[:, mine].astype(f32)
 
 
-def halve(chain, keep, recv, shift):
+def halve(chain, keep, recv, shift, us):
     count, rows, width = keep.shape
     half = rows // 2
     if half % 16:
@@ -146,7 +149,7 @@
         (shaped((count, half, width), f32), shaped((count, half, width))),
         [VMEM_SPEC] * 2,
         (keep, recv),
-        us=HALVE,
+        us=us,
     )
 
 
@@ -163,14 +166,14 @@
             keep_out[...] = value
 
 
-def spread(chain, keep, recv, shift, blocks):
+def spread(chain, keep, recv, shift, blocks, us):
     count, rows, width = keep.shape[0], keep.shape[1] // blocks, keep.shape[2]
     return chain(
         functools.partial(spread_body, shift),
         (shaped((count, rows, width), f32),) + (shaped((count, rows, width)),) * (blocks - 1),
         [VMEM_SPEC] * 2,
         (keep, recv),
-        us=SPREAD,
+        us=us,
     )
 
 
@@ -181,10 +184,10 @@
     rest[-1][0] = total.astype(bf16)
 
 
-def finish(chain, keep, recvs):
+def finish(chain, keep, recvs, us):
     if keep.shape[1] % 16:
         return (keep + sum(recv.astype(f32) for recv in recvs)).astype(bf16)[None]
-    return chain(finish_body, shaped((1, *keep.shape)), [VMEM_SPEC] * (1 + len(recvs)), (keep, *recvs), us=FINISH)
+    return chain(finish_body, shaped((1, *keep.shape)), [VMEM_SPEC] * (1 + len(recvs)), (keep, *recvs), us=us)
 
 
 def join_body(meta, *refs):
@@ -194,11 +197,11 @@
         at += ref.shape[0]
 
 
-def join(chain, parts):
+def join(chain, parts, us):
     blocks, shape = sum(part.shape[0] for part in parts), parts[0].shape[1:]
     if shape[1] % 16:
         return jnp.concatenate(parts, axis=0)
-    return chain(join_body, shaped((blocks, *shape)), [VMEM_SPEC] * len(parts), parts, us=JOIN)
+    return chain(join_body, shaped((blocks, *shape)), [VMEM_SPEC] * len(parts), parts, us=us)
 
 
 def swap_with(x, mask, size):
@@ -250,10 +253,10 @@
     own, other, (right, out) = refs[:parts], refs[parts : 2 * parts], refs[2 * parts :]
     blocks, rows, columns = out.shape
     me = block_of(meta, blocks)
-    mine, theirs = rows_of(own, at_branch), rows_of(other, at_branch)
+    left = jnp.concatenate([rows_of(own, at_branch), rows_of(other, at_branch)], axis=1)
     for at in range(columns // TILE):
         here = slice(at * TILE, (at + 1) * TILE)
-        value = dot(mine, right[0, :, here]) + dot(theirs, right[1, :, here])
+        value = dot(left, right[:, :, here].reshape(columns, TILE))
         value = value.astype(bf16).reshape(blocks, rows, TILE)
         for t in range(blocks):
             out[me ^ t, :, here] = value[t]
@@ -269,19 +272,9 @@
     )
 
 
-def joined_body(parts, at0, at1, at2, meta, *refs):
-    own0, other0, own1, other1, own2, other2 = (refs[at * parts : (at + 1) * parts] for at in range(6))
-    result, moved, right, out, sems = refs[-5:]
-    copies = []
-    for plane, refs_of in enumerate((own2, other2)):
-        at = 0
-        for ref in refs_of:
-            size = ref.shape[0]
-            copies.append(
-                pltpu.make_async_copy(ref.at[:, at2], moved.at[plane, pl.ds(at, size)], sems.at[len(copies)])
-            )
-            copies[-1].start()
-            at += size
+def joined_body(parts, at0, at1, meta, *refs):
+    own0, other0, own1, other1 = (refs[at * parts : (at + 1) * parts] for at in range(4))
+    out, right = refs[4 * parts :]
     blocks, rows, columns = out.shape
     width = columns // 2
     me = block_of(meta, blocks)
@@ -297,100 +290,93 @@
             right[1 - core, me ^ t, :, :width] = -imag
             right[1 - core, me ^ t, :, width:] = real
             t += 1
-    mine, theirs = rows_of(own0, at0), rows_of(other0, at0)
+    left = jnp.concatenate([rows_of(own0, at0), rows_of(other0, at0)], axis=1)
     for at in range(columns // TILE):
         here = slice(at * TILE, (at + 1) * TILE)
-        first = right[0, :, :, here].reshape(blocks * rows, TILE)
-        second = right[1, :, :, here].reshape(blocks * rows, TILE)
-        value = dot(mine, first) + dot(theirs, second)
+        value = dot(left, right[:, :, :, here].reshape(columns, TILE))
         value = value.astype(bf16).reshape(blocks, rows, TILE)
         for t in range(blocks):
             out[me ^ t, :, here] = value[t]
-    copies.append(pltpu.make_async_copy(out, result, sems.at[len(copies)]))
-    copies[-1].start()
-    for copy in copies:
-        copy.wait()
-
-
-def joined_right(chain, first, second, third):
+
+
+def joined_right(chain, first, second):
     blocks, rows, width = first.blocks, first.rows, first.width
     return chain(
-        functools.partial(joined_body, first.parts, first.at, second.at, third.at),
-        (shaped((blocks, rows, 2 * width)), shaped((2, blocks, rows, width))),
-        [VMEM_SPEC] * (4 * first.parts) + [ANY_SPEC] * (2 * first.parts),
-        (*first.operands, *second.operands, *third.operands),
-        [
-            pltpu.VMEM((2, blocks, rows, 2 * width), bf16),
-            pltpu.VMEM((blocks, rows, 2 * width), bf16),
-            pltpu.SemaphoreType.DMA((1 + 2 * first.parts,)),
-        ],
-        [HBM_SPEC] * 2,
+        functools.partial(joined_body, first.parts, first.at, second.at),
+        shaped((blocks, rows, 2 * width)),
+        [VMEM_SPEC] * (4 * first.parts),
+        (*first.operands, *second.operands),
+        [pltpu.VMEM((2, blocks, rows, 2 * width), bf16)],
         us=JOINED,
     )
 
 
-def last_body(meta, planes, stem, factor, out, left, given, both, right, middle, wide, done, sems):
-    _, blocks, rows, width = left.shape
+def right_body(meta, stem, factor, out, both):
+    count, columns = stem.shape
+    width = columns // 2
+    core = meta[0] & 1
+    value = factor[...]
+    both[:width] = value
+    both[width:, :width] = -value[:, width:]
+    both[width:, width:] = value[:, :width]
+    left = stem[...]
+    for at in range(columns // TILE):
+        here = slice(at * TILE, (at + 1) * TILE)
+        there = slice((at * TILE + width) % columns, (at * TILE + width) % columns + TILE)
+        value = dot(left, both[:, here])
+        turned = value if at * TILE < width else -value
+        out[core, :, here] = value.astype(bf16)
+        out[1 - core, :, there] = turned.astype(bf16)
+
+
+def right_product(chain, stem, factor):
+    count, columns = stem.shape
+    return chain(
+        right_body,
+        shaped((2, count, columns)),
+        [VMEM_SPEC] * 2,
+        (stem, factor),
+        [pltpu.VMEM((columns, columns), bf16)],
+        us=RIGHT,
+    )
+
+
+def last_body(parts, at_branch, meta, *refs):
+    own, other = refs[:parts], refs[parts : 2 * parts]
+    right, out, wide, done, sems = refs[2 * parts :]
+    blocks, rows, width = done.shape[0], done.shape[1] // 2, done.shape[2]
     total = blocks * rows
-    core = meta[0] & 1
     me = block_of(meta, blocks)
-    copies = [
-        pltpu.make_async_copy(source, target, sems.at[at])
-        for at, (source, target) in enumerate(((stem, given), (factor, both.at[0]), (planes, left)))
-    ]
-    for copy in copies:
-        copy.start()
-    copies[0].wait()
-    value = given[...]
-    right[core] = value
-    right[1 - core, :, :width] = -value[:, width:]
-    right[1 - core, :, width:] = value[:, :width]
-    for copy in copies[2:]:
-        copy.wait()
-    mine = left[0].reshape(total, width)
-    theirs = left[1].reshape(total, width)
-    for at in range(2 * width // TILE):
-        here = slice(at * TILE, (at + 1) * TILE)
-        middle[:, here] = (dot(mine, right[0, :, here]) + dot(theirs, right[1, :, here])).astype(bf16)
-    copies[1].wait()
-    value = both[0]
-    both[1, :, :width] = -value[:, width:]
-    both[1, :, width:] = value[:, :width]
+    left = jnp.concatenate([rows_of(own, at_branch), rows_of(other, at_branch)], axis=1)
+    target = out.reshape(blocks, 2 * rows, width)
     for at in range(width // TILE):
         for part in range(2):
             here = slice(part * width + at * TILE, part * width + (at + 1) * TILE)
-            value = dot(middle[:, :width], both[0, :, here]) + dot(middle[:, width:], both[1, :, here])
+            value = dot(left, right[:, :, here].reshape(2 * right.shape[1], TILE))
             for sub in range(TILE // 128):
                 wide[at * (TILE // 128) + sub, pl.ds(part, total, stride=2), :] = value[:, sub * 128 : (sub + 1) * 128]
-    target = out.reshape(blocks, 2 * rows, width)
     writes = []
     for t in range(blocks):
         for at in range(width // 128):
             piece = wide[at, 2 * rows * t : 2 * rows * (t + 1), :]
             done[t, :, at * 128 : (at + 1) * 128] = piece.astype(bf16)
-        writes.append(pltpu.make_async_copy(done.at[t], target.at[me ^ t], sems.at[len(copies) + t]))
+        writes.append(pltpu.make_async_copy(done.at[t], target.at[me ^ t], sems.at[t]))
         writes[-1].start()
     for copy in writes:
         copy.wait()
 
 
-def last_product(chain, planes, stem, factor, shape):
-    _, blocks, rows, width = planes.shape
-    count = stem.shape[0]
-    return chain(
-        last_body,
+def last_product(chain, branch, right, shape):
+    blocks, rows, width = branch.blocks, branch.rows, branch.width
+    return chain(
+        functools.partial(last_body, branch.parts, branch.at),
         shaped(shape),
-        [HBM_SPEC, ANY_SPEC, HBM_SPEC],
-        (planes, stem, factor),
+        [VMEM_SPEC] * (2 * branch.parts + 1),
+        (*branch.operands, right),
         [
-            pltpu.VMEM((2, blocks, rows, width), bf16),
-            pltpu.VMEM((count, 2 * width), bf16),
-            pltpu.VMEM((2, width, 2 * width), bf16),
-            pltpu.VMEM((2, count, 2 * width), bf16),
-            pltpu.VMEM((blocks * rows, 2 * width), bf16),
             pltpu.VMEM((width // 128, 2 * blocks * rows, 128), f32),
             pltpu.VMEM((blocks, 2 * rows, width), bf16),
-            pltpu.SemaphoreType.DMA((3 + blocks,)),
+            pltpu.SemaphoreType.DMA((blocks,)),
         ],
         [ANY_SPEC],
         us=LAST,
@@ -402,8 +388,8 @@
 
 
 class Sum:
-    def __init__(self, chain, size, keep, send):
-        self.chain, self.size = chain, size
+    def __init__(self, chain, size, times, direct, keep, send):
+        self.chain, self.size, self.times, self.direct = chain, size, times, direct
         self.levels = size.bit_length() - 1
         self.keep, self.recv = keep, self.swap(send, 0)
 
@@ -412,27 +398,31 @@
 
     def steps(self):
         levels, chain = self.levels, self.chain
+        halve_us, spread_us, finish_us, join_us = self.times
         blocks = 1 << (levels - 2)
         rows = self.keep.shape[1] // (2 * blocks)
-        keep, send = halve(chain, self.keep, self.recv, 1)
+        keep, send = halve(chain, self.keep, self.recv, 1, halve_us)
         recv = self.swap(send, 1)
         yield
-        if rows % 16:
+        if rows % 16 or not self.direct:
             for shift in range(2, levels):
-                keep, send = halve(chain, keep, recv, shift)
+                keep, send = halve(chain, keep, recv, shift, spread_us)
                 recv = self.swap(send, shift)
-            total = finish(chain, keep, [recv])
+                yield
+            total = finish(chain, keep, [recv], finish_us)
             for shift in reversed(range(2, levels)):
-                total = join(chain, (total, self.swap(total, shift)))
+                recv = self.swap(total, shift)
+                yield
+                total = join(chain, (total, recv), join_us)
         else:
             masks = [reversed_bits(t, levels - 2) << 2 for t in range(1, blocks)]
-            keep, *sends = spread(chain, keep, recv, 2, blocks)
+            keep, *sends = spread(chain, keep, recv, 2, blocks, spread_us)
             recvs = [swap_with(x, mask, self.size) for x, mask in zip(sends, masks, strict=True)]
             yield
-            total = finish(chain, keep, recvs)
+            total = finish(chain, keep, recvs, finish_us)
             recvs = [swap_with(total, mask, self.size) for mask in masks]
             yield
-            total = join(chain, (total, *recvs))
+            total = join(chain, (total, *recvs), join_us)
         across = self.swap(total, 1)
         self.own, self.other = (total, across), (self.swap(total, 0), self.swap(across, 0))
         if rows % 16:
@@ -452,26 +442,40 @@
     place = lax.axis_index("outer").astype(jnp.int32)
     chain = Calls(jnp.concatenate([place[None], slice_bits.astype(jnp.int32)]))
     given = exchange(stem_tensor[0])
-    groups = (0,), (2,), (1, 3)
-    sums = [Sum(chain, size, *parts) for parts in leaf_partials(chain, leaf_left, leaf_right, groups)]
-    p0, p1, q = (total.steps() for total in sums)
-    next(p0, None)
-    next(p1, None)
-    next(q, None)
+    early, late = ((0,),), ((1, 3), (2,))
+    sums = [
+        Sum(chain, size, times, direct, *parts)
+        for times, direct, parts in zip(STEPS, DIRECT, leaf_partials(chain, leaf_left, leaf_right, early, LEAVES[0]))
+    ]
+    a = sums[0].steps()
+    next(a, None)
+    sums += [
+        Sum(chain, size, times, direct, *parts)
+        for times, direct, parts in zip(STEPS[1:], DIRECT[1:], leaf_partials(chain, leaf_left, leaf_right, late, LEAVES[1]))
+    ]
+    b, c = (total.steps() for total in sums[1:])
+    next(a, None)
+    next(b, None)
     right = prepare(chain, given)
-    next(p0, None)
-    next(p1, None)
-    next(p0, None)
-    next(p1, None)
-    next(q, None)
-    next(p0, None)
-    next(p1, None)
-    next(q, None)
+    next(a, None)
+    next(b, None)
+    next(c, None)
+    next(a, None)
+    next(b, None)
+    next(c, None)
+    next(c, None)
+    for _ in a:
+        pass
     state = first_product(chain, sums[0].result(0), right).reshape(width, 2 * width)
     state = exchange(state)
-    next(q, None)
-    factor, planes = joined_right(chain, sums[2].result(0), sums[2].result(1), sums[1].result(0))
-    return last_product(chain, planes, state, factor.reshape(width, 2 * width), stem_tensor.shape)
+    next(b, None)
+    next(c, None)
+    for steps in (b, c):
+        for _ in steps:
+            pass
+    factor = joined_right(chain, sums[1].result(0), sums[1].result(1)).reshape(width, 2 * width)
+    right = right_product(chain, state, factor)
+    return last_product(chain, sums[2].result(0), right, stem_tensor.shape)
 
 
 def solution(mesh):

time: 129 us -> 126 us (0.977)
  starting transfers between devices: 52.9 us -> 48.8 us
  local copies, waits for them, and re-layouts: 3.31 us -> 5.42 us
    all_to_all x2, starting transfers between devices: 13.7 us -> 10.2 us  [exchange(): return lax.all_to_all(x, 'outer', split_axis=0, concat_axis=0, tiled=True)]
    unnamed x14 -> x18, local copies, waits for them, and re-layouts: 3.31 us -> 5.42 us
    pallas_call x17 -> x19, Pallas kernels: 31 us -> 30.6 us  [__call__(): pl.pallas_call(kernel, out_shape=shapes, in_specs=specs, out_specs=tuple(...]
  transfers between devices with their start and end apart: 35 -> 35, of which waited for: 10 -> 11; matrix products, arithmetic and copies ran while one was open for 1% -> 0% of each run, Pallas kernels for 21% -> 18%
where the time goes in v5:
time: 126 us
  starting transfers between devices  48.8 us (39%)
  waiting for transfers between devices  39.7 us (32%)
  Pallas kernels  30.6 us (24%)
  local copies, waits for them, and re-layouts  5.42 us (4%)
    ppermute x33, starting transfers between devices, swap_with(): return lax.ppermute(x, 'outer', [(i, i ^ mask) for i in range(size)])  38.5 us
    ppermute x33, waiting for transfers between devices, swap_with(): return lax.ppermute(x, 'outer', [(i, i ^ mask) for i in range(size)])  34 us
    pallas_call x19, Pallas kernels, __call__(): pl.pallas_call(kernel, out_shape=shapes, in_specs=specs, out_specs=tuple(...  30.6 us
    all_to_all x2, starting transfers between devices, exchange(): return lax.all_to_all(x, 'outer', split_axis=0, concat_axis=0, tiled=True)  10.2 us
    all_to_all x2, waiting for transfers between devices, exchange(): return lax.all_to_all(x, 'outer', split_axis=0, concat_axis=0, tiled=True)  5.71 us
    unnamed x18, local copies, waits for them, and re-layouts  5.42 us
  transfers between devices with their start and end apart: 35, of which 11 were waited for; matrix products, arithmetic and copies ran while one was open for 0% of the time, Pallas kernels for 18%

profile of v5, /device:TPU:11, one launch (start us, length us, event | category | flops | bytes accessed | tf_op | source)
XLA Modules:
  0.0 125.7 jit_solution(15043504327504656673)
XLA Ops:
  0.7 3.6 %shard_map.46 = (f32[1,512,512]{2,1,0:T(8,128)S(1)}, bf16[1,512,512]{2,1,0:T(8,128)(2,1)S(1)}) custom-call(s32[5]{0:T(128)S(1)} %pad_add_fusion.refs_0_, bf16[4,2,512,2,512]{4,3,2,1,0:T(2,128)(2,1)} %refs_1_.3, bf16[4,2,512,2,512]{4,3,2,1,0:T(2,128)(2,1)} %refs_2_.3), custom_call_target="tpu_custom_call" | custom-call | flops 100000000 | bytes 1024 | tf_op jit(solution)/shard_map/pallas_call | solution.py:40
  5.0 6.0 %all-to-all-start = ((bf16[512,2,512]{2,1,0:T(2,128)(2,1)}), bf16[512,2,512]{2,1,0:T(2,128)(2,1)S(1)}, u32[]{:S(2)}, u32[]{:S(2)}) async-start(bf16[512,2,512]{2,1,0:T(2,128)(2,1)} %bitcast.7), calls=%async_computation | async-start | bytes 2097152 | tf_op jit(solution)/shard_map/all_to_all | solution.py:387
  13.0 7.1 %shard_map.48 = (f32[2,512,512]{2,1,0:T(8,128)S(1)}, bf16[2,512,512]{2,1,0:T(8,128)(2,1)S(1)}, f32[1,512,512]{2,1,0:T(8,128)S(1)}, bf16[1,512,512]{2,1,0:T(8,128)(2,1)S(1)}) custom-call(s32[5]{0:T(128)S(1)} %pad_add_fusion.refs_0_, bf16[4,2,512,2,512]{4,3,2,1,0:T(2,128)(2,1)} %refs_1_.3, bf16[4,2,512,2,512]{4,3,2,1,0:T(2,128)(2,1)} %refs_2_.3, ...), custom_call_target="tpu_custom_call" | custom-call | flops 10000000000 | bytes 1024 | tf_op jit(solution)/shard_map/pallas_call | solution.py:40
  21.7 4.1 %collective-permute-done.3.refs_2_ = bf16[1,256,512]{2,1,0:T(8,128)(2,1)S(1)} collective-permute-done((bf16[1,256,512]{2,1,0:T(8,128)(2,1)S(1)}, bf16[1,256,512]{2,1,0:T(8,128)(2,1)S(1)}, u32[]{:S(2)}, u32[]{:S(2)}) %collective-permute-start.3) | collective-permute-done | bytes 262176 | tf_op jit(solution)/shard_map/ppermute | solution.py:208
  26.4 5.0 %collective-permute-start.5 = (bf16[1,64,512]{2,1,0:T(8,128)(2,1)S(1)}, bf16[1,64,512]{2,1,0:T(8,128)(2,1)S(1)}, u32[]{:S(2)}, u32[]{:S(2)}) collective-permute-start(bf16[1,64,512]{2,1,0:T(8,128)(2,1)S(1)} %get-tuple-element.40), channel_id=1, source_target_pairs={{0,8},{1,9},{2,10},{3,11},{4,12},{5,13},{6,14},{7,15},{8,0},{9,1},... | collective-permute-start | bytes 196616 | tf_op jit(solution)/shard_map/ppermute | solution.py:208
  33.6 5.2 %all-to-all-done.refs_1_ = bf16[512,2,512]{2,1,0:T(2,128)(2,1)S(1)} async-done(((bf16[512,2,512]{2,1,0:T(2,128)(2,1)}), bf16[512,2,512]{2,1,0:T(2,128)(2,1)S(1)}, u32[]{:S(2)}, u32[]{:S(2)}) %all-to-all-start) | async-done | bytes 1048608 | tf_op jit(solution)/shard_map/all_to_all | solution.py:387
  40.0 2.7 %shard_map.51.refs_5_ = bf16[2,512,1024]{2,1,0:T(8,128)(2,1)S(1)} custom-call(s32[5]{0:T(128)S(1)} %pad_add_fusion.refs_0_, bf16[512,2,512]{2,1,0:T(2,128)(2,1)S(1)} %all-to-all-done.refs_1_, f32[2,256,512]{2,1,0:T(8,128)S(1)} %copy-done.3), custom_call_target="tpu_custom_call" | custom-call | flops 5000000000 | bytes 1024 | tf_op jit(solution)/shard_map/pallas_call | solution.py:40
  49.4 2.7 %collective-permute-start.9 = (bf16[2,64,512]{2,1,0:T(8,128)(2,1)S(1)}, bf16[2,64,512]{2,1,0:T(8,128)(2,1)S(1)}, u32[]{:S(2)}, u32[]{:S(2)}) collective-permute-start(bf16[2,64,512]{2,1,0:T(8,128)(2,1)S(1)} %get-tuple-element.46), channel_id=1, source_target_pairs={{0,8},{1,9},{2,10},{3,11},{4,12},{5,13},{6,14},{7,15},{8,0},{9,1},... | collective-permute-start | bytes 393224 | tf_op jit(solution)/shard_map/ppermute | solution.py:208
  54.5 3.1 %collective-permute-done.10.refs_3_ = bf16[2,64,512]{2,1,0:T(8,128)(2,1)S(1)} collective-permute-done((bf16[2,64,512]{2,1,0:T(8,128)(2,1)S(1)}, bf16[2,64,512]{2,1,0:T(8,128)(2,1)S(1)}, u32[]{:S(2)}, u32[]{:S(2)}) %collective-permute-start.10) | collective-permute-done | bytes 131104 | tf_op jit(solution)/shard_map/ppermute | solution.py:208
  57.6 5.6 %collective-permute-done.11.refs_4_ = bf16[2,64,512]{2,1,0:T(8,128)(2,1)S(1)} collective-permute-done((bf16[2,64,512]{2,1,0:T(8,128)(2,1)S(1)}, bf16[2,64,512]{2,1,0:T(8,128)(2,1)S(1)}, u32[]{:S(2)}, u32[]{:S(2)}) %collective-permute-start.11) | collective-permute-done | bytes 131104 | tf_op jit(solution)/shard_map/ppermute | solution.py:208
  67.2 2.0 %collective-permute-start.25 = (bf16[4,1,64,512]{3,2,1,0:T(8,128)(2,1)S(1)}, bf16[4,1,64,512]{3,2,1,0:T(8,128)(2,1)S(1)}, u32[]{:S(2)}, u32[]{:S(2)}) collective-permute-start(bf16[4,1,64,512]{3,2,1,0:T(8,128)(2,1)S(1)} %shard_map.55.refs_5_.refs_1_), channel_id=1, source_target_pairs={{0,1},{1,0},{2,3},{3,2},{4,5},{5,4},{6,7},{7,6},{8,9},{9,8},{10,11... | collective-permute-start | bytes 786440 | tf_op jit(solution)/shard_map/ppermute | solution.py:208
  71.8 4.4 %collective-permute-start.26 = (bf16[4,1,64,512]{3,2,1,0:T(8,128)(2,1)S(1)}, bf16[4,1,64,512]{3,2,1,0:T(8,128)(2,1)S(1)}, u32[]{:S(2)}, u32[]{:S(2)}) collective-permute-start(bf16[4,1,64,512]{3,2,1,0:T(8,128)(2,1)S(1)} %collective-permute-done.24.refs_2_), channel_id=1, source_target_pairs={{0,1},{1,0},{2,3},{3,2},{4,5},{5,4},{6,7},{7,6},{8,9},{9,8},{10,11... | collective-permute-start | bytes 786440 | tf_op jit(solution)/shard_map/ppermute | solution.py:208
  77.4 2.8 %shard_map.59.refs_5_ = bf16[8,64,1024]{2,1,0:T(8,128)(2,1)} custom-call(s32[5]{0:T(128)S(1)} %pad_add_fusion.refs_0_, bf16[4,1,64,512]{3,2,1,0:T(8,128)(2,1)S(1)} %shard_map.55.refs_5_.refs_1_, bf16[4,1,64,512]{3,2,1,0:T(8,128)(2,1)S(1)} %collective-permute-done.24.refs_2_, bf16[4,1,64,512]{3,2,1,0:T(8,128)(2,1)S(1)} %collective-permute-done.25.refs_3_, ...), custom_call_target="tpu_custom_call" | custom-call | flops 100000000 | bytes 1024 | tf_op jit(solution)/shard_map/pallas_call | solution.py:40
  80.2 3.6 %collective-permute-done.23.refs_4_ = bf16[1,2,64,512]{3,2,1,0:T(8,128)(2,1)S(1)} collective-permute-done((bf16[1,2,64,512]{3,2,1,0:T(8,128)(2,1)S(1)}, bf16[1,2,64,512]{3,2,1,0:T(8,128)(2,1)S(1)}, u32[]{:S(2)}, u32[]{:S(2)}) %collective-permute-start.23) | collective-permute-done | bytes 131104 | tf_op jit(solution)/shard_map/ppermute | solution.py:208
  85.7 1.8 %collective-permute-start.19 = (bf16[1,1,64,512]{3,2,1,0:T(8,128)(2,1)S(1)}, bf16[1,1,64,512]{3,2,1,0:T(8,128)(2,1)S(1)}, u32[]{:S(2)}, u32[]{:S(2)}) collective-permute-start(bf16[1,1,64,512]{3,2,1,0:T(8,128)(2,1)S(1)} %shard_map.58.refs_6_.refs_1_), channel_id=1, source_target_pairs={{0,4},{1,5},{2,6},{3,7},{4,0},{5,1},{6,2},{7,3},{8,12},{9,13},{10,... | collective-permute-start | bytes 196616 | tf_op jit(solution)/shard_map/ppermute | solution.py:208
  88.3 1.9 %collective-permute-start.31 = (bf16[4,2,64,512]{3,2,1,0:T(8,128)(2,1)S(1)}, bf16[4,2,64,512]{3,2,1,0:T(8,128)(2,1)S(1)}, u32[]{:S(2)}, u32[]{:S(2)}) collective-permute-start(bf16[4,2,64,512]{3,2,1,0:T(8,128)(2,1)S(1)} %shard_map.60.refs_5_.refs_1_), channel_id=1, source_target_pairs={{0,1},{1,0},{2,3},{3,2},{4,5},{5,4},{6,7},{7,6},{8,9},{9,8},{10,11... | collective-permute-start | bytes 1572872 | tf_op jit(solution)/shard_map/ppermute | solution.py:208
  90.2 4.2 %all-to-all-start.1 = ((bf16[16,32,1024]{2,1,0:T(8,128)(2,1)}), bf16[16,32,1024]{2,1,0:T(8,128)(2,1)S(1)}, u32[]{:S(2)}, u32[]{:S(2)}) async-start(bf16[16,32,1024]{2,1,0:T(8,128)(2,1)} %bitcast.2), calls=%async_computation.1 | async-start | bytes 2097152 | tf_op jit(solution)/shard_map/all_to_all | solution.py:387
  94.4 2.9 %collective-permute-done.30.refs_2_.refs_6_ = bf16[4,2,64,512]{3,2,1,0:T(8,128)(2,1)S(1)} collective-permute-done((bf16[4,2,64,512]{3,2,1,0:T(8,128)(2,1)S(1)}, bf16[4,2,64,512]{3,2,1,0:T(8,128)(2,1)S(1)}, u32[]{:S(2)}, u32[]{:S(2)}) %collective-permute-start.30) | collective-permute-done | bytes 524320 | tf_op jit(solution)/shard_map/ppermute | solution.py:208
  97.3 3.1 %collective-permute-start.32 = (bf16[4,2,64,512]{3,2,1,0:T(8,128)(2,1)S(1)}, bf16[4,2,64,512]{3,2,1,0:T(8,128)(2,1)S(1)}, u32[]{:S(2)}, u32[]{:S(2)}) collective-permute-start(bf16[4,2,64,512]{3,2,1,0:T(8,128)(2,1)S(1)} %collective-permute-done.30.refs_2_.refs_6_), channel_id=1, source_target_pairs={{0,1},{1,0},{2,3},{3,2},{4,5},{5,4},{6,7},{7,6},{8,9},{9,8},{10,11... | collective-permute-start | bytes 1572872 | tf_op jit(solution)/shard_map/ppermute | solution.py:208
  101.0 2.3 %collective-permute-start.27 = (bf16[4,1,64,512]{3,2,1,0:T(8,128)(2,1)S(1)}, bf16[4,1,64,512]{3,2,1,0:T(8,128)(2,1)S(1)}, u32[]{:S(2)}, u32[]{:S(2)}) collective-permute-start(bf16[4,1,64,512]{3,2,1,0:T(8,128)(2,1)S(1)} %shard_map.61.refs_9_.refs_1_), channel_id=1, source_target_pairs={{0,2},{1,3},{2,0},{3,1},{4,6},{5,7},{6,4},{7,5},{8,10},{9,11},{10,... | collective-permute-start | bytes 786440 | tf_op jit(solution)/shard_map/ppermute | solution.py:208
  103.6 11.7 %collective-permute-done.27.refs_2_ = bf16[4,1,64,512]{3,2,1,0:T(8,128)(2,1)S(1)} collective-permute-done((bf16[4,1,64,512]{3,2,1,0:T(8,128)(2,1)S(1)}, bf16[4,1,64,512]{3,2,1,0:T(8,128)(2,1)S(1)}, u32[]{:S(2)}, u32[]{:S(2)}) %collective-permute-start.27) | collective-permute-done | bytes 262176 | tf_op jit(solution)/shard_map/ppermute | solution.py:208
  115.7 2.0 %shard_map.62.refs_3_ = bf16[8,64,1024]{2,1,0:T(8,128)(2,1)S(1)} custom-call(s32[5]{0:T(128)S(1)} %pad_add_fusion.refs_0_, bf16[4,2,64,512]{3,2,1,0:T(8,128)(2,1)S(1)} %shard_map.60.refs_5_.refs_1_, bf16[4,2,64,512]{3,2,1,0:T(8,128)(2,1)S(1)} %collective-permute-done.30.refs_2_.refs_6_, bf16[4,2,64,512]{3,2,1,0:T(8,128)(2,1)S(1)} %collective-permute-done.31.refs_3_.refs_7_, ...), custom_call_target="tpu_custom_call" | custom-call | flops 2000000000 | bytes 1024 | tf_op jit(solution)/shard_map/pallas_call | solution.py:40
  120.5 1.8 %shard_map.63.refs_5_.refs_6_ = bf16[2,512,1024]{2,1,0:T(8,128)(2,1)S(1)} custom-call(s32[5]{0:T(128)S(1)} %pad_add_fusion.refs_0_, bf16[512,1024]{1,0:T(8,128)(2,1)S(1)} %bitcast.5, bf16[512,1024]{1,0:T(8,128)(2,1)S(1)} %bitcast.6, bf16[8,64,1024]{2,1,0:T(8,128)(2,1)S(1)} %copy-done.1), custom_call_target="tpu_custom_call" | custom-call | flops 2000000000 | bytes 1024 | tf_op jit(solution)/shard_map/pallas_call | solution.py:40
  122.3 3.3 %shard_map.64 = bf16[1,512,2,512]{3,2,1,0:T(2,128)(2,1)} custom-call(s32[5]{0:T(128)S(1)} %pad_add_fusion.refs_0_, bf16[4,1,64,512]{3,2,1,0:T(8,128)(2,1)S(1)} %shard_map.61.refs_9_.refs_1_, bf16[4,1,64,512]{3,2,1,0:T(8,128)(2,1)S(1)} %collective-permute-done.27.refs_2_, bf16[4,1,64,512]{3,2,1,0:T(8,128)(2,1)S(1)} %collective-permute-done.28.refs_3_, ...), custom_call_target="tpu_custom_call" | custom-call | flops 5000000000 | bytes 1024 | tf_op jit(solution)/shard_map/pallas_call | solution.py:40
  (84 shorter events, 32.3 us)
Async XLA Ops:
  5.0 33.7 %all-to-all-start = ((bf16[512,2,512]{2,1,0:T(2,128)(2,1)}), bf16[512,2,512]{2,1,0:T(2,128)(2,1)S(1)}, u32[]{:S(2)}, u32[]{:S(2)}) async-start(bf16[512,2,512]{2,1,0:T(2,128)(2,1)} %bitcast.7), calls=%async_computation | async-start | bytes 2097152 | tf_op jit(solution)/shard_map/all_to_all | solution.py:387
  11.7 14.1 %collective-permute-start.3 = (bf16[1,256,512]{2,1,0:T(8,128)(2,1)S(1)}, bf16[1,256,512]{2,1,0:T(8,128)(2,1)S(1)}, u32[]{:S(2)}, u32[]{:S(2)}) collective-permute-start(bf16[1,256,512]{2,1,0:T(8,128)(2,1)S(1)} %get-tuple-element.36), channel_id=1, source_target_pairs={{0,2},{1,3},{2,0},{3,1},{4,6},{5,7},{6,4},{7,5},{8,10},{9,11},{10,... | collective-permute-start | bytes 786440 | tf_op jit(solution)/shard_map/ppermute | solution.py:208
  21.1 27.1 %collective-permute-start.1 = (bf16[1,512,512]{2,1,0:T(8,128)(2,1)S(1)}, bf16[1,512,512]{2,1,0:T(8,128)(2,1)S(1)}, u32[]{:S(2)}, u32[]{:S(2)}) collective-permute-start(bf16[1,512,512]{2,1,0:T(8,128)(2,1)S(1)} %get-tuple-element.33), channel_id=1, source_target_pairs={{0,1},{1,0},{2,3},{3,2},{4,5},{5,4},{6,7},{7,6},{8,9},{9,8},{10,11... | collective-permute-start | bytes 1572872 | tf_op jit(solution)/shard_map/ppermute | solution.py:208
  21.7 10.1 %collective-permute-start.2 = (bf16[2,512,512]{2,1,0:T(8,128)(2,1)S(1)}, bf16[2,512,512]{2,1,0:T(8,128)(2,1)S(1)}, u32[]{:S(2)}, u32[]{:S(2)}) collective-permute-start(bf16[2,512,512]{2,1,0:T(8,128)(2,1)S(1)} %get-tuple-element.35), channel_id=1, source_target_pairs={{0,1},{1,0},{2,3},{3,2},{4,5},{5,4},{6,7},{7,6},{8,9},{9,8},{10,11... | collective-permute-start | bytes 3145736 | tf_op jit(solution)/shard_map/ppermute | solution.py:208
  26.4 16.3 %collective-permute-start.5 = (bf16[1,64,512]{2,1,0:T(8,128)(2,1)S(1)}, bf16[1,64,512]{2,1,0:T(8,128)(2,1)S(1)}, u32[]{:S(2)}, u32[]{:S(2)}) collective-permute-start(bf16[1,64,512]{2,1,0:T(8,128)(2,1)S(1)} %get-tuple-element.40), channel_id=1, source_target_pairs={{0,8},{1,9},{2,10},{3,11},{4,12},{5,13},{6,14},{7,15},{8,0},{9,1},... | collective-permute-start | bytes 196616 | tf_op jit(solution)/shard_map/ppermute | solution.py:208
  31.4 11.3 %collective-permute-start.6 = (bf16[1,64,512]{2,1,0:T(8,128)(2,1)S(1)}, bf16[1,64,512]{2,1,0:T(8,128)(2,1)S(1)}, u32[]{:S(2)}, u32[]{:S(2)}) collective-permute-start(bf16[1,64,512]{2,1,0:T(8,128)(2,1)S(1)} %get-tuple-element.41), channel_id=1, source_target_pairs={{0,4},{1,5},{2,6},{3,7},{4,0},{5,1},{6,2},{7,3},{8,12},{9,13},{10,... | collective-permute-start | bytes 196616 | tf_op jit(solution)/shard_map/ppermute | solution.py:208
  31.5 11.3 %collective-permute-start.7 = (bf16[1,64,512]{2,1,0:T(8,128)(2,1)S(1)}, bf16[1,64,512]{2,1,0:T(8,128)(2,1)S(1)}, u32[]{:S(2)}, u32[]{:S(2)}) collective-permute-start(bf16[1,64,512]{2,1,0:T(8,128)(2,1)S(1)} %get-tuple-element.42), channel_id=1, source_target_pairs={{0,12},{1,13},{2,14},{3,15},{4,8},{5,9},{6,10},{7,11},{8,4},{9,5},... | collective-permute-start | bytes 196616 | tf_op jit(solution)/shard_map/ppermute | solution.py:208
  33.5 14.0 %collective-permute-start.4 = (bf16[2,256,512]{2,1,0:T(8,128)(2,1)S(1)}, bf16[2,256,512]{2,1,0:T(8,128)(2,1)S(1)}, u32[]{:S(2)}, u32[]{:S(2)}) collective-permute-start(bf16[2,256,512]{2,1,0:T(8,128)(2,1)S(1)} %get-tuple-element.39), channel_id=1, source_target_pairs={{0,2},{1,3},{2,0},{3,1},{4,6},{5,7},{6,4},{7,5},{8,10},{9,11},{10,... | collective-permute-start | bytes 1572872 | tf_op jit(solution)/shard_map/ppermute | solution.py:208
  48.9 15.0 %collective-permute-start.8 = (bf16[1,256,512]{2,1,0:T(8,128)(2,1)S(1)}, bf16[1,256,512]{2,1,0:T(8,128)(2,1)S(1)}, u32[]{:S(2)}, u32[]{:S(2)}) collective-permute-start(bf16[1,256,512]{2,1,0:T(8,128)(2,1)S(1)} %get-tuple-element.45), channel_id=1, source_target_pairs={{0,2},{1,3},{2,0},{3,1},{4,6},{5,7},{6,4},{7,5},{8,10},{9,11},{10,... | collective-permute-start | bytes 786440 | tf_op jit(solution)/shard_map/ppermute | solution.py:208
  52.1 11.1 %collective-permute-start.11 = (bf16[2,64,512]{2,1,0:T(8,128)(2,1)S(1)}, bf16[2,64,512]{2,1,0:T(8,128)(2,1)S(1)}, u32[]{:S(2)}, u32[]{:S(2)}) collective-permute-start(bf16[2,64,512]{2,1,0:T(8,128)(2,1)S(1)} %get-tuple-element.48), channel_id=1, source_target_pairs={{0,12},{1,13},{2,14},{3,15},{4,8},{5,9},{6,10},{7,11},{8,4},{9,5},... | collective-permute-start | bytes 393224 | tf_op jit(solution)/shard_map/ppermute | solution.py:208
  52.9 16.2 %collective-permute-start.24 = (bf16[4,1,64,512]{3,2,1,0:T(8,128)(2,1)S(1)}, bf16[4,1,64,512]{3,2,1,0:T(8,128)(2,1)S(1)}, u32[]{:S(2)}, u32[]{:S(2)}) collective-permute-start(bf16[4,1,64,512]{3,2,1,0:T(8,128)(2,1)S(1)} %shard_map.55.refs_5_.refs_1_), channel_id=1, source_target_pairs={{0,2},{1,3},{2,0},{3,1},{4,6},{5,7},{6,4},{7,5},{8,10},{9,11},{10,... | collective-permute-start | bytes 786440 | tf_op jit(solution)/shard_map/ppermute | solution.py:208
  67.2 9.6 %collective-permute-start.25 = (bf16[4,1,64,512]{3,2,1,0:T(8,128)(2,1)S(1)}, bf16[4,1,64,512]{3,2,1,0:T(8,128)(2,1)S(1)}, u32[]{:S(2)}, u32[]{:S(2)}) collective-permute-start(bf16[4,1,64,512]{3,2,1,0:T(8,128)(2,1)S(1)} %shard_map.55.refs_5_.refs_1_), channel_id=1, source_target_pairs={{0,1},{1,0},{2,3},{3,2},{4,5},{5,4},{6,7},{7,6},{8,9},{9,8},{10,11... | collective-permute-start | bytes 786440 | tf_op jit(solution)/shard_map/ppermute | solution.py:208
  69.2 11.1 %collective-permute-start.21 = (bf16[1,2,64,512]{3,2,1,0:T(8,128)(2,1)S(1)}, bf16[1,2,64,512]{3,2,1,0:T(8,128)(2,1)S(1)}, u32[]{:S(2)}, u32[]{:S(2)}) collective-permute-start(bf16[1,2,64,512]{3,2,1,0:T(8,128)(2,1)S(1)} %shard_map.56.refs_3_.refs_1_), channel_id=1, source_target_pairs={{0,8},{1,9},{2,10},{3,11},{4,12},{5,13},{6,14},{7,15},{8,0},{9,1},... | collective-permute-start | bytes 393224 | tf_op jit(solution)/shard_map/ppermute | solution.py:208
  70.4 9.8 %collective-permute-start.22 = (bf16[1,2,64,512]{3,2,1,0:T(8,128)(2,1)S(1)}, bf16[1,2,64,512]{3,2,1,0:T(8,128)(2,1)S(1)}, u32[]{:S(2)}, u32[]{:S(2)}) collective-permute-start(bf16[1,2,64,512]{3,2,1,0:T(8,128)(2,1)S(1)} %shard_map.56.refs_3_.refs_1_), channel_id=1, source_target_pairs={{0,4},{1,5},{2,6},{3,7},{4,0},{5,1},{6,2},{7,3},{8,12},{9,13},{10,... | collective-permute-start | bytes 393224 | tf_op jit(solution)/shard_map/ppermute | solution.py:208
  71.2 12.7 %collective-permute-start.23 = (bf16[1,2,64,512]{3,2,1,0:T(8,128)(2,1)S(1)}, bf16[1,2,64,512]{3,2,1,0:T(8,128)(2,1)S(1)}, u32[]{:S(2)}, u32[]{:S(2)}) collective-permute-start(bf16[1,2,64,512]{3,2,1,0:T(8,128)(2,1)S(1)} %shard_map.56.refs_3_.refs_1_), channel_id=1, source_target_pairs={{0,12},{1,13},{2,14},{3,15},{4,8},{5,9},{6,10},{7,11},{8,4},{9,5},... | collective-permute-start | bytes 393224 | tf_op jit(solution)/shard_map/ppermute | solution.py:208
  84.4 12.9 %collective-permute-start.30 = (bf16[4,2,64,512]{3,2,1,0:T(8,128)(2,1)S(1)}, bf16[4,2,64,512]{3,2,1,0:T(8,128)(2,1)S(1)}, u32[]{:S(2)}, u32[]{:S(2)}) collective-permute-start(bf16[4,2,64,512]{3,2,1,0:T(8,128)(2,1)S(1)} %shard_map.60.refs_5_.refs_1_), channel_id=1, source_target_pairs={{0,2},{1,3},{2,0},{3,1},{4,6},{5,7},{6,4},{7,5},{8,10},{9,11},{10,... | collective-permute-start | bytes 1572872 | tf_op jit(solution)/shard_map/ppermute | solution.py:208
  85.7 14.8 %collective-permute-start.18 = (bf16[1,1,64,512]{3,2,1,0:T(8,128)(2,1)S(1)}, bf16[1,1,64,512]{3,2,1,0:T(8,128)(2,1)S(1)}, u32[]{:S(2)}, u32[]{:S(2)}) collective-permute-start(bf16[1,1,64,512]{3,2,1,0:T(8,128)(2,1)S(1)} %shard_map.58.refs_6_.refs_1_), channel_id=1, source_target_pairs={{0,8},{1,9},{2,10},{3,11},{4,12},{5,13},{6,14},{7,15},{8,0},{9,1},... | collective-permute-start | bytes 196616 | tf_op jit(solution)/shard_map/ppermute | solution.py:208
  85.7 14.8 %collective-permute-start.19 = (bf16[1,1,64,512]{3,2,1,0:T(8,128)(2,1)S(1)}, bf16[1,1,64,512]{3,2,1,0:T(8,128)(2,1)S(1)}, u32[]{:S(2)}, u32[]{:S(2)}) collective-permute-start(bf16[1,1,64,512]{3,2,1,0:T(8,128)(2,1)S(1)} %shard_map.58.refs_6_.refs_1_), channel_id=1, source_target_pairs={{0,4},{1,5},{2,6},{3,7},{4,0},{5,1},{6,2},{7,3},{8,12},{9,13},{10,... | collective-permute-start | bytes 196616 | tf_op jit(solution)/shard_map/ppermute | solution.py:208
  87.5 13.0 %collective-permute-start.20 = (bf16[1,1,64,512]{3,2,1,0:T(8,128)(2,1)S(1)}, bf16[1,1,64,512]{3,2,1,0:T(8,128)(2,1)S(1)}, u32[]{:S(2)}, u32[]{:S(2)}) collective-permute-start(bf16[1,1,64,512]{3,2,1,0:T(8,128)(2,1)S(1)} %shard_map.58.refs_6_.refs_1_), channel_id=1, source_target_pairs={{0,12},{1,13},{2,14},{3,15},{4,8},{5,9},{6,10},{7,11},{8,4},{9,5},... | collective-permute-start | bytes 196616 | tf_op jit(solution)/shard_map/ppermute | solution.py:208
  88.3 27.4 %collective-permute-start.31 = (bf16[4,2,64,512]{3,2,1,0:T(8,128)(2,1)S(1)}, bf16[4,2,64,512]{3,2,1,0:T(8,128)(2,1)S(1)}, u32[]{:S(2)}, u32[]{:S(2)}) collective-permute-start(bf16[4,2,64,512]{3,2,1,0:T(8,128)(2,1)S(1)} %shard_map.60.refs_5_.refs_1_), channel_id=1, source_target_pairs={{0,1},{1,0},{2,3},{3,2},{4,5},{5,4},{6,7},{7,6},{8,9},{9,8},{10,11... | collective-permute-start | bytes 1572872 | tf_op jit(solution)/shard_map/ppermute | solution.py:208
  90.2 29.1 %all-to-all-start.1 = ((bf16[16,32,1024]{2,1,0:T(8,128)(2,1)}), bf16[16,32,1024]{2,1,0:T(8,128)(2,1)S(1)}, u32[]{:S(2)}, u32[]{:S(2)}) async-start(bf16[16,32,1024]{2,1,0:T(8,128)(2,1)} %bitcast.2), calls=%async_computation.1 | async-start | bytes 2097152 | tf_op jit(solution)/shard_map/all_to_all | solution.py:387
  97.3 18.4 %collective-permute-start.32 = (bf16[4,2,64,512]{3,2,1,0:T(8,128)(2,1)S(1)}, bf16[4,2,64,512]{3,2,1,0:T(8,128)(2,1)S(1)}, u32[]{:S(2)}, u32[]{:S(2)}) collective-permute-start(bf16[4,2,64,512]{3,2,1,0:T(8,128)(2,1)S(1)} %collective-permute-done.30.refs_2_.refs_6_), channel_id=1, source_target_pairs={{0,1},{1,0},{2,3},{3,2},{4,5},{5,4},{6,7},{7,6},{8,9},{9,8},{10,11... | collective-permute-start | bytes 1572872 | tf_op jit(solution)/shard_map/ppermute | solution.py:208
  101.0 14.3 %collective-permute-start.27 = (bf16[4,1,64,512]{3,2,1,0:T(8,128)(2,1)S(1)}, bf16[4,1,64,512]{3,2,1,0:T(8,128)(2,1)S(1)}, u32[]{:S(2)}, u32[]{:S(2)}) collective-permute-start(bf16[4,1,64,512]{3,2,1,0:T(8,128)(2,1)S(1)} %shard_map.61.refs_9_.refs_1_), channel_id=1, source_target_pairs={{0,2},{1,3},{2,0},{3,1},{4,6},{5,7},{6,4},{7,5},{8,10},{9,11},{10,... | collective-permute-start | bytes 786440 | tf_op jit(solution)/shard_map/ppermute | solution.py:208
  103.3 19.0 %collective-permute-start.28 = (bf16[4,1,64,512]{3,2,1,0:T(8,128)(2,1)S(1)}, bf16[4,1,64,512]{3,2,1,0:T(8,128)(2,1)S(1)}, u32[]{:S(2)}, u32[]{:S(2)}) collective-permute-start(bf16[4,1,64,512]{3,2,1,0:T(8,128)(2,1)S(1)} %shard_map.61.refs_9_.refs_1_), channel_id=1, source_target_pairs={{0,1},{1,0},{2,3},{3,2},{4,5},{5,4},{6,7},{7,6},{8,9},{9,8},{10,11... | collective-permute-start | bytes 786440 | tf_op jit(solution)/shard_map/ppermute | solution.py:208
  (20 other events, 96.4 us)

commit v6 on v5

--- a/solution.py
+++ b/solution.py
@@ -11,8 +11,8 @@
 LEAF_LIMIT = 48 << 20
 DIRECT = True, True, True
 LEAVES = 0.1, 10.0
-STEPS = (1.0, 20.0, 20.0, 10.0), (2.0, 3.0, 20.0, 20.0), (3.0, 5.0, 10.0, 20.0)
-PREPARE, FIRST, JOINED, LAST = 5.0, 0.1, 2.0, 5.0
+STEPS = (0.1, 20.0, 3.0, 10.0), (0.5, 20.0, 20.0, 20.0), (0.5, 5.0, 10.0, 20.0)
+PREPARE, FIRST, JOINED, LAST = 0.1, 1.0, 2.0, 1.0
 RIGHT = 2.0
 TILE = 256
 bf16, f32 = jnp.bfloat16, jnp.float32
@@ -456,13 +456,13 @@
     b, c = (total.steps() for total in sums[1:])
     next(a, None)
     next(b, None)
+    next(c, None)
     right = prepare(chain, given)
     next(a, None)
     next(b, None)
     next(c, None)
     next(a, None)
     next(b, None)
-    next(c, None)
     next(c, None)
     for _ in a:
         pass

time: 126 us -> 121 us (0.960)
  waiting for transfers between devices: 39.7 us -> 28.6 us
  starting transfers between devices: 48.8 us -> 55.5 us
  local copies, waits for them, and re-layouts: 5.42 us -> 2.23 us
  Pallas kernels: 30.6 us -> 33.5 us
    ppermute x33, starting transfers between devices: 38.5 us -> 45.3 us  [swap_with(): return lax.ppermute(x, 'outer', [(i, i ^ mask) for i in range(size)])]
    all_to_all x2, waiting for transfers between devices: 5.71 us -> 0.06 us  [exchange(): return lax.all_to_all(x, 'outer', split_axis=0, concat_axis=0, tiled=True)]
    ppermute x33, waiting for transfers between devices: 34 us -> 28.6 us  [swap_with(): return lax.ppermute(x, 'outer', [(i, i ^ mask) for i in range(size)])]
    unnamed x18 -> x4, local copies, waits for them, and re-layouts: 5.42 us -> 2.23 us
    pallas_call x19, Pallas kernels: 30.6 us -> 33.5 us  [__call__(): pl.pallas_call(kernel, out_shape=shapes, in_specs=specs, out_specs=tuple(...]
  transfers between devices with their start and end apart: 35 -> 35, of which waited for: 11 -> 9; matrix products, arithmetic and copies ran while one was open for 0% -> 0% of each run, Pallas kernels for 18% -> 22%
where the time goes in v6:
time: 121 us
  starting transfers between devices  55.5 us (46%)
  Pallas kernels  33.5 us (28%)
  waiting for transfers between devices  28.6 us (24%)
  local copies, waits for them, and re-layouts  2.23 us (2%)
    ppermute x33, starting transfers between devices, swap_with(): return lax.ppermute(x, 'outer', [(i, i ^ mask) for i in range(size)])  45.3 us
    pallas_call x19, Pallas kernels, __call__(): pl.pallas_call(kernel, out_shape=shapes, in_specs=specs, out_specs=tuple(...  33.5 us
    ppermute x33, waiting for transfers between devices, swap_with(): return lax.ppermute(x, 'outer', [(i, i ^ mask) for i in range(size)])  28.6 us
    all_to_all x2, starting transfers between devices, exchange(): return lax.all_to_all(x, 'outer', split_axis=0, concat_axis=0, tiled=True)  10.2 us
  transfers between devices with their start and end apart: 35, of which 9 were waited for; matrix products, arithmetic and copies ran while one was open for 0% of the time, Pallas kernels for 22%

profile of v6, /device:TPU:11, one launch (start us, length us, event | category | flops | bytes accessed | tf_op | source)
XLA Modules:
  0.0 120.9 jit_solution(9834990603183803796)
XLA Ops:
  0.7 3.6 %shard_map.46 = (f32[1,512,512]{2,1,0:T(8,128)S(1)}, bf16[1,512,512]{2,1,0:T(8,128)(2,1)S(1)}) custom-call(s32[5]{0:T(128)S(1)} %pad_add_fusion.refs_0_, bf16[4,2,512,2,512]{4,3,2,1,0:T(2,128)(2,1)} %refs_1_.3, bf16[4,2,512,2,512]{4,3,2,1,0:T(2,128)(2,1)} %refs_2_.3), custom_call_target="tpu_custom_call" | custom-call | flops 100000000 | bytes 1024 | tf_op jit(solution)/shard_map/pallas_call | solution.py:40
  5.0 6.0 %all-to-all-start = ((bf16[512,2,512]{2,1,0:T(2,128)(2,1)}), bf16[512,2,512]{2,1,0:T(2,128)(2,1)S(1)}, u32[]{:S(2)}, u32[]{:S(2)}) async-start(bf16[512,2,512]{2,1,0:T(2,128)(2,1)} %bitcast.7), calls=%async_computation | async-start | bytes 2097152 | tf_op jit(solution)/shard_map/all_to_all | solution.py:387
  13.0 7.1 %shard_map.48 = (f32[2,512,512]{2,1,0:T(8,128)S(1)}, bf16[2,512,512]{2,1,0:T(8,128)(2,1)S(1)}, f32[1,512,512]{2,1,0:T(8,128)S(1)}, bf16[1,512,512]{2,1,0:T(8,128)(2,1)S(1)}) custom-call(s32[5]{0:T(128)S(1)} %pad_add_fusion.refs_0_, bf16[4,2,512,2,512]{4,3,2,1,0:T(2,128)(2,1)} %refs_1_.3, bf16[4,2,512,2,512]{4,3,2,1,0:T(2,128)(2,1)} %refs_2_.3, ...), custom_call_target="tpu_custom_call" | custom-call | flops 10000000000 | bytes 1024 | tf_op jit(solution)/shard_map/pallas_call | solution.py:40
  20.9 4.9 %collective-permute-done.3.refs_2_ = bf16[1,256,512]{2,1,0:T(8,128)(2,1)S(1)} collective-permute-done((bf16[1,256,512]{2,1,0:T(8,128)(2,1)S(1)}, bf16[1,256,512]{2,1,0:T(8,128)(2,1)S(1)}, u32[]{:S(2)}, u32[]{:S(2)}) %collective-permute-start.3) | collective-permute-done | bytes 262176 | tf_op jit(solution)/shard_map/ppermute | solution.py:208
  29.0 4.6 %collective-permute-start.6 = (bf16[1,64,512]{2,1,0:T(8,128)(2,1)}, bf16[1,64,512]{2,1,0:T(8,128)(2,1)}, u32[]{:S(2)}, u32[]{:S(2)}) collective-permute-start(bf16[1,64,512]{2,1,0:T(8,128)(2,1)} %get-tuple-element.42), channel_id=1, source_target_pairs={{0,8},{1,9},{2,10},{3,11},{4,12},{5,13},{6,14},{7,15},{8,0},{9,1},... | collective-permute-start | bytes 196616 | tf_op jit(solution)/shard_map/ppermute | solution.py:208
  36.6 2.7 %shard_map.52.refs_5_ = bf16[2,512,1024]{2,1,0:T(8,128)(2,1)S(1)} custom-call(s32[5]{0:T(128)S(1)} %pad_add_fusion.refs_0_, bf16[512,2,512]{2,1,0:T(2,128)(2,1)S(1)} %all-to-all-done.refs_1_, f32[1,256,512]{2,1,0:T(8,128)S(1)} %get-tuple-element.39.refs_2_.refs_1_), custom_call_target="tpu_custom_call" | custom-call | flops 100000000 | bytes 1024 | tf_op jit(solution)/shard_map/pallas_call | solution.py:40
  39.4 2.1 %collective-permute-done.8.refs_4_ = bf16[1,64,512]{2,1,0:T(8,128)(2,1)} collective-permute-done((bf16[1,64,512]{2,1,0:T(8,128)(2,1)}, bf16[1,64,512]{2,1,0:T(8,128)(2,1)}, u32[]{:S(2)}, u32[]{:S(2)}) %collective-permute-start.8) | collective-permute-done | bytes 65568 | tf_op jit(solution)/shard_map/ppermute | solution.py:208
  45.8 2.1 %collective-permute-start.12 = (bf16[2,64,512]{2,1,0:T(8,128)(2,1)S(1)}, bf16[2,64,512]{2,1,0:T(8,128)(2,1)S(1)}, u32[]{:S(2)}, u32[]{:S(2)}) collective-permute-start(bf16[2,64,512]{2,1,0:T(8,128)(2,1)S(1)} %get-tuple-element.50), channel_id=1, source_target_pairs={{0,8},{1,9},{2,10},{3,11},{4,12},{5,13},{6,14},{7,15},{8,0},{9,1},... | collective-permute-start | bytes 393224 | tf_op jit(solution)/shard_map/ppermute | solution.py:208
  48.0 2.7 %collective-permute-start.13 = (bf16[2,64,512]{2,1,0:T(8,128)(2,1)S(1)}, bf16[2,64,512]{2,1,0:T(8,128)(2,1)S(1)}, u32[]{:S(2)}, u32[]{:S(2)}) collective-permute-start(bf16[2,64,512]{2,1,0:T(8,128)(2,1)S(1)} %get-tuple-element.51), channel_id=1, source_target_pairs={{0,4},{1,5},{2,6},{3,7},{4,0},{5,1},{6,2},{7,3},{8,12},{9,13},{10,... | collective-permute-start | bytes 393224 | tf_op jit(solution)/shard_map/ppermute | solution.py:208
  55.3 2.2 %collective-permute-start.25 = (bf16[4,1,64,512]{3,2,1,0:T(8,128)(2,1)S(1)}, bf16[4,1,64,512]{3,2,1,0:T(8,128)(2,1)S(1)}, u32[]{:S(2)}, u32[]{:S(2)}) collective-permute-start(bf16[4,1,64,512]{3,2,1,0:T(8,128)(2,1)S(1)} %shard_map.56.refs_5_.refs_1_), channel_id=1, source_target_pairs={{0,1},{1,0},{2,3},{3,2},{4,5},{5,4},{6,7},{7,6},{8,9},{9,8},{10,11... | collective-permute-start | bytes 786440 | tf_op jit(solution)/shard_map/ppermute | solution.py:208
  57.5 2.2 %collective-permute-start.9 = (bf16[1,64,512]{2,1,0:T(8,128)(2,1)S(1)}, bf16[1,64,512]{2,1,0:T(8,128)(2,1)S(1)}, u32[]{:S(2)}, u32[]{:S(2)}) collective-permute-start(bf16[1,64,512]{2,1,0:T(8,128)(2,1)S(1)} %get-tuple-element.47), channel_id=1, source_target_pairs={{0,8},{1,9},{2,10},{3,11},{4,12},{5,13},{6,14},{7,15},{8,0},{9,1},... | collective-permute-start | bytes 196616 | tf_op jit(solution)/shard_map/ppermute | solution.py:208
  59.7 2.5 %collective-permute-done.14.refs_4_ = bf16[2,64,512]{2,1,0:T(8,128)(2,1)S(1)} collective-permute-done((bf16[2,64,512]{2,1,0:T(8,128)(2,1)S(1)}, bf16[2,64,512]{2,1,0:T(8,128)(2,1)S(1)}, u32[]{:S(2)}, u32[]{:S(2)}) %collective-permute-start.14) | collective-permute-done | bytes 131104 | tf_op jit(solution)/shard_map/ppermute | solution.py:208
  65.6 3.2 %collective-permute-done.11.refs_4_ = bf16[1,64,512]{2,1,0:T(8,128)(2,1)S(1)} collective-permute-done((bf16[1,64,512]{2,1,0:T(8,128)(2,1)S(1)}, bf16[1,64,512]{2,1,0:T(8,128)(2,1)S(1)}, u32[]{:S(2)}, u32[]{:S(2)}) %collective-permute-start.11) | collective-permute-done | bytes 65568 | tf_op jit(solution)/shard_map/ppermute | solution.py:208
  68.8 5.3 %collective-permute-start.26 = (bf16[4,1,64,512]{3,2,1,0:T(8,128)(2,1)S(1)}, bf16[4,1,64,512]{3,2,1,0:T(8,128)(2,1)S(1)}, u32[]{:S(2)}, u32[]{:S(2)}) collective-permute-start(bf16[4,1,64,512]{3,2,1,0:T(8,128)(2,1)S(1)} %collective-permute-done.24.refs_2_), channel_id=1, source_target_pairs={{0,1},{1,0},{2,3},{3,2},{4,5},{5,4},{6,7},{7,6},{8,9},{9,8},{10,11... | collective-permute-start | bytes 786440 | tf_op jit(solution)/shard_map/ppermute | solution.py:208
  75.2 2.8 %shard_map.59.refs_5_ = bf16[8,64,1024]{2,1,0:T(8,128)(2,1)} custom-call(s32[5]{0:T(128)S(1)} %pad_add_fusion.refs_0_, bf16[4,1,64,512]{3,2,1,0:T(8,128)(2,1)S(1)} %shard_map.56.refs_5_.refs_1_, bf16[4,1,64,512]{3,2,1,0:T(8,128)(2,1)S(1)} %collective-permute-done.24.refs_2_, bf16[4,1,64,512]{3,2,1,0:T(8,128)(2,1)S(1)} %collective-permute-done.25.refs_3_, ...), custom_call_target="tpu_custom_call" | custom-call | flops 1000000000 | bytes 1024 | tf_op jit(solution)/shard_map/pallas_call | solution.py:40
  80.5 2.3 %collective-permute-start.19 = (bf16[1,1,64,512]{3,2,1,0:T(8,128)(2,1)S(1)}, bf16[1,1,64,512]{3,2,1,0:T(8,128)(2,1)S(1)}, u32[]{:S(2)}, u32[]{:S(2)}) collective-permute-start(bf16[1,1,64,512]{3,2,1,0:T(8,128)(2,1)S(1)} %shard_map.58.refs_6_.refs_1_), channel_id=1, source_target_pairs={{0,4},{1,5},{2,6},{3,7},{4,0},{5,1},{6,2},{7,3},{8,12},{9,13},{10,... | collective-permute-start | bytes 196616 | tf_op jit(solution)/shard_map/ppermute | solution.py:208
  83.1 2.7 %collective-permute-start.31 = (bf16[4,2,64,512]{3,2,1,0:T(8,128)(2,1)S(1)}, bf16[4,2,64,512]{3,2,1,0:T(8,128)(2,1)}, u32[]{:S(2)}, u32[]{:S(2)}) collective-permute-start(bf16[4,2,64,512]{3,2,1,0:T(8,128)(2,1)S(1)} %shard_map.60.refs_5_.refs_1_), channel_id=1, source_target_pairs={{0,1},{1,0},{2,3},{3,2},{4,5},{5,4},{6,7},{7,6},{8,9},{9,8},{10,11... | collective-permute-start | bytes 1572872 | tf_op jit(solution)/shard_map/ppermute | solution.py:208
  85.8 4.2 %all-to-all-start.1 = ((bf16[16,32,1024]{2,1,0:T(8,128)(2,1)}), bf16[16,32,1024]{2,1,0:T(8,128)(2,1)S(1)}, u32[]{:S(2)}, u32[]{:S(2)}) async-start(bf16[16,32,1024]{2,1,0:T(8,128)(2,1)} %bitcast.2), calls=%async_computation.1 | async-start | bytes 2097152 | tf_op jit(solution)/shard_map/all_to_all | solution.py:387
  90.0 2.1 %collective-permute-done.30.refs_2_.refs_6_ = bf16[4,2,64,512]{3,2,1,0:T(8,128)(2,1)S(1)} collective-permute-done((bf16[4,2,64,512]{3,2,1,0:T(8,128)(2,1)S(1)}, bf16[4,2,64,512]{3,2,1,0:T(8,128)(2,1)S(1)}, u32[]{:S(2)}, u32[]{:S(2)}) %collective-permute-start.30) | collective-permute-done | bytes 524320 | tf_op jit(solution)/shard_map/ppermute | solution.py:208
  92.1 3.4 %collective-permute-start.32 = (bf16[4,2,64,512]{3,2,1,0:T(8,128)(2,1)S(1)}, bf16[4,2,64,512]{3,2,1,0:T(8,128)(2,1)S(1)}, u32[]{:S(2)}, u32[]{:S(2)}) collective-permute-start(bf16[4,2,64,512]{3,2,1,0:T(8,128)(2,1)S(1)} %collective-permute-done.30.refs_2_.refs_6_), channel_id=1, source_target_pairs={{0,1},{1,0},{2,3},{3,2},{4,5},{5,4},{6,7},{7,6},{8,9},{9,8},{10,11... | collective-permute-start | bytes 1572872 | tf_op jit(solution)/shard_map/ppermute | solution.py:208
  96.0 2.2 %collective-permute-start.27 = (bf16[4,1,64,512]{3,2,1,0:T(8,128)(2,1)S(1)}, bf16[4,1,64,512]{3,2,1,0:T(8,128)(2,1)S(1)}, u32[]{:S(2)}, u32[]{:S(2)}) collective-permute-start(bf16[4,1,64,512]{3,2,1,0:T(8,128)(2,1)S(1)} %shard_map.61.refs_9_.refs_1_), channel_id=1, source_target_pairs={{0,2},{1,3},{2,0},{3,1},{4,6},{5,7},{6,4},{7,5},{8,10},{9,11},{10,... | collective-permute-start | bytes 786440 | tf_op jit(solution)/shard_map/ppermute | solution.py:208
  98.5 11.9 %collective-permute-done.27.refs_2_ = bf16[4,1,64,512]{3,2,1,0:T(8,128)(2,1)S(1)} collective-permute-done((bf16[4,1,64,512]{3,2,1,0:T(8,128)(2,1)S(1)}, bf16[4,1,64,512]{3,2,1,0:T(8,128)(2,1)S(1)}, u32[]{:S(2)}, u32[]{:S(2)}) %collective-permute-start.27) | collective-permute-done | bytes 262176 | tf_op jit(solution)/shard_map/ppermute | solution.py:208
  111.0 2.8 %shard_map.62.refs_3_ = bf16[8,64,1024]{2,1,0:T(8,128)(2,1)S(1)} custom-call(s32[5]{0:T(128)S(1)} %pad_add_fusion.refs_0_, bf16[4,2,64,512]{3,2,1,0:T(8,128)(2,1)S(1)} %shard_map.60.refs_5_.refs_1_, bf16[4,2,64,512]{3,2,1,0:T(8,128)(2,1)S(1)} %collective-permute-done.30.refs_2_.refs_6_, bf16[4,2,64,512]{3,2,1,0:T(8,128)(2,1)} %collective-permute-done.31.refs_3_.refs_7_, ...), custom_call_target="tpu_custom_call" | custom-call | flops 2000000000 | bytes 1024 | tf_op jit(solution)/shard_map/pallas_call | solution.py:40
  117.9 2.8 %shard_map.64 = bf16[1,512,2,512]{3,2,1,0:T(2,128)(2,1)} custom-call(s32[5]{0:T(128)S(1)} %pad_add_fusion.refs_0_, bf16[4,1,64,512]{3,2,1,0:T(8,128)(2,1)S(1)} %shard_map.61.refs_9_.refs_1_, bf16[4,1,64,512]{3,2,1,0:T(8,128)(2,1)S(1)} %collective-permute-done.27.refs_2_, bf16[4,1,64,512]{3,2,1,0:T(8,128)(2,1)S(1)} %collective-permute-done.28.refs_3_, ...), custom_call_target="tpu_custom_call" | custom-call | flops 1000000000 | bytes 1024 | tf_op jit(solution)/shard_map/pallas_call | solution.py:40
  (70 shorter events, 32.0 us)
Async XLA Ops:
  5.0 31.6 %all-to-all-start = ((bf16[512,2,512]{2,1,0:T(2,128)(2,1)}), bf16[512,2,512]{2,1,0:T(2,128)(2,1)S(1)}, u32[]{:S(2)}, u32[]{:S(2)}) async-start(bf16[512,2,512]{2,1,0:T(2,128)(2,1)} %bitcast.7), calls=%async_computation | async-start | bytes 2097152 | tf_op jit(solution)/shard_map/all_to_all | solution.py:387
  11.7 14.1 %collective-permute-start.3 = (bf16[1,256,512]{2,1,0:T(8,128)(2,1)S(1)}, bf16[1,256,512]{2,1,0:T(8,128)(2,1)S(1)}, u32[]{:S(2)}, u32[]{:S(2)}) collective-permute-start(bf16[1,256,512]{2,1,0:T(8,128)(2,1)S(1)} %get-tuple-element.36), channel_id=1, source_target_pairs={{0,2},{1,3},{2,0},{3,1},{4,6},{5,7},{6,4},{7,5},{8,10},{9,11},{10,... | collective-permute-start | bytes 786440 | tf_op jit(solution)/shard_map/ppermute | solution.py:208
  20.1 13.7 %collective-permute-start.1 = (bf16[1,512,512]{2,1,0:T(8,128)(2,1)S(1)}, bf16[1,512,512]{2,1,0:T(8,128)(2,1)S(1)}, u32[]{:S(2)}, u32[]{:S(2)}) collective-permute-start(bf16[1,512,512]{2,1,0:T(8,128)(2,1)S(1)} %get-tuple-element.33), channel_id=1, source_target_pairs={{0,1},{1,0},{2,3},{3,2},{4,5},{5,4},{6,7},{7,6},{8,9},{9,8},{10,11... | collective-permute-start | bytes 1572872 | tf_op jit(solution)/shard_map/ppermute | solution.py:208
  28.6 16.6 %collective-permute-start.5 = (bf16[2,256,512]{2,1,0:T(8,128)(2,1)}, bf16[2,256,512]{2,1,0:T(8,128)(2,1)S(1)}, u32[]{:S(2)}, u32[]{:S(2)}) collective-permute-start(bf16[2,256,512]{2,1,0:T(8,128)(2,1)} %get-tuple-element.41), channel_id=1, source_target_pairs={{0,2},{1,3},{2,0},{3,1},{4,6},{5,7},{6,4},{7,5},{8,10},{9,11},{10,... | collective-permute-start | bytes 1572872 | tf_op jit(solution)/shard_map/ppermute | solution.py:208
  29.0 10.4 %collective-permute-start.6 = (bf16[1,64,512]{2,1,0:T(8,128)(2,1)}, bf16[1,64,512]{2,1,0:T(8,128)(2,1)}, u32[]{:S(2)}, u32[]{:S(2)}) collective-permute-start(bf16[1,64,512]{2,1,0:T(8,128)(2,1)} %get-tuple-element.42), channel_id=1, source_target_pairs={{0,8},{1,9},{2,10},{3,11},{4,12},{5,13},{6,14},{7,15},{8,0},{9,1},... | collective-permute-start | bytes 196616 | tf_op jit(solution)/shard_map/ppermute | solution.py:208
  35.1 12.8 %collective-permute-start.4 = (bf16[1,256,512]{2,1,0:T(8,128)(2,1)}, bf16[1,256,512]{2,1,0:T(8,128)(2,1)S(1)}, u32[]{:S(2)}, u32[]{:S(2)}) collective-permute-start(bf16[1,256,512]{2,1,0:T(8,128)(2,1)} %get-tuple-element.40), channel_id=1, source_target_pairs={{0,2},{1,3},{2,0},{3,1},{4,6},{5,7},{6,4},{7,5},{8,10},{9,11},{10,... | collective-permute-start | bytes 786440 | tf_op jit(solution)/shard_map/ppermute | solution.py:208
  43.7 9.2 %collective-permute-start.16 = (bf16[1,1,64,512]{3,2,1,0:T(8,128)(2,1)S(1)}, bf16[1,1,64,512]{3,2,1,0:T(8,128)(2,1)S(1)}, u32[]{:S(2)}, u32[]{:S(2)}) collective-permute-start(bf16[1,1,64,512]{3,2,1,0:T(8,128)(2,1)S(1)} %shard_map.53.refs_3_.refs_1_), channel_id=1, source_target_pairs={{0,4},{1,5},{2,6},{3,7},{4,0},{5,1},{6,2},{7,3},{8,12},{9,13},{10,... | collective-permute-start | bytes 196616 | tf_op jit(solution)/shard_map/ppermute | solution.py:208
  45.8 11.7 %collective-permute-start.12 = (bf16[2,64,512]{2,1,0:T(8,128)(2,1)S(1)}, bf16[2,64,512]{2,1,0:T(8,128)(2,1)S(1)}, u32[]{:S(2)}, u32[]{:S(2)}) collective-permute-start(bf16[2,64,512]{2,1,0:T(8,128)(2,1)S(1)} %get-tuple-element.50), channel_id=1, source_target_pairs={{0,8},{1,9},{2,10},{3,11},{4,12},{5,13},{6,14},{7,15},{8,0},{9,1},... | collective-permute-start | bytes 393224 | tf_op jit(solution)/shard_map/ppermute | solution.py:208
  48.0 11.8 %collective-permute-start.13 = (bf16[2,64,512]{2,1,0:T(8,128)(2,1)S(1)}, bf16[2,64,512]{2,1,0:T(8,128)(2,1)S(1)}, u32[]{:S(2)}, u32[]{:S(2)}) collective-permute-start(bf16[2,64,512]{2,1,0:T(8,128)(2,1)S(1)} %get-tuple-element.51), channel_id=1, source_target_pairs={{0,4},{1,5},{2,6},{3,7},{4,0},{5,1},{6,2},{7,3},{8,12},{9,13},{10,... | collective-permute-start | bytes 393224 | tf_op jit(solution)/shard_map/ppermute | solution.py:208
  51.3 10.9 %collective-permute-start.14 = (bf16[2,64,512]{2,1,0:T(8,128)(2,1)S(1)}, bf16[2,64,512]{2,1,0:T(8,128)(2,1)S(1)}, u32[]{:S(2)}, u32[]{:S(2)}) collective-permute-start(bf16[2,64,512]{2,1,0:T(8,128)(2,1)S(1)} %get-tuple-element.52), channel_id=1, source_target_pairs={{0,12},{1,13},{2,14},{3,15},{4,8},{5,9},{6,10},{7,11},{8,4},{9,5},... | collective-permute-start | bytes 393224 | tf_op jit(solution)/shard_map/ppermute | solution.py:208
  53.5 15.3 %collective-permute-start.24 = (bf16[4,1,64,512]{3,2,1,0:T(8,128)(2,1)S(1)}, bf16[4,1,64,512]{3,2,1,0:T(8,128)(2,1)S(1)}, u32[]{:S(2)}, u32[]{:S(2)}) collective-permute-start(bf16[4,1,64,512]{3,2,1,0:T(8,128)(2,1)S(1)} %shard_map.56.refs_5_.refs_1_), channel_id=1, source_target_pairs={{0,2},{1,3},{2,0},{3,1},{4,6},{5,7},{6,4},{7,5},{8,10},{9,11},{10,... | collective-permute-start | bytes 786440 | tf_op jit(solution)/shard_map/ppermute | solution.py:208
  55.3 19.3 %collective-permute-start.25 = (bf16[4,1,64,512]{3,2,1,0:T(8,128)(2,1)S(1)}, bf16[4,1,64,512]{3,2,1,0:T(8,128)(2,1)S(1)}, u32[]{:S(2)}, u32[]{:S(2)}) collective-permute-start(bf16[4,1,64,512]{3,2,1,0:T(8,128)(2,1)S(1)} %shard_map.56.refs_5_.refs_1_), channel_id=1, source_target_pairs={{0,1},{1,0},{2,3},{3,2},{4,5},{5,4},{6,7},{7,6},{8,9},{9,8},{10,11... | collective-permute-start | bytes 786440 | tf_op jit(solution)/shard_map/ppermute | solution.py:208
  63.3 14.7 %collective-permute-start.21 = (bf16[1,2,64,512]{3,2,1,0:T(8,128)(2,1)S(1)}, bf16[1,2,64,512]{3,2,1,0:T(8,128)(2,1)S(1)}, u32[]{:S(2)}, u32[]{:S(2)}) collective-permute-start(bf16[1,2,64,512]{3,2,1,0:T(8,128)(2,1)S(1)} %shard_map.57.refs_5_.refs_1_), channel_id=1, source_target_pairs={{0,8},{1,9},{2,10},{3,11},{4,12},{5,13},{6,14},{7,15},{8,0},{9,1},... | collective-permute-start | bytes 393224 | tf_op jit(solution)/shard_map/ppermute | solution.py:208
  64.7 13.3 %collective-permute-start.22 = (bf16[1,2,64,512]{3,2,1,0:T(8,128)(2,1)S(1)}, bf16[1,2,64,512]{3,2,1,0:T(8,128)(2,1)S(1)}, u32[]{:S(2)}, u32[]{:S(2)}) collective-permute-start(bf16[1,2,64,512]{3,2,1,0:T(8,128)(2,1)S(1)} %shard_map.57.refs_5_.refs_1_), channel_id=1, source_target_pairs={{0,4},{1,5},{2,6},{3,7},{4,0},{5,1},{6,2},{7,3},{8,12},{9,13},{10,... | collective-permute-start | bytes 393224 | tf_op jit(solution)/shard_map/ppermute | solution.py:208
  68.8 10.4 %collective-permute-start.23 = (bf16[1,2,64,512]{3,2,1,0:T(8,128)(2,1)S(1)}, bf16[1,2,64,512]{3,2,1,0:T(8,128)(2,1)S(1)}, u32[]{:S(2)}, u32[]{:S(2)}) collective-permute-start(bf16[1,2,64,512]{3,2,1,0:T(8,128)(2,1)S(1)} %shard_map.57.refs_5_.refs_1_), channel_id=1, source_target_pairs={{0,12},{1,13},{2,14},{3,15},{4,8},{5,9},{6,10},{7,11},{8,4},{9,5},... | collective-permute-start | bytes 393224 | tf_op jit(solution)/shard_map/ppermute | solution.py:208
  79.8 12.3 %collective-permute-start.30 = (bf16[4,2,64,512]{3,2,1,0:T(8,128)(2,1)S(1)}, bf16[4,2,64,512]{3,2,1,0:T(8,128)(2,1)S(1)}, u32[]{:S(2)}, u32[]{:S(2)}) collective-permute-start(bf16[4,2,64,512]{3,2,1,0:T(8,128)(2,1)S(1)} %shard_map.60.refs_5_.refs_1_), channel_id=1, source_target_pairs={{0,2},{1,3},{2,0},{3,1},{4,6},{5,7},{6,4},{7,5},{8,10},{9,11},{10,... | collective-permute-start | bytes 1572872 | tf_op jit(solution)/shard_map/ppermute | solution.py:208
  80.5 15.0 %collective-permute-start.18 = (bf16[1,1,64,512]{3,2,1,0:T(8,128)(2,1)S(1)}, bf16[1,1,64,512]{3,2,1,0:T(8,128)(2,1)S(1)}, u32[]{:S(2)}, u32[]{:S(2)}) collective-permute-start(bf16[1,1,64,512]{3,2,1,0:T(8,128)(2,1)S(1)} %shard_map.58.refs_6_.refs_1_), channel_id=1, source_target_pairs={{0,8},{1,9},{2,10},{3,11},{4,12},{5,13},{6,14},{7,15},{8,0},{9,1},... | collective-permute-start | bytes 196616 | tf_op jit(solution)/shard_map/ppermute | solution.py:208
  80.5 15.0 %collective-permute-start.19 = (bf16[1,1,64,512]{3,2,1,0:T(8,128)(2,1)S(1)}, bf16[1,1,64,512]{3,2,1,0:T(8,128)(2,1)S(1)}, u32[]{:S(2)}, u32[]{:S(2)}) collective-permute-start(bf16[1,1,64,512]{3,2,1,0:T(8,128)(2,1)S(1)} %shard_map.58.refs_6_.refs_1_), channel_id=1, source_target_pairs={{0,4},{1,5},{2,6},{3,7},{4,0},{5,1},{6,2},{7,3},{8,12},{9,13},{10,... | collective-permute-start | bytes 196616 | tf_op jit(solution)/shard_map/ppermute | solution.py:208
  82.8 12.7 %collective-permute-start.20 = (bf16[1,1,64,512]{3,2,1,0:T(8,128)(2,1)S(1)}, bf16[1,1,64,512]{3,2,1,0:T(8,128)(2,1)S(1)}, u32[]{:S(2)}, u32[]{:S(2)}) collective-permute-start(bf16[1,1,64,512]{3,2,1,0:T(8,128)(2,1)S(1)} %shard_map.58.refs_6_.refs_1_), channel_id=1, source_target_pairs={{0,12},{1,13},{2,14},{3,15},{4,8},{5,9},{6,10},{7,11},{8,4},{9,5},... | collective-permute-start | bytes 196616 | tf_op jit(solution)/shard_map/ppermute | solution.py:208
  83.1 27.9 %collective-permute-start.31 = (bf16[4,2,64,512]{3,2,1,0:T(8,128)(2,1)S(1)}, bf16[4,2,64,512]{3,2,1,0:T(8,128)(2,1)}, u32[]{:S(2)}, u32[]{:S(2)}) collective-permute-start(bf16[4,2,64,512]{3,2,1,0:T(8,128)(2,1)S(1)} %shard_map.60.refs_5_.refs_1_), channel_id=1, source_target_pairs={{0,1},{1,0},{2,3},{3,2},{4,5},{5,4},{6,7},{7,6},{8,9},{9,8},{10,11... | collective-permute-start | bytes 1572872 | tf_op jit(solution)/shard_map/ppermute | solution.py:208
  85.8 29.1 %all-to-all-start.1 = ((bf16[16,32,1024]{2,1,0:T(8,128)(2,1)}), bf16[16,32,1024]{2,1,0:T(8,128)(2,1)S(1)}, u32[]{:S(2)}, u32[]{:S(2)}) async-start(bf16[16,32,1024]{2,1,0:T(8,128)(2,1)} %bitcast.2), calls=%async_computation.1 | async-start | bytes 2097152 | tf_op jit(solution)/shard_map/all_to_all | solution.py:387
  92.1 18.9 %collective-permute-start.32 = (bf16[4,2,64,512]{3,2,1,0:T(8,128)(2,1)S(1)}, bf16[4,2,64,512]{3,2,1,0:T(8,128)(2,1)S(1)}, u32[]{:S(2)}, u32[]{:S(2)}) collective-permute-start(bf16[4,2,64,512]{3,2,1,0:T(8,128)(2,1)S(1)} %collective-permute-done.30.refs_2_.refs_6_), channel_id=1, source_target_pairs={{0,1},{1,0},{2,3},{3,2},{4,5},{5,4},{6,7},{7,6},{8,9},{9,8},{10,11... | collective-permute-start | bytes 1572872 | tf_op jit(solution)/shard_map/ppermute | solution.py:208
  96.0 14.5 %collective-permute-start.27 = (bf16[4,1,64,512]{3,2,1,0:T(8,128)(2,1)S(1)}, bf16[4,1,64,512]{3,2,1,0:T(8,128)(2,1)S(1)}, u32[]{:S(2)}, u32[]{:S(2)}) collective-permute-start(bf16[4,1,64,512]{3,2,1,0:T(8,128)(2,1)S(1)} %shard_map.61.refs_9_.refs_1_), channel_id=1, source_target_pairs={{0,2},{1,3},{2,0},{3,1},{4,6},{5,7},{6,4},{7,5},{8,10},{9,11},{10,... | collective-permute-start | bytes 786440 | tf_op jit(solution)/shard_map/ppermute | solution.py:208
  98.3 19.6 %collective-permute-start.28 = (bf16[4,1,64,512]{3,2,1,0:T(8,128)(2,1)S(1)}, bf16[4,1,64,512]{3,2,1,0:T(8,128)(2,1)S(1)}, u32[]{:S(2)}, u32[]{:S(2)}) collective-permute-start(bf16[4,1,64,512]{3,2,1,0:T(8,128)(2,1)S(1)} %shard_map.61.refs_9_.refs_1_), channel_id=1, source_target_pairs={{0,1},{1,0},{2,3},{3,2},{4,5},{5,4},{6,7},{7,6},{8,9},{9,8},{10,11... | collective-permute-start | bytes 786440 | tf_op jit(solution)/shard_map/ppermute | solution.py:208
  (13 other events, 77.9 us)

commit v7 on v6

--- a/solution.py
+++ b/solution.py
@@ -311,12 +311,14 @@
     )
 
 
-def right_body(meta, stem, factor, out, both):
+def right_body(meta, stem, factor, out, both, sem):
     count, columns = stem.shape
     width = columns // 2
     core = meta[0] & 1
-    value = factor[...]
-    both[:width] = value
+    copy = pltpu.make_async_copy(factor, both.at[pl.ds(0, width)], sem)
+    copy.start()
+    copy.wait()
+    value = both[:width]
     both[width:, :width] = -value[:, width:]
     both[width:, width:] = value[:, :width]
     left = stem[...]
@@ -334,9 +336,9 @@
     return chain(
         right_body,
         shaped((2, count, columns)),
-        [VMEM_SPEC] * 2,
+        [VMEM_SPEC, HBM_SPEC],
         (stem, factor),
-        [pltpu.VMEM((columns, columns), bf16)],
+        [pltpu.VMEM((columns, columns), bf16), pltpu.SemaphoreType.DMA],
         us=RIGHT,
     )
 

time: 121 us -> 121 us (level)
  no operation moved by 1% of the time
where the time goes in v7:
time: 121 us
  starting transfers between devices  55.5 us (46%)
  Pallas kernels  33.6 us (28%)
  waiting for transfers between devices  28.6 us (24%)
  local copies, waits for them, and re-layouts  2.23 us (2%)
    ppermute x33, starting transfers between devices, swap_with(): return lax.ppermute(x, 'outer', [(i, i ^ mask) for i in range(size)])  45.3 us
    pallas_call x19, Pallas kernels, __call__(): pl.pallas_call(kernel, out_shape=shapes, in_specs=specs, out_specs=tuple(...  33.6 us
    ppermute x33, waiting for transfers between devices, swap_with(): return lax.ppermute(x, 'outer', [(i, i ^ mask) for i in range(size)])  28.6 us
    all_to_all x2, starting transfers between devices, exchange(): return lax.all_to_all(x, 'outer', split_axis=0, concat_axis=0, tiled=True)  10.2 us
  transfers between devices with their start and end apart: 35, of which 9 were waited for; matrix products, arithmetic and copies ran while one was open for 0% of the time, Pallas kernels for 22%

profile of v7, /device:TPU:11, one launch (start us, length us, event | category | flops | bytes accessed | tf_op | source)
XLA Modules:
  0.0 121.0 jit_solution(11761101974831489998)
XLA Ops:
  0.7 3.6 %shard_map.46 = (f32[1,512,512]{2,1,0:T(8,128)S(1)}, bf16[1,512,512]{2,1,0:T(8,128)(2,1)S(1)}) custom-call(s32[5]{0:T(128)S(1)} %pad_add_fusion.refs_0_, bf16[4,2,512,2,512]{4,3,2,1,0:T(2,128)(2,1)} %refs_1_.3, bf16[4,2,512,2,512]{4,3,2,1,0:T(2,128)(2,1)} %refs_2_.3), custom_call_target="tpu_custom_call" | custom-call | flops 100000000 | bytes 1024 | tf_op jit(solution)/shard_map/pallas_call | solution.py:40
  5.0 6.0 %all-to-all-start = ((bf16[512,2,512]{2,1,0:T(2,128)(2,1)}), bf16[512,2,512]{2,1,0:T(2,128)(2,1)S(1)}, u32[]{:S(2)}, u32[]{:S(2)}) async-start(bf16[512,2,512]{2,1,0:T(2,128)(2,1)} %bitcast.7), calls=%async_computation | async-start | bytes 2097152 | tf_op jit(solution)/shard_map/all_to_all | solution.py:389
  13.0 7.1 %shard_map.48 = (f32[2,512,512]{2,1,0:T(8,128)S(1)}, bf16[2,512,512]{2,1,0:T(8,128)(2,1)S(1)}, f32[1,512,512]{2,1,0:T(8,128)S(1)}, bf16[1,512,512]{2,1,0:T(8,128)(2,1)S(1)}) custom-call(s32[5]{0:T(128)S(1)} %pad_add_fusion.refs_0_, bf16[4,2,512,2,512]{4,3,2,1,0:T(2,128)(2,1)} %refs_1_.3, bf16[4,2,512,2,512]{4,3,2,1,0:T(2,128)(2,1)} %refs_2_.3, ...), custom_call_target="tpu_custom_call" | custom-call | flops 10000000000 | bytes 1024 | tf_op jit(solution)/shard_map/pallas_call | solution.py:40
  20.9 4.9 %collective-permute-done.3.refs_2_ = bf16[1,256,512]{2,1,0:T(8,128)(2,1)S(1)} collective-permute-done((bf16[1,256,512]{2,1,0:T(8,128)(2,1)S(1)}, bf16[1,256,512]{2,1,0:T(8,128)(2,1)S(1)}, u32[]{:S(2)}, u32[]{:S(2)}) %collective-permute-start.3) | collective-permute-done | bytes 262176 | tf_op jit(solution)/shard_map/ppermute | solution.py:208
  29.0 4.6 %collective-permute-start.6 = (bf16[1,64,512]{2,1,0:T(8,128)(2,1)}, bf16[1,64,512]{2,1,0:T(8,128)(2,1)}, u32[]{:S(2)}, u32[]{:S(2)}) collective-permute-start(bf16[1,64,512]{2,1,0:T(8,128)(2,1)} %get-tuple-element.42), channel_id=1, source_target_pairs={{0,8},{1,9},{2,10},{3,11},{4,12},{5,13},{6,14},{7,15},{8,0},{9,1},... | collective-permute-start | bytes 196616 | tf_op jit(solution)/shard_map/ppermute | solution.py:208
  36.6 2.7 %shard_map.52.refs_5_ = bf16[2,512,1024]{2,1,0:T(8,128)(2,1)S(1)} custom-call(s32[5]{0:T(128)S(1)} %pad_add_fusion.refs_0_, bf16[512,2,512]{2,1,0:T(2,128)(2,1)S(1)} %all-to-all-done.refs_1_, f32[1,256,512]{2,1,0:T(8,128)S(1)} %get-tuple-element.39.refs_2_.refs_1_), custom_call_target="tpu_custom_call" | custom-call | flops 100000000 | bytes 1024 | tf_op jit(solution)/shard_map/pallas_call | solution.py:40
  39.4 2.1 %collective-permute-done.8.refs_4_ = bf16[1,64,512]{2,1,0:T(8,128)(2,1)} collective-permute-done((bf16[1,64,512]{2,1,0:T(8,128)(2,1)}, bf16[1,64,512]{2,1,0:T(8,128)(2,1)}, u32[]{:S(2)}, u32[]{:S(2)}) %collective-permute-start.8) | collective-permute-done | bytes 65568 | tf_op jit(solution)/shard_map/ppermute | solution.py:208
  45.8 2.1 %collective-permute-start.12 = (bf16[2,64,512]{2,1,0:T(8,128)(2,1)S(1)}, bf16[2,64,512]{2,1,0:T(8,128)(2,1)S(1)}, u32[]{:S(2)}, u32[]{:S(2)}) collective-permute-start(bf16[2,64,512]{2,1,0:T(8,128)(2,1)S(1)} %get-tuple-element.50), channel_id=1, source_target_pairs={{0,8},{1,9},{2,10},{3,11},{4,12},{5,13},{6,14},{7,15},{8,0},{9,1},... | collective-permute-start | bytes 393224 | tf_op jit(solution)/shard_map/ppermute | solution.py:208
  48.0 2.7 %collective-permute-start.13 = (bf16[2,64,512]{2,1,0:T(8,128)(2,1)S(1)}, bf16[2,64,512]{2,1,0:T(8,128)(2,1)S(1)}, u32[]{:S(2)}, u32[]{:S(2)}) collective-permute-start(bf16[2,64,512]{2,1,0:T(8,128)(2,1)S(1)} %get-tuple-element.51), channel_id=1, source_target_pairs={{0,4},{1,5},{2,6},{3,7},{4,0},{5,1},{6,2},{7,3},{8,12},{9,13},{10,... | collective-permute-start | bytes 393224 | tf_op jit(solution)/shard_map/ppermute | solution.py:208
  55.3 2.2 %collective-permute-start.25 = (bf16[4,1,64,512]{3,2,1,0:T(8,128)(2,1)S(1)}, bf16[4,1,64,512]{3,2,1,0:T(8,128)(2,1)S(1)}, u32[]{:S(2)}, u32[]{:S(2)}) collective-permute-start(bf16[4,1,64,512]{3,2,1,0:T(8,128)(2,1)S(1)} %shard_map.56.refs_5_.refs_1_), channel_id=1, source_target_pairs={{0,1},{1,0},{2,3},{3,2},{4,5},{5,4},{6,7},{7,6},{8,9},{9,8},{10,11... | collective-permute-start | bytes 786440 | tf_op jit(solution)/shard_map/ppermute | solution.py:208
  57.5 2.2 %collective-permute-start.9 = (bf16[1,64,512]{2,1,0:T(8,128)(2,1)S(1)}, bf16[1,64,512]{2,1,0:T(8,128)(2,1)S(1)}, u32[]{:S(2)}, u32[]{:S(2)}) collective-permute-start(bf16[1,64,512]{2,1,0:T(8,128)(2,1)S(1)} %get-tuple-element.47), channel_id=1, source_target_pairs={{0,8},{1,9},{2,10},{3,11},{4,12},{5,13},{6,14},{7,15},{8,0},{9,1},... | collective-permute-start | bytes 196616 | tf_op jit(solution)/shard_map/ppermute | solution.py:208
  59.7 2.5 %collective-permute-done.14.refs_4_ = bf16[2,64,512]{2,1,0:T(8,128)(2,1)S(1)} collective-permute-done((bf16[2,64,512]{2,1,0:T(8,128)(2,1)S(1)}, bf16[2,64,512]{2,1,0:T(8,128)(2,1)S(1)}, u32[]{:S(2)}, u32[]{:S(2)}) %collective-permute-start.14) | collective-permute-done | bytes 131104 | tf_op jit(solution)/shard_map/ppermute | solution.py:208
  65.6 3.2 %collective-permute-done.11.refs_4_ = bf16[1,64,512]{2,1,0:T(8,128)(2,1)S(1)} collective-permute-done((bf16[1,64,512]{2,1,0:T(8,128)(2,1)S(1)}, bf16[1,64,512]{2,1,0:T(8,128)(2,1)S(1)}, u32[]{:S(2)}, u32[]{:S(2)}) %collective-permute-start.11) | collective-permute-done | bytes 65568 | tf_op jit(solution)/shard_map/ppermute | solution.py:208
  68.8 5.3 %collective-permute-start.26 = (bf16[4,1,64,512]{3,2,1,0:T(8,128)(2,1)S(1)}, bf16[4,1,64,512]{3,2,1,0:T(8,128)(2,1)S(1)}, u32[]{:S(2)}, u32[]{:S(2)}) collective-permute-start(bf16[4,1,64,512]{3,2,1,0:T(8,128)(2,1)S(1)} %collective-permute-done.24.refs_2_), channel_id=1, source_target_pairs={{0,1},{1,0},{2,3},{3,2},{4,5},{5,4},{6,7},{7,6},{8,9},{9,8},{10,11... | collective-permute-start | bytes 786440 | tf_op jit(solution)/shard_map/ppermute | solution.py:208
  75.2 2.8 %shard_map.59.refs_5_ = bf16[8,64,1024]{2,1,0:T(8,128)(2,1)} custom-call(s32[5]{0:T(128)S(1)} %pad_add_fusion.refs_0_, bf16[4,1,64,512]{3,2,1,0:T(8,128)(2,1)S(1)} %shard_map.56.refs_5_.refs_1_, bf16[4,1,64,512]{3,2,1,0:T(8,128)(2,1)S(1)} %collective-permute-done.24.refs_2_, bf16[4,1,64,512]{3,2,1,0:T(8,128)(2,1)S(1)} %collective-permute-done.25.refs_3_, ...), custom_call_target="tpu_custom_call" | custom-call | flops 1000000000 | bytes 1024 | tf_op jit(solution)/shard_map/pallas_call | solution.py:40
  80.5 2.3 %collective-permute-start.19 = (bf16[1,1,64,512]{3,2,1,0:T(8,128)(2,1)S(1)}, bf16[1,1,64,512]{3,2,1,0:T(8,128)(2,1)S(1)}, u32[]{:S(2)}, u32[]{:S(2)}) collective-permute-start(bf16[1,1,64,512]{3,2,1,0:T(8,128)(2,1)S(1)} %shard_map.58.refs_6_.refs_1_), channel_id=1, source_target_pairs={{0,4},{1,5},{2,6},{3,7},{4,0},{5,1},{6,2},{7,3},{8,12},{9,13},{10,... | collective-permute-start | bytes 196616 | tf_op jit(solution)/shard_map/ppermute | solution.py:208
  83.1 2.7 %collective-permute-start.31 = (bf16[4,2,64,512]{3,2,1,0:T(8,128)(2,1)S(1)}, bf16[4,2,64,512]{3,2,1,0:T(8,128)(2,1)}, u32[]{:S(2)}, u32[]{:S(2)}) collective-permute-start(bf16[4,2,64,512]{3,2,1,0:T(8,128)(2,1)S(1)} %shard_map.60.refs_5_.refs_1_), channel_id=1, source_target_pairs={{0,1},{1,0},{2,3},{3,2},{4,5},{5,4},{6,7},{7,6},{8,9},{9,8},{10,11... | collective-permute-start | bytes 1572872 | tf_op jit(solution)/shard_map/ppermute | solution.py:208
  85.8 4.2 %all-to-all-start.1 = ((bf16[16,32,1024]{2,1,0:T(8,128)(2,1)}), bf16[16,32,1024]{2,1,0:T(8,128)(2,1)S(1)}, u32[]{:S(2)}, u32[]{:S(2)}) async-start(bf16[16,32,1024]{2,1,0:T(8,128)(2,1)} %bitcast.2), calls=%async_computation.1 | async-start | bytes 2097152 | tf_op jit(solution)/shard_map/all_to_all | solution.py:389
  90.0 2.1 %collective-permute-done.30.refs_2_.refs_6_ = bf16[4,2,64,512]{3,2,1,0:T(8,128)(2,1)S(1)} collective-permute-done((bf16[4,2,64,512]{3,2,1,0:T(8,128)(2,1)S(1)}, bf16[4,2,64,512]{3,2,1,0:T(8,128)(2,1)S(1)}, u32[]{:S(2)}, u32[]{:S(2)}) %collective-permute-start.30) | collective-permute-done | bytes 524320 | tf_op jit(solution)/shard_map/ppermute | solution.py:208
  92.1 3.4 %collective-permute-start.32 = (bf16[4,2,64,512]{3,2,1,0:T(8,128)(2,1)S(1)}, bf16[4,2,64,512]{3,2,1,0:T(8,128)(2,1)S(1)}, u32[]{:S(2)}, u32[]{:S(2)}) collective-permute-start(bf16[4,2,64,512]{3,2,1,0:T(8,128)(2,1)S(1)} %collective-permute-done.30.refs_2_.refs_6_), channel_id=1, source_target_pairs={{0,1},{1,0},{2,3},{3,2},{4,5},{5,4},{6,7},{7,6},{8,9},{9,8},{10,11... | collective-permute-start | bytes 1572872 | tf_op jit(solution)/shard_map/ppermute | solution.py:208
  96.0 2.2 %collective-permute-start.27 = (bf16[4,1,64,512]{3,2,1,0:T(8,128)(2,1)S(1)}, bf16[4,1,64,512]{3,2,1,0:T(8,128)(2,1)S(1)}, u32[]{:S(2)}, u32[]{:S(2)}) collective-permute-start(bf16[4,1,64,512]{3,2,1,0:T(8,128)(2,1)S(1)} %shard_map.61.refs_9_.refs_1_), channel_id=1, source_target_pairs={{0,2},{1,3},{2,0},{3,1},{4,6},{5,7},{6,4},{7,5},{8,10},{9,11},{10,... | collective-permute-start | bytes 786440 | tf_op jit(solution)/shard_map/ppermute | solution.py:208
  98.5 11.9 %collective-permute-done.27.refs_2_ = bf16[4,1,64,512]{3,2,1,0:T(8,128)(2,1)S(1)} collective-permute-done((bf16[4,1,64,512]{3,2,1,0:T(8,128)(2,1)S(1)}, bf16[4,1,64,512]{3,2,1,0:T(8,128)(2,1)S(1)}, u32[]{:S(2)}, u32[]{:S(2)}) %collective-permute-start.27) | collective-permute-done | bytes 262176 | tf_op jit(solution)/shard_map/ppermute | solution.py:208
  111.0 2.8 %shard_map.62.refs_3_ = bf16[8,64,1024]{2,1,0:T(8,128)(2,1)S(1)} custom-call(s32[5]{0:T(128)S(1)} %pad_add_fusion.refs_0_, bf16[4,2,64,512]{3,2,1,0:T(8,128)(2,1)S(1)} %shard_map.60.refs_5_.refs_1_, bf16[4,2,64,512]{3,2,1,0:T(8,128)(2,1)S(1)} %collective-permute-done.30.refs_2_.refs_6_, bf16[4,2,64,512]{3,2,1,0:T(8,128)(2,1)} %collective-permute-done.31.refs_3_.refs_7_, ...), custom_call_target="tpu_custom_call" | custom-call | flops 2000000000 | bytes 1024 | tf_op jit(solution)/shard_map/pallas_call | solution.py:40
  118.0 2.8 %shard_map.64 = bf16[1,512,2,512]{3,2,1,0:T(2,128)(2,1)} custom-call(s32[5]{0:T(128)S(1)} %pad_add_fusion.refs_0_, bf16[4,1,64,512]{3,2,1,0:T(8,128)(2,1)S(1)} %shard_map.61.refs_9_.refs_1_, bf16[4,1,64,512]{3,2,1,0:T(8,128)(2,1)S(1)} %collective-permute-done.27.refs_2_, bf16[4,1,64,512]{3,2,1,0:T(8,128)(2,1)S(1)} %collective-permute-done.28.refs_3_, ...), custom_call_target="tpu_custom_call" | custom-call | flops 1000000000 | bytes 1024 | tf_op jit(solution)/shard_map/pallas_call | solution.py:40
  (70 shorter events, 32.1 us)
Async XLA Ops:
  5.0 31.6 %all-to-all-start = ((bf16[512,2,512]{2,1,0:T(2,128)(2,1)}), bf16[512,2,512]{2,1,0:T(2,128)(2,1)S(1)}, u32[]{:S(2)}, u32[]{:S(2)}) async-start(bf16[512,2,512]{2,1,0:T(2,128)(2,1)} %bitcast.7), calls=%async_computation | async-start | bytes 2097152 | tf_op jit(solution)/shard_map/all_to_all | solution.py:389
  11.7 14.1 %collective-permute-start.3 = (bf16[1,256,512]{2,1,0:T(8,128)(2,1)S(1)}, bf16[1,256,512]{2,1,0:T(8,128)(2,1)S(1)}, u32[]{:S(2)}, u32[]{:S(2)}) collective-permute-start(bf16[1,256,512]{2,1,0:T(8,128)(2,1)S(1)} %get-tuple-element.36), channel_id=1, source_target_pairs={{0,2},{1,3},{2,0},{3,1},{4,6},{5,7},{6,4},{7,5},{8,10},{9,11},{10,... | collective-permute-start | bytes 786440 | tf_op jit(solution)/shard_map/ppermute | solution.py:208
  20.1 13.7 %collective-permute-start.1 = (bf16[1,512,512]{2,1,0:T(8,128)(2,1)S(1)}, bf16[1,512,512]{2,1,0:T(8,128)(2,1)S(1)}, u32[]{:S(2)}, u32[]{:S(2)}) collective-permute-start(bf16[1,512,512]{2,1,0:T(8,128)(2,1)S(1)} %get-tuple-element.33), channel_id=1, source_target_pairs={{0,1},{1,0},{2,3},{3,2},{4,5},{5,4},{6,7},{7,6},{8,9},{9,8},{10,11... | collective-permute-start | bytes 1572872 | tf_op jit(solution)/shard_map/ppermute | solution.py:208
  28.6 16.6 %collective-permute-start.5 = (bf16[2,256,512]{2,1,0:T(8,128)(2,1)}, bf16[2,256,512]{2,1,0:T(8,128)(2,1)S(1)}, u32[]{:S(2)}, u32[]{:S(2)}) collective-permute-start(bf16[2,256,512]{2,1,0:T(8,128)(2,1)} %get-tuple-element.41), channel_id=1, source_target_pairs={{0,2},{1,3},{2,0},{3,1},{4,6},{5,7},{6,4},{7,5},{8,10},{9,11},{10,... | collective-permute-start | bytes 1572872 | tf_op jit(solution)/shard_map/ppermute | solution.py:208
  29.0 10.4 %collective-permute-start.6 = (bf16[1,64,512]{2,1,0:T(8,128)(2,1)}, bf16[1,64,512]{2,1,0:T(8,128)(2,1)}, u32[]{:S(2)}, u32[]{:S(2)}) collective-permute-start(bf16[1,64,512]{2,1,0:T(8,128)(2,1)} %get-tuple-element.42), channel_id=1, source_target_pairs={{0,8},{1,9},{2,10},{3,11},{4,12},{5,13},{6,14},{7,15},{8,0},{9,1},... | collective-permute-start | bytes 196616 | tf_op jit(solution)/shard_map/ppermute | solution.py:208
  35.1 12.8 %collective-permute-start.4 = (bf16[1,256,512]{2,1,0:T(8,128)(2,1)}, bf16[1,256,512]{2,1,0:T(8,128)(2,1)S(1)}, u32[]{:S(2)}, u32[]{:S(2)}) collective-permute-start(bf16[1,256,512]{2,1,0:T(8,128)(2,1)} %get-tuple-element.40), channel_id=1, source_target_pairs={{0,2},{1,3},{2,0},{3,1},{4,6},{5,7},{6,4},{7,5},{8,10},{9,11},{10,... | collective-permute-start | bytes 786440 | tf_op jit(solution)/shard_map/ppermute | solution.py:208
  43.7 9.2 %collective-permute-start.16 = (bf16[1,1,64,512]{3,2,1,0:T(8,128)(2,1)S(1)}, bf16[1,1,64,512]{3,2,1,0:T(8,128)(2,1)S(1)}, u32[]{:S(2)}, u32[]{:S(2)}) collective-permute-start(bf16[1,1,64,512]{3,2,1,0:T(8,128)(2,1)S(1)} %shard_map.53.refs_3_.refs_1_), channel_id=1, source_target_pairs={{0,4},{1,5},{2,6},{3,7},{4,0},{5,1},{6,2},{7,3},{8,12},{9,13},{10,... | collective-permute-start | bytes 196616 | tf_op jit(solution)/shard_map/ppermute | solution.py:208
  45.8 11.7 %collective-permute-start.12 = (bf16[2,64,512]{2,1,0:T(8,128)(2,1)S(1)}, bf16[2,64,512]{2,1,0:T(8,128)(2,1)S(1)}, u32[]{:S(2)}, u32[]{:S(2)}) collective-permute-start(bf16[2,64,512]{2,1,0:T(8,128)(2,1)S(1)} %get-tuple-element.50), channel_id=1, source_target_pairs={{0,8},{1,9},{2,10},{3,11},{4,12},{5,13},{6,14},{7,15},{8,0},{9,1},... | collective-permute-start | bytes 393224 | tf_op jit(solution)/shard_map/ppermute | solution.py:208
  48.0 11.8 %collective-permute-start.13 = (bf16[2,64,512]{2,1,0:T(8,128)(2,1)S(1)}, bf16[2,64,512]{2,1,0:T(8,128)(2,1)S(1)}, u32[]{:S(2)}, u32[]{:S(2)}) collective-permute-start(bf16[2,64,512]{2,1,0:T(8,128)(2,1)S(1)} %get-tuple-element.51), channel_id=1, source_target_pairs={{0,4},{1,5},{2,6},{3,7},{4,0},{5,1},{6,2},{7,3},{8,12},{9,13},{10,... | collective-permute-start | bytes 393224 | tf_op jit(solution)/shard_map/ppermute | solution.py:208
  51.3 10.9 %collective-permute-start.14 = (bf16[2,64,512]{2,1,0:T(8,128)(2,1)S(1)}, bf16[2,64,512]{2,1,0:T(8,128)(2,1)S(1)}, u32[]{:S(2)}, u32[]{:S(2)}) collective-permute-start(bf16[2,64,512]{2,1,0:T(8,128)(2,1)S(1)} %get-tuple-element.52), channel_id=1, source_target_pairs={{0,12},{1,13},{2,14},{3,15},{4,8},{5,9},{6,10},{7,11},{8,4},{9,5},... | collective-permute-start | bytes 393224 | tf_op jit(solution)/shard_map/ppermute | solution.py:208
  53.5 15.3 %collective-permute-start.24 = (bf16[4,1,64,512]{3,2,1,0:T(8,128)(2,1)S(1)}, bf16[4,1,64,512]{3,2,1,0:T(8,128)(2,1)S(1)}, u32[]{:S(2)}, u32[]{:S(2)}) collective-permute-start(bf16[4,1,64,512]{3,2,1,0:T(8,128)(2,1)S(1)} %shard_map.56.refs_5_.refs_1_), channel_id=1, source_target_pairs={{0,2},{1,3},{2,0},{3,1},{4,6},{5,7},{6,4},{7,5},{8,10},{9,11},{10,... | collective-permute-start | bytes 786440 | tf_op jit(solution)/shard_map/ppermute | solution.py:208
  55.3 19.3 %collective-permute-start.25 = (bf16[4,1,64,512]{3,2,1,0:T(8,128)(2,1)S(1)}, bf16[4,1,64,512]{3,2,1,0:T(8,128)(2,1)S(1)}, u32[]{:S(2)}, u32[]{:S(2)}) collective-permute-start(bf16[4,1,64,512]{3,2,1,0:T(8,128)(2,1)S(1)} %shard_map.56.refs_5_.refs_1_), channel_id=1, source_target_pairs={{0,1},{1,0},{2,3},{3,2},{4,5},{5,4},{6,7},{7,6},{8,9},{9,8},{10,11... | collective-permute-start | bytes 786440 | tf_op jit(solution)/shard_map/ppermute | solution.py:208
  63.3 14.7 %collective-permute-start.21 = (bf16[1,2,64,512]{3,2,1,0:T(8,128)(2,1)S(1)}, bf16[1,2,64,512]{3,2,1,0:T(8,128)(2,1)S(1)}, u32[]{:S(2)}, u32[]{:S(2)}) collective-permute-start(bf16[1,2,64,512]{3,2,1,0:T(8,128)(2,1)S(1)} %shard_map.57.refs_5_.refs_1_), channel_id=1, source_target_pairs={{0,8},{1,9},{2,10},{3,11},{4,12},{5,13},{6,14},{7,15},{8,0},{9,1},... | collective-permute-start | bytes 393224 | tf_op jit(solution)/shard_map/ppermute | solution.py:208
  64.7 13.3 %collective-permute-start.22 = (bf16[1,2,64,512]{3,2,1,0:T(8,128)(2,1)S(1)}, bf16[1,2,64,512]{3,2,1,0:T(8,128)(2,1)S(1)}, u32[]{:S(2)}, u32[]{:S(2)}) collective-permute-start(bf16[1,2,64,512]{3,2,1,0:T(8,128)(2,1)S(1)} %shard_map.57.refs_5_.refs_1_), channel_id=1, source_target_pairs={{0,4},{1,5},{2,6},{3,7},{4,0},{5,1},{6,2},{7,3},{8,12},{9,13},{10,... | collective-permute-start | bytes 393224 | tf_op jit(solution)/shard_map/ppermute | solution.py:208
  68.8 10.4 %collective-permute-start.23 = (bf16[1,2,64,512]{3,2,1,0:T(8,128)(2,1)S(1)}, bf16[1,2,64,512]{3,2,1,0:T(8,128)(2,1)S(1)}, u32[]{:S(2)}, u32[]{:S(2)}) collective-permute-start(bf16[1,2,64,512]{3,2,1,0:T(8,128)(2,1)S(1)} %shard_map.57.refs_5_.refs_1_), channel_id=1, source_target_pairs={{0,12},{1,13},{2,14},{3,15},{4,8},{5,9},{6,10},{7,11},{8,4},{9,5},... | collective-permute-start | bytes 393224 | tf_op jit(solution)/shard_map/ppermute | solution.py:208
  79.8 12.3 %collective-permute-start.30 = (bf16[4,2,64,512]{3,2,1,0:T(8,128)(2,1)S(1)}, bf16[4,2,64,512]{3,2,1,0:T(8,128)(2,1)S(1)}, u32[]{:S(2)}, u32[]{:S(2)}) collective-permute-start(bf16[4,2,64,512]{3,2,1,0:T(8,128)(2,1)S(1)} %shard_map.60.refs_5_.refs_1_), channel_id=1, source_target_pairs={{0,2},{1,3},{2,0},{3,1},{4,6},{5,7},{6,4},{7,5},{8,10},{9,11},{10,... | collective-permute-start | bytes 1572872 | tf_op jit(solution)/shard_map/ppermute | solution.py:208
  80.5 15.0 %collective-permute-start.18 = (bf16[1,1,64,512]{3,2,1,0:T(8,128)(2,1)S(1)}, bf16[1,1,64,512]{3,2,1,0:T(8,128)(2,1)S(1)}, u32[]{:S(2)}, u32[]{:S(2)}) collective-permute-start(bf16[1,1,64,512]{3,2,1,0:T(8,128)(2,1)S(1)} %shard_map.58.refs_6_.refs_1_), channel_id=1, source_target_pairs={{0,8},{1,9},{2,10},{3,11},{4,12},{5,13},{6,14},{7,15},{8,0},{9,1},... | collective-permute-start | bytes 196616 | tf_op jit(solution)/shard_map/ppermute | solution.py:208
  80.5 15.0 %collective-permute-start.19 = (bf16[1,1,64,512]{3,2,1,0:T(8,128)(2,1)S(1)}, bf16[1,1,64,512]{3,2,1,0:T(8,128)(2,1)S(1)}, u32[]{:S(2)}, u32[]{:S(2)}) collective-permute-start(bf16[1,1,64,512]{3,2,1,0:T(8,128)(2,1)S(1)} %shard_map.58.refs_6_.refs_1_), channel_id=1, source_target_pairs={{0,4},{1,5},{2,6},{3,7},{4,0},{5,1},{6,2},{7,3},{8,12},{9,13},{10,... | collective-permute-start | bytes 196616 | tf_op jit(solution)/shard_map/ppermute | solution.py:208
  82.8 12.7 %collective-permute-start.20 = (bf16[1,1,64,512]{3,2,1,0:T(8,128)(2,1)S(1)}, bf16[1,1,64,512]{3,2,1,0:T(8,128)(2,1)S(1)}, u32[]{:S(2)}, u32[]{:S(2)}) collective-permute-start(bf16[1,1,64,512]{3,2,1,0:T(8,128)(2,1)S(1)} %shard_map.58.refs_6_.refs_1_), channel_id=1, source_target_pairs={{0,12},{1,13},{2,14},{3,15},{4,8},{5,9},{6,10},{7,11},{8,4},{9,5},... | collective-permute-start | bytes 196616 | tf_op jit(solution)/shard_map/ppermute | solution.py:208
  83.1 27.9 %collective-permute-start.31 = (bf16[4,2,64,512]{3,2,1,0:T(8,128)(2,1)S(1)}, bf16[4,2,64,512]{3,2,1,0:T(8,128)(2,1)}, u32[]{:S(2)}, u32[]{:S(2)}) collective-permute-start(bf16[4,2,64,512]{3,2,1,0:T(8,128)(2,1)S(1)} %shard_map.60.refs_5_.refs_1_), channel_id=1, source_target_pairs={{0,1},{1,0},{2,3},{3,2},{4,5},{5,4},{6,7},{7,6},{8,9},{9,8},{10,11... | collective-permute-start | bytes 1572872 | tf_op jit(solution)/shard_map/ppermute | solution.py:208
  85.8 29.1 %all-to-all-start.1 = ((bf16[16,32,1024]{2,1,0:T(8,128)(2,1)}), bf16[16,32,1024]{2,1,0:T(8,128)(2,1)S(1)}, u32[]{:S(2)}, u32[]{:S(2)}) async-start(bf16[16,32,1024]{2,1,0:T(8,128)(2,1)} %bitcast.2), calls=%async_computation.1 | async-start | bytes 2097152 | tf_op jit(solution)/shard_map/all_to_all | solution.py:389
  92.1 18.9 %collective-permute-start.32 = (bf16[4,2,64,512]{3,2,1,0:T(8,128)(2,1)S(1)}, bf16[4,2,64,512]{3,2,1,0:T(8,128)(2,1)S(1)}, u32[]{:S(2)}, u32[]{:S(2)}) collective-permute-start(bf16[4,2,64,512]{3,2,1,0:T(8,128)(2,1)S(1)} %collective-permute-done.30.refs_2_.refs_6_), channel_id=1, source_target_pairs={{0,1},{1,0},{2,3},{3,2},{4,5},{5,4},{6,7},{7,6},{8,9},{9,8},{10,11... | collective-permute-start | bytes 1572872 | tf_op jit(solution)/shard_map/ppermute | solution.py:208
  96.0 14.5 %collective-permute-start.27 = (bf16[4,1,64,512]{3,2,1,0:T(8,128)(2,1)S(1)}, bf16[4,1,64,512]{3,2,1,0:T(8,128)(2,1)S(1)}, u32[]{:S(2)}, u32[]{:S(2)}) collective-permute-start(bf16[4,1,64,512]{3,2,1,0:T(8,128)(2,1)S(1)} %shard_map.61.refs_9_.refs_1_), channel_id=1, source_target_pairs={{0,2},{1,3},{2,0},{3,1},{4,6},{5,7},{6,4},{7,5},{8,10},{9,11},{10,... | collective-permute-start | bytes 786440 | tf_op jit(solution)/shard_map/ppermute | solution.py:208
  98.3 19.7 %collective-permute-start.28 = (bf16[4,1,64,512]{3,2,1,0:T(8,128)(2,1)S(1)}, bf16[4,1,64,512]{3,2,1,0:T(8,128)(2,1)S(1)}, u32[]{:S(2)}, u32[]{:S(2)}) collective-permute-start(bf16[4,1,64,512]{3,2,1,0:T(8,128)(2,1)S(1)} %shard_map.61.refs_9_.refs_1_), channel_id=1, source_target_pairs={{0,1},{1,0},{2,3},{3,2},{4,5},{5,4},{6,7},{7,6},{8,9},{9,8},{10,11... | collective-permute-start | bytes 786440 | tf_op jit(solution)/shard_map/ppermute | solution.py:208
  (13 other events, 78.0 us)
